TPU v7x, 32 devices: a whole 2x2x4 slice. The times are simulated.
32 devices in a mesh: group: 2 (over x), scan: 16 (over z, y, core).
Axes of the slice: x: 2, y: 2, z: 4, core: 2. Of those that a mesh axis runs over, the one named last changes fastest.
Arguments:
- object_blocks: float32 [1024, 8, 1024], P(('group', 'scan')), parts along dimension 0, may hold values from -2 to 2
- probe: float32 [4, 256, 256], P('group'), parts along dimension 0, may hold values from -6 to 6
- positions: int32 [64, 2], P(('group', 'scan')), parts along dimension 0, may hold values from 0 to 256
- anchors: int32 [32, 2], P(('group', 'scan')), parts along dimension 0, may hold values from 0 to 16, as said below
- amplitudes: float32 [64, 256, 256], P(('group', 'scan')), parts along dimension 0, may hold values from 0.1 to 3
Outputs:
- object_gradient: float32 [1024, 8, 1024], P(('group', 'scan')), parts along dimension 0
- probe_gradient: float32 [4, 256, 256], P('group'), parts along dimension 0
There are 2 independent parts, one for each index of `group`. A program takes and returns all parts, laid end to end along the dimension named above; each array names one. Nothing has to cross between parts.
Inputs may be any that keep to these rules, and one draw needn't show every extreme that they name: `anchors`: each device's footprint of 16 x 16 blocks lies inside the region: block rows up to 0, block columns up to 16. `positions`: rows p * 2 to p * 2 + 1 belong to device p, and give offsets from that device's anchors times 32.
All inputs are finite; a program needn't handle non-finite values.
Results may differ from a plain program's by a relative error of at most 0.017.
Values may be sent and summed in bfloat16 or wider, within the bound.
No kernel may reach another device: no remote copies, remote signals or barrier semaphores. Data moves between devices by JAX's collectives and lax.ppermute only.
A program may use at most 192 MiB of HBM per device.

v0:
```python
import math

import jax
import jax.numpy as jnp
import numpy as np
from jax import lax
from jax.experimental import pallas as pl
from jax.experimental.pallas import tpu as pltpu
from jax.sharding import PartitionSpec as P

PATCH = 256
SLICES = 4
BSIDE = 32
FOOT = 16
OWN_COLS = 16
COL_BANDS = 2
FLOOR = 0.25
WIN = 9
TALL = FOOT * BSIDE
VMEM_BYTES = 48 * 1024 * 1024
F32 = jnp.float32
BF16 = jnp.bfloat16


def lane_rows():
    lane = np.arange(PATCH)
    return lane % 8 * BSIDE + lane // 8


def stacked_right(table):
    real, imag = table
    return np.block([[real, imag], [-imag, real]])


def stacked_left(table):
    real, imag = table
    return np.block([[real, -imag], [imag, real]])


def tables():
    counter = np.arange(PATCH)
    turns = counter[:, None] * counter[None, :] % PATCH
    angles = turns.astype(np.float64) * (2.0 * math.pi / PATCH)
    scaled = 1.0 / math.sqrt(PATCH)
    dft = (np.cos(angles) * scaled, -np.sin(angles) * scaled)
    centred = (counter + PATCH // 2) % PATCH - PATCH // 2
    turns = (4 * counter[:, None] * counter[None, :] - centred[None, :] ** 2) % (4 * PATCH)
    angles = turns.astype(np.float64) * (2.0 * math.pi / (4 * PATCH))
    gap = (counter[:, None] - counter[None, :]) % PATCH
    fresnel = ((np.cos(angles).sum(1) / PATCH)[gap], (np.sin(angles).sum(1) / PATCH)[gap])
    order = lane_rows()
    across = tuple(part.T[np.ix_(order, order)] for part in fresnel)
    down = tuple(part.T for part in fresnel)
    wanted = (
        stacked_right(across),
        stacked_left(down),
        stacked_left(dft),
        stacked_right(dft),
    )
    return tuple(jnp.asarray(t.astype(np.float32)).astype(BF16) for t in wanted)


def dot(left, right):
    return jnp.dot(left, right, preferred_element_type=F32)


def dot_nt(left, right):
    return lax.dot_general(left, right, (((1,), (1,)), ((), ())), preferred_element_type=F32)


def row_of_lane(shape):
    lane = lax.broadcasted_iota(jnp.int32, shape, 1)
    return (lane & 7) * BSIDE + (lane >> 3)


def shifts(meta, p, dtype=BF16):
    top, left = meta[p, 0], meta[p, 1]
    shape = (PATCH, PATCH)
    i = lax.broadcasted_iota(jnp.int32, shape, 0)
    j = lax.broadcasted_iota(jnp.int32, shape, 1)
    my = jnp.where(row_of_lane(shape) == ((i + top) & (PATCH - 1)), 1.0, 0.0).astype(dtype)
    mx = jnp.where(i == ((j + left) & (PATCH - 1)), 1.0, 0.0).astype(dtype)
    return my, mx


def cols(c):
    return pl.ds(c * PATCH, PATCH)


def fetch(meta, sources, window, sems, patches):
    per = sources[0].shape[0]

    def copy(source, place, p, k):
        return pltpu.make_async_copy(source.at[place], window.at[p, k], sems.at[p, k])

    for p in range(patches):
        for k in range(WIN):
            place = meta[p, 2 + k]
            for n, source in enumerate(sources):

                @pl.when(place // per == n)
                def _(source=source, place=place, n=n, p=p, k=k):
                    copy(source, place - n * per, p, k).start()

    for p in range(patches):
        for k in range(WIN):
            copy(sources[0], 0, p, k).wait()


def patch_rows(meta, window, p, k):
    top, left = meta[p, 0], meta[p, 1]
    low = row_of_lane((BSIDE, PATCH)) < top
    out = []
    for c in range(2):

        def pick(slot):
            strip = window[p, slot, c].astype(F32)
            return jnp.where(low, strip[:, PATCH:], strip[:, :PATCH])

        value = pick(k)
        if k == 0:
            b = lax.broadcasted_iota(jnp.int32, (BSIDE, PATCH), 0)
            value = jnp.where(b < left, pick(WIN - 1), value)
        out.append(value)
    return out


def propagate(field, half, right, left, patches, put):
    for p in range(patches):
        y = dot(field[cols(p), :], right[...])
        for c in range(2):
            half[cols(c), cols(p)] = y[:, c * PATCH : (c + 1) * PATCH].astype(BF16)
    for c in range(2):
        put(c, dot(left[cols(c), :], half[...]))


def add_gradient(meta, grid, p, k, pair):
    top, left = meta[p, 0], meta[p, 1]
    low = row_of_lane((BSIDE, PATCH)) < top
    b = lax.broadcasted_iota(jnp.int32, (BSIDE, PATCH), 0)

    def put(slot, c, value):
        place = meta[p, 2 + WIN + slot]
        for half in range(2):
            piece = jnp.where(low if half else jnp.logical_not(low), value, 0.0)
            spot = (place, c, slice(None), slice(half * PATCH, (half + 1) * PATCH))
            if p > 0 or slot == WIN - 1:
                piece = piece + grid[spot].astype(F32)
            grid[spot] = piece.astype(BF16)

    if k > 0:
        for c in range(2):
            put(k, c, pair[c])
        return
    for c in range(2):
        put(0, c, jnp.where(b < left, 0.0, pair[c]))

    @pl.when(left > 0)
    def _():
        for c in range(2):
            put(WIN - 1, c, jnp.where(b < left, pair[c], 0.0))


def send_out(grid, outs, sems):
    start = 0
    copies = []
    for n, out in enumerate(outs):
        size = out.shape[0]
        copies.append(pltpu.make_async_copy(grid.at[pl.ds(start, size)], out, sems.at[n]))
        start += size
    for copy in copies:
        copy.start()
    return copies


def rows(k):
    return pl.ds(k * BSIDE, BSIDE)


def at_rows(c, k):
    return pl.ds(c * PATCH + k * BSIDE, BSIDE)


def any_spec():
    return pl.BlockSpec(memory_space=pl.ANY)


def vmem_spec():
    return pl.BlockSpec(memory_space=pltpu.VMEM)


def smem_spec():
    return pl.BlockSpec(memory_space=pltpu.SMEM)


def params():
    return pltpu.CompilerParams(vmem_limit_bytes=VMEM_BYTES)


def cost(products, bytes_accessed):
    return pl.CostEstimate(
        flops=products * 8 * PATCH**3, bytes_accessed=bytes_accessed, transcendentals=0
    )


def wrap_probe(meta, probe, patches):
    def kernel(meta, probe, out):
        for p in range(patches):
            my, mx = shifts(meta, p, F32)
            for c in range(2):
                half = lax.dot_general(
                    mx,
                    probe[c],
                    (((1,), (1,)), ((), ())),
                    precision=lax.Precision.HIGHEST,
                    preferred_element_type=F32,
                )
                out[p, c] = jnp.dot(
                    half, my, precision=lax.Precision.HIGHEST, preferred_element_type=F32
                )

    return pl.pallas_call(
        kernel,
        out_shape=jax.ShapeDtypeStruct((patches, 2, PATCH, PATCH), F32),
        in_specs=[smem_spec(), vmem_spec()],
        out_specs=vmem_spec(),
        compiler_params=params(),
        cost_estimate=cost(patches * 6, 2 << 20),
        name="wrap_probe",
    )(meta, probe)


def forward(layer, meta, sources, before, right, left, patches):
    wide = patches * PATCH

    def kernel(meta, *refs):
        sources, refs = refs[: -9], refs[-9:]
        before, right, left, trans, after, window, field, half, sems = refs
        fetch(meta, sources, window, sems, patches)
        for p in range(patches):
            for k in range(PATCH // BSIDE):
                tr, ti = patch_rows(meta, window, p, k)
                trans[at_rows(0, k), cols(p)] = tr.astype(BF16)
                trans[at_rows(1, k), cols(p)] = ti.astype(BF16)
                tr = tr + 1.0
                if layer == 0:
                    fr, fi = before[p, 0, rows(k), :], before[p, 1, rows(k), :]
                else:
                    fr = before[at_rows(0, k), cols(p)].astype(F32)
                    fi = before[at_rows(1, k), cols(p)].astype(F32)
                field[at_rows(p, k), cols(0)] = (tr * fr - ti * fi).astype(BF16)
                field[at_rows(p, k), cols(1)] = (tr * fi + ti * fr).astype(BF16)

        def put(c, value):
            after[cols(c), :] = value.astype(BF16)

        propagate(field, half, right, left, patches, put)

    plane = jax.ShapeDtypeStruct((2 * PATCH, wide), BF16)
    return pl.pallas_call(
        kernel,
        out_shape=(plane, plane),
        in_specs=[smem_spec()] + [any_spec()] * len(sources) + [vmem_spec()] * 3,
        out_specs=(vmem_spec(), vmem_spec()),
        scratch_shapes=[
            pltpu.VMEM((patches, WIN, 2, BSIDE, TALL), BF16),
            pltpu.VMEM((wide, 2 * PATCH), BF16),
            pltpu.VMEM((2 * PATCH, wide), BF16),
            pltpu.SemaphoreType.DMA((patches, WIN)),
        ],
        compiler_params=params(),
        cost_estimate=cost(patches * 2, 4 << 20),
        name=f"forward_{layer}",
    )(meta, *sources, before, right, left)


def back_step(meta, p, k, g, q, t, grid, field):
    gr, gi = g
    qr, qi = q
    tr, ti = t
    add_gradient(meta, grid, p, k, (gr * qr + gi * qi, gi * qr - gr * qi))
    field[at_rows(p, k), cols(0)] = (tr * gr + ti * gi).astype(BF16)
    field[at_rows(p, k), cols(1)] = (ti * gr - tr * gi).astype(BF16)


def clear(grid):
    @pl.loop(0, grid.shape[0])
    def _(n):
        grid[n] = jnp.zeros(grid.shape[1:], BF16)


def put_conjugate(out):
    def put(c, value):
        out[cols(c), :] = (-value if c else value).astype(BF16)

    return put


def far_field(meta, sources, before, amplitudes, tabs, pieces, patches):
    wide = patches * PATCH
    n_out = len(pieces)

    def kernel(meta, *refs):
        n_in = len(sources)
        sources_, refs = refs[:n_in], refs[n_in:]
        before, measured, hr, hl, fl, fr = refs[:6]
        outs, refs = refs[6 : 6 + n_out], refs[6 + n_out :]
        after, window, field, half, other, trans, grid, sems, out_sems = refs
        fetch(meta, sources_, window, sems, patches)
        clear(grid)
        for p in range(patches):
            for k in range(PATCH // BSIDE):
                tr, ti = patch_rows(meta, window, p, k)
                trans[at_rows(0, k), cols(p)] = tr.astype(BF16)
                trans[at_rows(1, k), cols(p)] = ti.astype(BF16)
                tr = tr + 1.0
                qr = before[at_rows(0, k), cols(p)].astype(F32)
                qi = before[at_rows(1, k), cols(p)].astype(F32)
                field[at_rows(p, k), cols(0)] = (tr * qr - ti * qi).astype(BF16)
                field[at_rows(p, k), cols(1)] = (tr * qi + ti * qr).astype(BF16)
        for p in range(patches):
            my, mx = shifts(meta, p)
            for c in range(2):
                turned = dot_nt(my, field[cols(p), cols(c)]).astype(BF16)
                half[cols(c), cols(p)] = dot(turned, mx).astype(BF16)
        for c in range(2):
            y = dot(fl[cols(c), :], half[...])
            for p in range(patches):
                other[cols(p), cols(c)] = y[:, p * PATCH : (p + 1) * PATCH].astype(BF16)
        for p in range(patches):
            far = dot(other[cols(p), :], fr[...])
            real, imag = far[:, :PATCH], far[:, PATCH:]
            modulus = jnp.sqrt(real * real + imag * imag)
            keeping = 1.0 - measured[p] / jnp.maximum(modulus, FLOOR)
            half[cols(0), cols(p)] = (real * keeping).astype(BF16)
            half[cols(1), cols(p)] = (-imag * keeping).astype(BF16)
        for c in range(2):
            y = dot(fl[cols(c), :], half[...])
            for p in range(patches):
                other[cols(p), cols(c)] = y[:, p * PATCH : (p + 1) * PATCH].astype(BF16)
        for p in range(patches):
            g = dot(other[cols(p), :], fr[...])
            my, mx = shifts(meta, p)
            for c in range(2):
                part = g[:, c * PATCH : (c + 1) * PATCH]
                part = (-part if c else part).astype(BF16)
                turned = dot_nt(mx, part).astype(BF16)
                half[cols(c), cols(p)] = dot(turned, my).astype(BF16)
        for p in range(patches):
            for k in range(PATCH // BSIDE):
                load = lambda ref, c: ref[at_rows(c, k), cols(p)].astype(F32)
                back_step(
                    meta,
                    p,
                    k,
                    (load(half, 0), load(half, 1)),
                    (load(before, 0), load(before, 1)),
                    (load(trans, 0) + 1.0, load(trans, 1)),
                    grid,
                    field,
                )
        copies = send_out(grid, outs, out_sems)
        propagate(field, half, hr, hl, patches, put_conjugate(after))
        for copy in copies:
            copy.wait()

    plane = jax.ShapeDtypeStruct((2 * PATCH, wide), BF16)
    strips = [jax.ShapeDtypeStruct((n, 2, BSIDE, TALL), BF16) for n in pieces]
    *outs, after = pl.pallas_call(
        kernel,
        out_shape=(*strips, plane),
        in_specs=[smem_spec()] + [any_spec()] * len(sources) + [vmem_spec()] * 6,
        out_specs=(*[any_spec()] * n_out, vmem_spec()),
        scratch_shapes=[
            pltpu.VMEM((patches, WIN, 2, BSIDE, TALL), BF16),
            pltpu.VMEM((wide, 2 * PATCH), BF16),
            pltpu.VMEM((2 * PATCH, wide), BF16),
            pltpu.VMEM((wide, 2 * PATCH), BF16),
            pltpu.VMEM((2 * PATCH, wide), BF16),
            pltpu.VMEM((sum(pieces), 2, BSIDE, TALL), BF16),
            pltpu.SemaphoreType.DMA((patches, WIN)),
            pltpu.SemaphoreType.DMA((n_out,)),
        ],
        compiler_params=params(),
        cost_estimate=cost(patches * 8, 8 << 20),
        name="far_field",
    )(meta, *sources, before, amplitudes, *tabs)
    return outs, after


def backward(layer, meta, adjoint, carried, trans, right, left, pieces, patches):
    wide = patches * PATCH
    n_out = len(pieces)

    def kernel(meta, adjoint, carried, trans, right, left, *refs):
        outs, refs = refs[:n_out], refs[n_out:]
        after, field, half, grid, out_sems = refs
        clear(grid)
        for p in range(patches):
            for k in range(PATCH // BSIDE):
                load = lambda ref, c: ref[at_rows(c, k), cols(p)].astype(F32)
                back_step(
                    meta,
                    p,
                    k,
                    (load(adjoint, 0), load(adjoint, 1)),
                    (load(carried, 0), load(carried, 1)),
                    (load(trans, 0) + 1.0, load(trans, 1)),
                    grid,
                    field,
                )
        copies = send_out(grid, outs, out_sems)
        propagate(field, half, right, left, patches, put_conjugate(after))
        for copy in copies:
            copy.wait()

    plane = jax.ShapeDtypeStruct((2 * PATCH, wide), BF16)
    strips = [jax.ShapeDtypeStruct((n, 2, BSIDE, TALL), BF16) for n in pieces]
    *outs, after = pl.pallas_call(
        kernel,
        out_shape=(*strips, plane),
        in_specs=[smem_spec()] + [vmem_spec()] * 5,
        out_specs=(*[any_spec()] * n_out, vmem_spec()),
        scratch_shapes=[
            pltpu.VMEM((wide, 2 * PATCH), BF16),
            pltpu.VMEM((2 * PATCH, wide), BF16),
            pltpu.VMEM((sum(pieces), 2, BSIDE, TALL), BF16),
            pltpu.SemaphoreType.DMA((n_out,)),
        ],
        compiler_params=params(),
        cost_estimate=cost(patches * 2, 6 << 20),
        name=f"backward_{layer}",
    )(meta, adjoint, carried, trans, right, left)
    return outs, after


def first_slice(meta, adjoint, probe, trans, pieces, patches):
    wide = patches * PATCH
    n_out = len(pieces)

    def kernel(meta, adjoint, probe, trans, *refs):
        outs, refs = refs[:n_out], refs[n_out:]
        total, field, grid, out_sems = refs
        clear(grid)
        for p in range(patches):
            for k in range(PATCH // BSIDE):
                load = lambda ref, c: ref[at_rows(c, k), cols(p)].astype(F32)
                gr, gi = load(adjoint, 0), load(adjoint, 1)
                tr, ti = load(trans, 0) + 1.0, load(trans, 1)
                pr, pi = probe[p, 0, rows(k), :], probe[p, 1, rows(k), :]
                add_gradient(meta, grid, p, k, (gr * pr + gi * pi, gi * pr - gr * pi))
                field[at_rows(p, k), cols(0)] = (gr * tr + gi * ti).astype(BF16)
                field[at_rows(p, k), cols(1)] = (gi * tr - gr * ti).astype(BF16)
        copies = send_out(grid, outs, out_sems)
        moves = [shifts(meta, p) for p in range(patches)]
        for c in range(2):
            terms = [
                dot(dot_nt(my, field[cols(p), cols(c)]).astype(BF16), mx)
                for p, (my, mx) in enumerate(moves)
            ]
            total[c] = sum(terms[1:], terms[0]).astype(BF16)
        for copy in copies:
            copy.wait()

    strips = [jax.ShapeDtypeStruct((n, 2, BSIDE, TALL), BF16) for n in pieces]
    *outs, total = pl.pallas_call(
        kernel,
        out_shape=(*strips, jax.ShapeDtypeStruct((2, PATCH, PATCH), BF16)),
        in_specs=[smem_spec()] + [vmem_spec()] * 3,
        out_specs=(*[any_spec()] * n_out, vmem_spec()),
        scratch_shapes=[
            pltpu.VMEM((wide, 2 * PATCH), BF16),
            pltpu.VMEM((sum(pieces), 2, BSIDE, TALL), BF16),
            pltpu.SemaphoreType.DMA((n_out,)),
        ],
        compiler_params=params(),
        cost_estimate=cost(patches, 6 << 20),
        name="first_slice",
    )(meta, adjoint, probe, trans)
    return outs, total


def lane_group(shape):
    return lax.broadcasted_iota(jnp.int32, shape, 1) // BSIDE


def to_strips(blocks):
    flat = blocks.reshape(-1, BSIDE * BSIDE)

    def kernel(flat, *refs):
        outs, lanes = refs[:-1], refs[-1]
        group = lane_group((8, 128))
        for ag in range(8):
            lanes[ag] = flat[:, ag * 128 : (ag + 1) * 128]
        for s in range(SLICES):
            for t in range(2):
                tall = []
                for ag in range(8):
                    chunk = [
                        lanes[ag, pl.ds(t * 128 + band * 8 + 2 * s + c, 8, stride=16), :]
                        for band in range(2)
                        for c in range(2)
                    ]
                    for a4 in range(4):
                        value = None
                        for n in range(4):
                            move = (n - a4) % 4 * BSIDE
                            moved = pltpu.roll(chunk[n], move, 1) if move else chunk[n]
                            value = moved if n == 0 else jnp.where(group == n, moved, value)
                        tall.append(value)
                for half in range(2):
                    square = jnp.concatenate(tall[half * 16 : half * 16 + 16], axis=0)
                    square = jnp.transpose(square).astype(BF16)
                    for n in range(4):
                        outs[s][n // 2, n % 2, :, pl.ds(t * PATCH + half * 128, 128)] = square[
                            n * BSIDE : (n + 1) * BSIDE
                        ]

    return pl.pallas_call(
        kernel,
        out_shape=[jax.ShapeDtypeStruct((2, 2, BSIDE, TALL), BF16)] * SLICES,
        in_specs=[vmem_spec()],
        out_specs=[vmem_spec()] * SLICES,
        scratch_shapes=[pltpu.VMEM((8, flat.shape[0], 128), F32)],
        compiler_params=params(),
        cost_estimate=pl.CostEstimate(flops=0, bytes_accessed=2 << 20, transcendentals=0),
        name="to_strips",
    )(flat)


def to_blocks(terms):
    counts = [len(term) for term in terms]

    def kernel(*refs):
        out, lanes = refs[-2:]
        group = lane_group((8, 128))
        start = 0
        for s in range(SLICES):
            parts = refs[start : start + counts[s]]
            start += counts[s]
            for t in range(2):
                for half in range(2):
                    pieces = []
                    for n in range(4):
                        spot = (n // 2, n % 2, slice(None), pl.ds(t * PATCH + half * 128, 128))
                        value = parts[0][spot].astype(F32)
                        for part in parts[1:]:
                            value = value + part[spot].astype(F32)
                        pieces.append(value)
                    tall = jnp.transpose(jnp.concatenate(pieces, axis=0))
                    for g in range(4):
                        chunk = [tall[(g * 4 + a4) * 8 : (g * 4 + a4) * 8 + 8] for a4 in range(4)]
                        ag = half * 4 + g
                        for n in range(4):
                            value = None
                            for a4 in range(4):
                                move = (a4 - n) % 4 * BSIDE
                                moved = pltpu.roll(chunk[a4], move, 1) if move else chunk[a4]
                                value = moved if a4 == 0 else jnp.where(group == a4, moved, value)
                            row = t * 128 + n // 2 * 8 + 2 * s + n % 2
                            lanes[ag, pl.ds(row, 8, stride=16), :] = value
        for ag in range(8):
            out[:, ag * 128 : (ag + 1) * 128] = lanes[ag]

    flat = [part for term in terms for part in term]
    out = pl.pallas_call(
        kernel,
        out_shape=jax.ShapeDtypeStruct((FOOT * COL_BANDS * 2 * SLICES, BSIDE * BSIDE), F32),
        in_specs=[vmem_spec()] * len(flat),
        out_specs=vmem_spec(),
        scratch_shapes=[pltpu.VMEM((8, FOOT * COL_BANDS * 2 * SLICES, 128), F32)],
        compiler_params=params(),
        cost_estimate=pl.CostEstimate(flops=0, bytes_accessed=2 << 20, transcendentals=0),
        name="to_blocks",
    )(*flat)
    return out.reshape(FOOT * COL_BANDS, 2 * SLICES, BSIDE * BSIDE)


def work(meta, get_sources, probe, amplitudes, pieces):
    patches = amplitudes.shape[0]
    hr, hl, fl, fr = tables()
    probes = wrap_probe(meta, probe, patches)
    carried, trans = [probes], []
    for layer in range(SLICES - 1):
        t, q = forward(layer, meta, get_sources(layer), carried[-1], hr, hl, patches)
        trans.append(t)
        carried.append(q)
    grads = [None] * SLICES
    grads[-1], adjoint = far_field(
        meta, get_sources(SLICES - 1), carried[-1], amplitudes, (hr, hl, fl, fr), pieces, patches
    )
    for layer in range(SLICES - 2, 0, -1):
        grads[layer], adjoint = backward(
            layer, meta, adjoint, carried[layer], trans[layer], hr, hl, pieces, patches
        )
    grads[0], total = first_slice(meta, adjoint, probes, trans[0], pieces, patches)
    return grads, total


def describe(top, left, source_of, target_of, last):
    first = left // BSIDE
    strips = jnp.minimum(first[:, None] + jnp.arange(WIN, dtype=jnp.int32)[None, :], last)
    columns = [top[:, None], (left % BSIDE)[:, None], source_of(strips), target_of(strips)]
    return jnp.concatenate(columns, axis=1).astype(jnp.int32)


RING = (0, 1, 3, 2)


def ring_place(z):
    return z ^ (z >> 1)


def scan_pairs(move):
    out = []
    for i in range(16):
        z, y, core = i // 4, i // 2 % 2, i % 2
        z, y, core = move(z, y, core)
        out.append((i, z * 4 + y * 2 + core))
    return out


def ring_pairs(steps):
    return scan_pairs(lambda z, y, core: (RING[(RING.index(z) + steps) % 4], y, core))


Y_PAIRS = scan_pairs(lambda z, y, core: (z, 1 - y, core))
CORE_PAIRS = scan_pairs(lambda z, y, core: (z, y, 1 - core))


def send(value, pairs):
    return lax.ppermute(value, "scan", pairs)


def gather_slice(own):
    ring = [own]
    for _ in range(3):
        ring.append(send(ring[-1], ring_pairs(1)))
    line = jnp.concatenate(ring, axis=0)
    line_core = send(line, CORE_PAIRS)
    plane = send(line, Y_PAIRS)
    plane_core = send(plane, CORE_PAIRS)
    return (line, plane, line_core, plane_core)


def widen(value):
    return value.astype(F32)


def scatter_slice(grads):
    here, over_y, over_core = grads
    came = send(over_core, CORE_PAIRS)
    over_y = (widen(over_y) + widen(came[8:])).astype(BF16)
    came_y = send(over_y, Y_PAIRS)
    line = (widen(here) + widen(came[:8]) + widen(came_y)).astype(BF16)
    line = line.reshape(4, COL_BANDS, *line.shape[1:])
    return [line[0]] + [send(line[d], ring_pairs(d)) for d in range(1, 4)]


def sum_probe(total, n_terms):
    core = lax.axis_index("scan") % 2
    mine = jnp.where(core == 0, total[0], total[1])
    theirs = jnp.where(core == 0, total[1], total[0])
    mine = (widen(mine) + widen(send(theirs, CORE_PAIRS))).astype(BF16)
    mine = (widen(mine) + widen(send(mine, Y_PAIRS))).astype(BF16)
    parts = [send(mine, ring_pairs(d)) for d in range(1, 4)]
    mine = sum((widen(part) for part in parts), widen(mine)) / math.sqrt(n_terms)
    other = send(mine, CORE_PAIRS)
    return jnp.where(core == 0, jnp.stack([mine, other]), jnp.stack([other, mine]))


def on_small(object_blocks, probe, positions, anchors, amplitudes):
    me = lax.axis_index("scan")
    z, y, core = me // 4, me // 2 % 2, me % 2
    corner = anchors[0] * BSIDE

    def place(strips, sign):
        owner, band = strips % OWN_COLS, strips // OWN_COLS
        step = (sign * (ring_place(owner // 4) - ring_place(z))) % 4
        over = (owner % 2 ^ core) * 8 + (owner // 2 % 2 ^ y) * 4 + step
        return over * COL_BANDS + band

    meta = describe(
        positions[:, 0] + corner[0],
        positions[:, 1] + corner[1],
        lambda strips: place(strips, -1),
        lambda strips: place(strips, 1),
        OWN_COLS * COL_BANDS - 1,
    )
    own = to_strips(object_blocks)
    sources = [gather_slice(part) for part in own]
    grads, total = work(meta, lambda s: sources[s], probe, amplitudes, (8, 8, 16))
    terms = [scatter_slice(grad) for grad in grads]
    n_terms = lax.axis_size("scan") * positions.shape[0]
    return (to_blocks(terms), sum_probe(total, n_terms))


def footprint_slots(anchor_row, anchor_col, target, slot_number, own_rows):
    per_col = FOOT // OWN_COLS
    first_row = (target // OWN_COLS - anchor_row) % own_rows
    first_col = (target % OWN_COLS - anchor_col) % OWN_COLS
    inner_row = first_row + own_rows * (slot_number // per_col)
    inner_col = first_col + OWN_COLS * (slot_number % per_col)
    row_block = anchor_row + inner_row
    col_block = anchor_col + inner_col
    local = row_block // own_rows * COL_BANDS + col_block // OWN_COLS
    return (inner_row * FOOT + inner_col, local)


def on_any(object_blocks, probe, positions, anchors, amplitudes):
    n_scan = lax.axis_size("scan")
    own_rows = n_scan // OWN_COLS
    capacity = FOOT * FOOT // n_scan
    per_col = FOOT // OWN_COLS
    channels = object_blocks.shape[1]
    anchor_row = anchors[0, 0]
    anchor_col = anchors[0, 1]
    targets = jnp.arange(n_scan, dtype=jnp.int32)[:, None]
    slots = jnp.arange(capacity, dtype=jnp.int32)[None, :]
    send_order, wanted = footprint_slots(anchor_row, anchor_col, targets, slots, own_rows)
    inner = jnp.arange(FOOT, dtype=jnp.int32)
    inner_row = inner[:, None]
    inner_col = inner[None, :]
    holder = (anchor_row + inner_row) % own_rows * OWN_COLS + (anchor_col + inner_col) % OWN_COLS
    arrival = (holder * capacity + inner_row // own_rows * per_col + inner_col // OWN_COLS).reshape(
        -1
    )
    stored = object_blocks.astype(BF16)
    asked = lax.all_to_all(wanted, "scan", split_axis=0, concat_axis=0, tiled=True)
    found = jnp.take(stored, asked, axis=0)
    received = lax.all_to_all(found, "scan", split_axis=0, concat_axis=0, tiled=True)
    footprint = jnp.take(
        received.reshape(n_scan * capacity, channels, BSIDE * BSIDE), arrival, axis=0
    )
    strips = (
        footprint.reshape(2, 8, FOOT, SLICES, 2, BSIDE, BSIDE)
        .transpose(3, 2, 4, 6, 0, 5, 1)
        .reshape(SLICES, FOOT, 2, BSIDE, TALL)
    )
    meta = describe(
        positions[:, 0], positions[:, 1], lambda strips: strips, lambda strips: strips, FOOT - 1
    )
    grads, total = work(meta, lambda s: (strips[s],), probe, amplitudes, (FOOT,))
    blocked = (
        jnp.stack([grad[0] for grad in grads])
        .reshape(SLICES, FOOT, 2, BSIDE, 2, BSIDE, 8)
        .transpose(4, 6, 1, 0, 2, 5, 3)
        .reshape(FOOT * FOOT, channels, BSIDE * BSIDE)
    )
    outgoing = jnp.take(blocked, send_order.reshape(-1), axis=0).reshape(
        n_scan, capacity, channels, BSIDE * BSIDE
    )
    incoming = lax.all_to_all(outgoing, "scan", split_axis=0, concat_axis=0, tiled=True)
    owned = jnp.arange(object_blocks.shape[0], dtype=jnp.int32)
    selector = (asked.reshape(-1)[:, None] == owned[None, :]).astype(F32)
    object_gradient = jnp.einsum(
        "sk,scb->kcb",
        selector,
        incoming.reshape(n_scan * capacity, channels, BSIDE * BSIDE).astype(F32),
        precision=lax.Precision.HIGHEST,
    )
    summed = lax.psum(widen(total), "scan")
    return (object_gradient, summed / math.sqrt(n_scan * positions.shape[0]))


def solution(mesh):
    in_specs = (
        P(("group", "scan"), None, None),
        P("group", None, None),
        P(("group", "scan"), None),
        P(("group", "scan"), None),
        P(("group", "scan"), None, None),
    )
    out_specs = (P(("group", "scan"), None, None), P("group", None, None))
    small = mesh.shape["scan"] == OWN_COLS
    return jax.shard_map(
        on_small if small else on_any,
        mesh=mesh,
        in_specs=in_specs,
        out_specs=out_specs,
        check_vma=False,
    )
```

profile of v0, /device:TPU:0, one launch (start us, length us, event | category | flops | bytes accessed | tf_op | source)
XLA Modules:
  0.0 220.9 jit_solution(16339043141573702339)
XLA Ops:
  2.7 3.1 %collective-permute-start = (bf16[2,2,32,512]{3,2,1,0:T(8,128)(2,1)S(1)}, bf16[2,2,32,512]{3,2,1,0:T(8,128)(2,1)S(1)}, u32[]{:S(2)}, u32[]{:S(2)}) collective-permute-start(bf16[2,2,32,512]{3,2,1,0:T(8,128)(2,1)S(1)} %get-tuple-element.28), channel_id=1, source_target_pairs={{0,4},{1,5},{2,6},{3,7},{4,12},{5,13},{6,14},{7,15},{8,0},{9,1},{1... | collective-permute-start | bytes 393224 | tf_op jit(solution)/shard_map/ppermute | solution.py:632
  5.8 2.6 %collective-permute-start.6 = (bf16[2,2,32,512]{3,2,1,0:T(8,128)(2,1)S(1)}, bf16[2,2,32,512]{3,2,1,0:T(8,128)(2,1)S(1)}, u32[]{:S(2)}, u32[]{:S(2)}) collective-permute-start(bf16[2,2,32,512]{3,2,1,0:T(8,128)(2,1)S(1)} %get-tuple-element.29), channel_id=1, source_target_pairs={{0,4},{1,5},{2,6},{3,7},{4,12},{5,13},{6,14},{7,15},{8,0},{9,1},{1... | collective-permute-start | bytes 393224 | tf_op jit(solution)/shard_map/ppermute | solution.py:632
  22.0 3.2 %collective-permute-done.7 = bf16[2,2,32,512]{3,2,1,0:T(8,128)(2,1)S(1)} collective-permute-done((bf16[2,2,32,512]{3,2,1,0:T(8,128)(2,1)S(1)}, bf16[2,2,32,512]{3,2,1,0:T(8,128)(2,1)S(1)}, u32[]{:S(2)}, u32[]{:S(2)}) %collective-permute-start.7) | collective-permute-done | bytes 131104 | tf_op jit(solution)/shard_map/ppermute | solution.py:632
  26.4 4.5 %collective-permute-done.19 = bf16[2,2,32,512]{3,2,1,0:T(8,128)(2,1)S(1)} collective-permute-done((bf16[2,2,32,512]{3,2,1,0:T(8,128)(2,1)S(1)}, bf16[2,2,32,512]{3,2,1,0:T(8,128)(2,1)S(1)}, u32[]{:S(2)}, u32[]{:S(2)}) %collective-permute-start.19) | collective-permute-done | bytes 131104 | tf_op jit(solution)/shard_map/ppermute | solution.py:632
  39.6 3.3 %collective-permute-start.14 = (bf16[2,2,32,512]{3,2,1,0:T(8,128)(2,1)S(1)}, bf16[2,2,32,512]{3,2,1,0:T(8,128)(2,1)S(1)}, u32[]{:S(2)}, u32[]{:S(2)}) collective-permute-start(bf16[2,2,32,512]{3,2,1,0:T(8,128)(2,1)S(1)} %collective-permute-done.13), channel_id=1, source_target_pairs={{0,4},{1,5},{2,6},{3,7},{4,12},{5,13},{6,14},{7,15},{8,0},{9,1},{1... | collective-permute-start | bytes 393224 | tf_op jit(solution)/shard_map/ppermute | solution.py:632
  43.7 2.3 %collective-permute-done.14 = bf16[2,2,32,512]{3,2,1,0:T(8,128)(2,1)S(1)} collective-permute-done((bf16[2,2,32,512]{3,2,1,0:T(8,128)(2,1)S(1)}, bf16[2,2,32,512]{3,2,1,0:T(8,128)(2,1)S(1)}, u32[]{:S(2)}, u32[]{:S(2)}) %collective-permute-start.14) | collective-permute-done | bytes 131104 | tf_op jit(solution)/shard_map/ppermute | solution.py:632
  49.7 9.3 %collective-permute-done.21.refs_1_ = bf16[8,2,32,512]{3,2,1,0:T(8,128)(2,1)S(1)} collective-permute-done((bf16[8,2,32,512]{3,2,1,0:T(8,128)(2,1)S(1)}, bf16[8,2,32,512]{3,2,1,0:T(8,128)(2,1)S(1)}, u32[]{:S(2)}, u32[]{:S(2)}) %collective-permute-start.21) | collective-permute-done | bytes 524320 | tf_op jit(solution)/shard_map/ppermute | solution.py:632
  61.8 18.0 %collective-permute-done.3.refs_1_ = bf16[8,2,32,512]{3,2,1,0:T(8,128)(2,1)} collective-permute-done((bf16[8,2,32,512]{3,2,1,0:T(8,128)(2,1)}, bf16[8,2,32,512]{3,2,1,0:T(8,128)(2,1)}, u32[]{:S(2)}, u32[]{:S(2)}) %collective-permute-start.3) | collective-permute-done | bytes 524320 | tf_op jit(solution)/shard_map/ppermute | solution.py:632
  82.9 3.3 %wrap_probe.1.refs_4_.probe = f32[2,2,256,256]{3,2,1,0:T(8,128)S(1)} custom-call(s32[2,20]{1,0:T(2,128)S(1)} %pad_add_fusion.meta, f32[2,256,256]{2,1,0:T(8,128)S(1)} %copy-done.5), custom_call_target="tpu_custom_call" | custom-call | flops 1610612736 | bytes 2097152 | tf_op jit(solution)/shard_map/wrap_probe/pallas_call | solution.py:222
  86.3 3.7 %forward_0.1 = (bf16[512,512]{1,0:T(8,128)(2,1)S(1)}, bf16[512,512]{1,0:T(8,128)(2,1)S(1)}) custom-call(s32[2,20]{1,0:T(2,128)S(1)} %pad_add_fusion.meta, bf16[8,2,32,512]{3,2,1,0:T(8,128)(2,1)S(1)} %constant_dynamic-update-slice_fusion.12.refs_0_, bf16[8,2,32,512]{3,2,1,0:T(8,128)(2,1)S(1)} %collective-permute-done.21.refs_1_, ...), custom_call_target="tpu_custom_call" | custom-call | flops 536870912 | bytes 4194304 | tf_op jit(solution)/shard_map/forward_0/pallas_call | solution.py:260
  90.1 3.6 %forward_1.1 = (bf16[512,512]{1,0:T(8,128)(2,1)S(1)}, bf16[512,512]{1,0:T(8,128)(2,1)S(1)}) custom-call(s32[2,20]{1,0:T(2,128)S(1)} %pad_add_fusion.meta, bf16[8,2,32,512]{3,2,1,0:T(8,128)(2,1)S(1)} %constant_dynamic-update-slice_fusion.8.refs_0_, bf16[8,2,32,512]{3,2,1,0:T(8,128)(2,1)} %collective-permute-done.15.refs_1_, ...), custom_call_target="tpu_custom_call" | custom-call | flops 536870912 | bytes 4194304 | tf_op jit(solution)/shard_map/forward_1/pallas_call | solution.py:260
  93.7 3.3 %forward_2.1 = (bf16[512,512]{1,0:T(8,128)(2,1)S(1)}, bf16[512,512]{1,0:T(8,128)(2,1)S(1)}) custom-call(s32[2,20]{1,0:T(2,128)S(1)} %pad_add_fusion.meta, bf16[8,2,32,512]{3,2,1,0:T(8,128)(2,1)S(1)} %constant_dynamic-update-slice_fusion.4.refs_0_, bf16[8,2,32,512]{3,2,1,0:T(8,128)(2,1)} %collective-permute-done.9.refs_1_, ...), custom_call_target="tpu_custom_call" | custom-call | flops 536870912 | bytes 4194304 | tf_op jit(solution)/shard_map/forward_2/pallas_call | solution.py:260
  97.0 7.6 %far_field.1 = (bf16[8,2,32,512]{3,2,1,0:T(8,128)(2,1)S(1)}, bf16[8,2,32,512]{3,2,1,0:T(8,128)(2,1)S(1)}, bf16[16,2,32,512]{3,2,1,0:T(8,128)(2,1)}, bf16[512,512]{1,0:T(8,128)(2,1)S(1)}) custom-call(s32[2,20]{1,0:T(2,128)S(1)} %pad_add_fusion.meta, bf16[8,2,32,512]{3,2,1,0:T(8,128)(2,1)} %constant_dynamic-update-slice_fusion.refs_0_, ...), custom_call_target="tpu_custom_call" | custom-call | flops 2147483648 | bytes 8388608 | tf_op jit(solution)/shard_map/far_field/pallas_call | solution.py:369
  104.7 2.4 %backward_2.1 = (bf16[8,2,32,512]{3,2,1,0:T(8,128)(2,1)S(1)}, bf16[8,2,32,512]{3,2,1,0:T(8,128)(2,1)S(1)}, bf16[16,2,32,512]{3,2,1,0:T(8,128)(2,1)S(1)}, bf16[512,512]{1,0:T(8,128)(2,1)S(1)}) custom-call(s32[2,20]{1,0:T(2,128)S(1)} %pad_add_fusion.meta, bf16[512,512]{1,0:T(8,128)(2,1)S(1)} %get-tuple-element.35.adjoint, ...), custom_call_target="tpu_custom_call" | custom-call | flops 536870912 | bytes 6291456 | tf_op jit(solution)/shard_map/backward_2/pallas_call | solution.py:419
  107.1 2.4 %backward_1.1 = (bf16[8,2,32,512]{3,2,1,0:T(8,128)(2,1)S(1)}, bf16[8,2,32,512]{3,2,1,0:T(8,128)(2,1)S(1)}, bf16[16,2,32,512]{3,2,1,0:T(8,128)(2,1)S(1)}, bf16[512,512]{1,0:T(8,128)(2,1)S(1)}) custom-call(s32[2,20]{1,0:T(2,128)S(1)} %pad_add_fusion.meta, bf16[512,512]{1,0:T(8,128)(2,1)S(1)} %get-tuple-element.37.adjoint, ...), custom_call_target="tpu_custom_call" | custom-call | flops 536870912 | bytes 6291456 | tf_op jit(solution)/shard_map/backward_1/pallas_call | solution.py:419
  109.4 2.1 first_slice.1
  115.1 4.1 %collective-permute-done.45 = bf16[256,256]{1,0:T(8,128)(2,1)S(1)} collective-permute-done((bf16[256,256]{1,0:T(8,128)(2,1)S(1)}, bf16[256,256]{1,0:T(8,128)(2,1)S(1)}, u32[]{:S(2)}, u32[]{:S(2)}) %collective-permute-start.45) | collective-permute-done | bytes 131104 | tf_op jit(solution)/shard_map/ppermute | solution.py:632
  120.7 2.0 collective-permute-start.47
  124.3 3.4 %collective-permute-start.46 = (bf16[256,256]{1,0:T(8,128)(2,1)S(1)}, bf16[256,256]{1,0:T(8,128)(2,1)S(1)}, u32[]{:S(2)}, u32[]{:S(2)}) collective-permute-start(bf16[256,256]{1,0:T(8,128)(2,1)S(1)} %add_convert_fusion.8), channel_id=1, source_target_pairs={{0,4},{1,5},{2,6},{3,7},{4,12},{5,13},{6,14},{7,15},{8,0},{9,1},{1... | collective-permute-start | bytes 393224 | tf_op jit(solution)/shard_map/ppermute | solution.py:632
  127.7 2.2 collective-permute-done.47
  129.9 4.4 %collective-permute-done.46 = bf16[256,256]{1,0:T(8,128)(2,1)S(1)} collective-permute-done((bf16[256,256]{1,0:T(8,128)(2,1)S(1)}, bf16[256,256]{1,0:T(8,128)(2,1)S(1)}, u32[]{:S(2)}, u32[]{:S(2)}) %collective-permute-start.46) | collective-permute-done | bytes 131104 | tf_op jit(solution)/shard_map/ppermute | solution.py:632
  139.4 9.9 %collective-permute-done.25 = bf16[8,2,32,512]{3,2,1,0:T(8,128)(2,1)S(1)} collective-permute-done((bf16[8,2,32,512]{3,2,1,0:T(8,128)(2,1)S(1)}, bf16[8,2,32,512]{3,2,1,0:T(8,128)(2,1)S(1)}, u32[]{:S(2)}, u32[]{:S(2)}) %collective-permute-start.25) | collective-permute-done | bytes 524320 | tf_op jit(solution)/shard_map/ppermute | solution.py:632
  149.8 10.9 %collective-permute-done.30 = bf16[8,2,32,512]{3,2,1,0:T(8,128)(2,1)S(1)} collective-permute-done((bf16[8,2,32,512]{3,2,1,0:T(8,128)(2,1)S(1)}, bf16[8,2,32,512]{3,2,1,0:T(8,128)(2,1)S(1)}, u32[]{:S(2)}, u32[]{:S(2)}) %collective-permute-start.30) | collective-permute-done | bytes 524320 | tf_op jit(solution)/shard_map/ppermute | solution.py:632
  162.5 9.3 %collective-permute-done.35 = bf16[8,2,32,512]{3,2,1,0:T(8,128)(2,1)S(1)} collective-permute-done((bf16[8,2,32,512]{3,2,1,0:T(8,128)(2,1)S(1)}, bf16[8,2,32,512]{3,2,1,0:T(8,128)(2,1)S(1)}, u32[]{:S(2)}, u32[]{:S(2)}) %collective-permute-start.35) | collective-permute-done | bytes 524320 | tf_op jit(solution)/shard_map/ppermute | solution.py:632
  172.1 10.6 %collective-permute-done.40 = bf16[8,2,32,512]{3,2,1,0:T(8,128)(2,1)S(1)} collective-permute-done((bf16[8,2,32,512]{3,2,1,0:T(8,128)(2,1)S(1)}, bf16[8,2,32,512]{3,2,1,0:T(8,128)(2,1)S(1)}, u32[]{:S(2)}, u32[]{:S(2)}) %collective-permute-start.40) | collective-permute-done | bytes 524320 | tf_op jit(solution)/shard_map/ppermute | solution.py:632
  187.7 2.3 %collective-permute-start.37 = (bf16[2,2,32,512]{3,2,1,0:T(8,128)(2,1)S(1)}, bf16[2,2,32,512]{3,2,1,0:T(8,128)(2,1)S(1)}, u32[]{:S(2)}, u32[]{:S(2)}) collective-permute-start(bf16[2,2,32,512]{3,2,1,0:T(8,128)(2,1)S(1)} %get-tuple-element.59), channel_id=1, source_target_pairs={{0,12},{1,13},{2,14},{3,15},{4,8},{5,9},{6,10},{7,11},{8,4},{9,5},... | collective-permute-start | bytes 393224 | tf_op jit(solution)/shard_map/ppermute | solution.py:632
  191.3 4.4 %collective-permute-start.43 = (bf16[2,2,32,512]{3,2,1,0:T(8,128)(2,1)S(1)}, bf16[2,2,32,512]{3,2,1,0:T(8,128)(2,1)S(1)}, u32[]{:S(2)}, u32[]{:S(2)}) collective-permute-start(bf16[2,2,32,512]{3,2,1,0:T(8,128)(2,1)S(1)} %get-tuple-element.54), channel_id=1, source_target_pairs={{0,8},{1,9},{2,10},{3,11},{4,0},{5,1},{6,2},{7,3},{8,12},{9,13},{1... | collective-permute-start | bytes 393224 | tf_op jit(solution)/shard_map/ppermute | solution.py:632
  195.7 6.9 %collective-permute-done.31.refs_5_ = bf16[2,2,32,512]{3,2,1,0:T(8,128)(2,1)S(1)} collective-permute-done((bf16[2,2,32,512]{3,2,1,0:T(8,128)(2,1)S(1)}, bf16[2,2,32,512]{3,2,1,0:T(8,128)(2,1)S(1)}, u32[]{:S(2)}, u32[]{:S(2)}) %collective-permute-start.31) | collective-permute-done | bytes 131104 | tf_op jit(solution)/shard_map/ppermute | solution.py:632
  202.6 2.4 %collective-permute-start.42 = (bf16[2,2,32,512]{3,2,1,0:T(8,128)(2,1)S(1)}, bf16[2,2,32,512]{3,2,1,0:T(8,128)(2,1)S(1)}, u32[]{:S(2)}, u32[]{:S(2)}) collective-permute-start(bf16[2,2,32,512]{3,2,1,0:T(8,128)(2,1)S(1)} %get-tuple-element.55), channel_id=1, source_target_pairs={{0,12},{1,13},{2,14},{3,15},{4,8},{5,9},{6,10},{7,11},{8,4},{9,5},... | collective-permute-start | bytes 393224 | tf_op jit(solution)/shard_map/ppermute | solution.py:632
  205.9 7.2 %collective-permute-done.36.refs_9_ = bf16[2,2,32,512]{3,2,1,0:T(8,128)(2,1)S(1)} collective-permute-done((bf16[2,2,32,512]{3,2,1,0:T(8,128)(2,1)S(1)}, bf16[2,2,32,512]{3,2,1,0:T(8,128)(2,1)S(1)}, u32[]{:S(2)}, u32[]{:S(2)}) %collective-permute-start.36) | collective-permute-done | bytes 131104 | tf_op jit(solution)/shard_map/ppermute | solution.py:632
  213.1 5.5 %collective-permute-done.41.refs_13_ = bf16[2,2,32,512]{3,2,1,0:T(8,128)(2,1)S(1)} collective-permute-done((bf16[2,2,32,512]{3,2,1,0:T(8,128)(2,1)S(1)}, bf16[2,2,32,512]{3,2,1,0:T(8,128)(2,1)S(1)}, u32[]{:S(2)}, u32[]{:S(2)}) %collective-permute-start.41) | collective-permute-done | bytes 131104 | tf_op jit(solution)/shard_map/ppermute | solution.py:632
  218.6 2.2 %to_blocks.1 = f32[256,1024]{1,0:T(8,128)} custom-call(bf16[2,2,32,512]{3,2,1,0:T(8,128)(2,1)S(1)} %get-tuple-element.69.refs_0_, bf16[2,2,32,512]{3,2,1,0:T(8,128)(2,1)S(1)} %collective-permute-done.26.refs_1_, bf16[2,2,32,512]{3,2,1,0:T(8,128)(2,1)S(1)} %collective-permute-done.27.refs_2_, bf16[2,2,32,512]{3,2,1,0:T(8,128)(2,1)S(1)} %collective-permute-done.28.refs_3_, ...), custom_call_target="tpu_custom_call" | custom-call | bytes 2097152 | tf_op jit(solution)/shard_map/to_blocks/pallas_call | solution.py:566
  (134 shorter events, 57.3 us)
Async XLA Ops:
  11.2 27.5 %collective-permute-start.1 = (bf16[2,2,32,512]{3,2,1,0:T(8,128)(2,1)S(1)}, bf16[2,2,32,512]{3,2,1,0:T(8,128)(2,1)S(1)}, u32[]{:S(2)}, u32[]{:S(2)}) collective-permute-start(bf16[2,2,32,512]{3,2,1,0:T(8,128)(2,1)S(1)} %collective-permute-done), channel_id=1, source_target_pairs={{0,4},{1,5},{2,6},{3,7},{4,12},{5,13},{6,14},{7,15},{8,0},{9,1},{1... | collective-permute-start | bytes 393224 | tf_op jit(solution)/shard_map/ppermute | solution.py:632
  14.0 11.2 %collective-permute-start.7 = (bf16[2,2,32,512]{3,2,1,0:T(8,128)(2,1)S(1)}, bf16[2,2,32,512]{3,2,1,0:T(8,128)(2,1)S(1)}, u32[]{:S(2)}, u32[]{:S(2)}) collective-permute-start(bf16[2,2,32,512]{3,2,1,0:T(8,128)(2,1)S(1)} %collective-permute-done.6), channel_id=1, source_target_pairs={{0,4},{1,5},{2,6},{3,7},{4,12},{5,13},{6,14},{7,15},{8,0},{9,1},{1... | collective-permute-start | bytes 393224 | tf_op jit(solution)/shard_map/ppermute | solution.py:632
  16.8 22.8 %collective-permute-start.13 = (bf16[2,2,32,512]{3,2,1,0:T(8,128)(2,1)S(1)}, bf16[2,2,32,512]{3,2,1,0:T(8,128)(2,1)S(1)}, u32[]{:S(2)}, u32[]{:S(2)}) collective-permute-start(bf16[2,2,32,512]{3,2,1,0:T(8,128)(2,1)S(1)} %collective-permute-done.12), channel_id=1, source_target_pairs={{0,4},{1,5},{2,6},{3,7},{4,12},{5,13},{6,14},{7,15},{8,0},{9,1},{1... | collective-permute-start | bytes 393224 | tf_op jit(solution)/shard_map/ppermute | solution.py:632
  19.6 11.2 %collective-permute-start.19 = (bf16[2,2,32,512]{3,2,1,0:T(8,128)(2,1)S(1)}, bf16[2,2,32,512]{3,2,1,0:T(8,128)(2,1)S(1)}, u32[]{:S(2)}, u32[]{:S(2)}) collective-permute-start(bf16[2,2,32,512]{3,2,1,0:T(8,128)(2,1)S(1)} %collective-permute-done.18), channel_id=1, source_target_pairs={{0,4},{1,5},{2,6},{3,7},{4,12},{5,13},{6,14},{7,15},{8,0},{9,1},{1... | collective-permute-start | bytes 393224 | tf_op jit(solution)/shard_map/ppermute | solution.py:632
  32.8 15.0 %collective-permute-start.9 = (bf16[8,2,32,512]{3,2,1,0:T(8,128)(2,1)S(1)}, bf16[8,2,32,512]{3,2,1,0:T(8,128)(2,1)}, u32[]{:S(2)}, u32[]{:S(2)}) collective-permute-start(bf16[8,2,32,512]{3,2,1,0:T(8,128)(2,1)S(1)} %constant_dynamic-update-slice_fusion.4.refs_0_), channel_id=1, source_target_pairs={{0,2},{1,3},{2,0},{3,1},{4,6},{5,7},{6,4},{7,5},{8,10},{9,11},{10,... | collective-permute-start | bytes 1572872 | tf_op jit(solution)/shard_map/ppermute | solution.py:632
  36.7 22.3 %collective-permute-start.21 = (bf16[8,2,32,512]{3,2,1,0:T(8,128)(2,1)S(1)}, bf16[8,2,32,512]{3,2,1,0:T(8,128)(2,1)S(1)}, u32[]{:S(2)}, u32[]{:S(2)}) collective-permute-start(bf16[8,2,32,512]{3,2,1,0:T(8,128)(2,1)S(1)} %constant_dynamic-update-slice_fusion.12.refs_0_), channel_id=1, source_target_pairs={{0,2},{1,3},{2,0},{3,1},{4,6},{5,7},{6,4},{7,5},{8,10},{9,11},{10,... | collective-permute-start | bytes 1572872 | tf_op jit(solution)/shard_map/ppermute | solution.py:632
  43.6 36.2 %collective-permute-start.22 = (bf16[8,2,32,512]{3,2,1,0:T(8,128)(2,1)S(1)}, bf16[8,2,32,512]{3,2,1,0:T(8,128)(2,1)S(1)}, u32[]{:S(2)}, u32[]{:S(2)}) collective-permute-start(bf16[8,2,32,512]{3,2,1,0:T(8,128)(2,1)S(1)} %constant_dynamic-update-slice_fusion.12.refs_0_), channel_id=1, source_target_pairs={{0,1},{1,0},{2,3},{3,2},{4,5},{5,4},{6,7},{7,6},{8,9},{9,8},{10,11... | collective-permute-start | bytes 1572872 | tf_op jit(solution)/shard_map/ppermute | solution.py:632
  46.0 34.3 %collective-permute-start.16 = (bf16[8,2,32,512]{3,2,1,0:T(8,128)(2,1)S(1)}, bf16[8,2,32,512]{3,2,1,0:T(8,128)(2,1)S(1)}, u32[]{:S(2)}, u32[]{:S(2)}) collective-permute-start(bf16[8,2,32,512]{3,2,1,0:T(8,128)(2,1)S(1)} %constant_dynamic-update-slice_fusion.8.refs_0_), channel_id=1, source_target_pairs={{0,1},{1,0},{2,3},{3,2},{4,5},{5,4},{6,7},{7,6},{8,9},{9,8},{10,11... | collective-permute-start | bytes 1572872 | tf_op jit(solution)/shard_map/ppermute | solution.py:632
  46.1 35.0 %collective-permute-start.15 = (bf16[8,2,32,512]{3,2,1,0:T(8,128)(2,1)S(1)}, bf16[8,2,32,512]{3,2,1,0:T(8,128)(2,1)}, u32[]{:S(2)}, u32[]{:S(2)}) collective-permute-start(bf16[8,2,32,512]{3,2,1,0:T(8,128)(2,1)S(1)} %constant_dynamic-update-slice_fusion.8.refs_0_), channel_id=1, source_target_pairs={{0,2},{1,3},{2,0},{3,1},{4,6},{5,7},{6,4},{7,5},{8,10},{9,11},{10,... | collective-permute-start | bytes 1572872 | tf_op jit(solution)/shard_map/ppermute | solution.py:632
  47.8 32.0 %collective-permute-start.3 = (bf16[8,2,32,512]{3,2,1,0:T(8,128)(2,1)}, bf16[8,2,32,512]{3,2,1,0:T(8,128)(2,1)}, u32[]{:S(2)}, u32[]{:S(2)}) collective-permute-start(bf16[8,2,32,512]{3,2,1,0:T(8,128)(2,1)} %constant_dynamic-update-slice_fusion.refs_0_), channel_id=1, source_target_pairs={{0,2},{1,3},{2,0},{3,1},{4,6},{5,7},{6,4},{7,5},{8,10},{9,11},{10,... | collective-permute-start | bytes 1572872 | tf_op jit(solution)/shard_map/ppermute | solution.py:632
  59.0 22.7 %collective-permute-start.23 = (bf16[8,2,32,512]{3,2,1,0:T(8,128)(2,1)S(1)}, bf16[8,2,32,512]{3,2,1,0:T(8,128)(2,1)S(1)}, u32[]{:S(2)}, u32[]{:S(2)}) collective-permute-start(bf16[8,2,32,512]{3,2,1,0:T(8,128)(2,1)S(1)} %collective-permute-done.21.refs_1_), channel_id=1, source_target_pairs={{0,1},{1,0},{2,3},{3,2},{4,5},{5,4},{6,7},{7,6},{8,9},{9,8},{10,11... | collective-permute-start | bytes 1572872 | tf_op jit(solution)/shard_map/ppermute | solution.py:632
  79.8 13.9 %collective-permute-start.10 = (bf16[8,2,32,512]{3,2,1,0:T(8,128)(2,1)S(1)}, bf16[8,2,32,512]{3,2,1,0:T(8,128)(2,1)}, u32[]{:S(2)}, u32[]{:S(2)}) collective-permute-start(bf16[8,2,32,512]{3,2,1,0:T(8,128)(2,1)S(1)} %constant_dynamic-update-slice_fusion.4.refs_0_), channel_id=1, source_target_pairs={{0,1},{1,0},{2,3},{3,2},{4,5},{5,4},{6,7},{7,6},{8,9},{9,8},{10,11... | collective-permute-start | bytes 1572872 | tf_op jit(solution)/shard_map/ppermute | solution.py:632
  79.8 17.2 %collective-permute-start.4 = (bf16[8,2,32,512]{3,2,1,0:T(8,128)(2,1)}, bf16[8,2,32,512]{3,2,1,0:T(8,128)(2,1)}, u32[]{:S(2)}, u32[]{:S(2)}) collective-permute-start(bf16[8,2,32,512]{3,2,1,0:T(8,128)(2,1)} %constant_dynamic-update-slice_fusion.refs_0_), channel_id=1, source_target_pairs={{0,1},{1,0},{2,3},{3,2},{4,5},{5,4},{6,7},{7,6},{8,9},{9,8},{10,11... | collective-permute-start | bytes 1572872 | tf_op jit(solution)/shard_map/ppermute | solution.py:632
  81.1 12.6 %collective-permute-start.11 = (bf16[8,2,32,512]{3,2,1,0:T(8,128)(2,1)}, bf16[8,2,32,512]{3,2,1,0:T(8,128)(2,1)}, u32[]{:S(2)}, u32[]{:S(2)}) collective-permute-start(bf16[8,2,32,512]{3,2,1,0:T(8,128)(2,1)} %collective-permute-done.9.refs_1_), channel_id=1, source_target_pairs={{0,1},{1,0},{2,3},{3,2},{4,5},{5,4},{6,7},{7,6},{8,9},{9,8},{10,11... | collective-permute-start | bytes 1572872 | tf_op jit(solution)/shard_map/ppermute | solution.py:632
  81.1 15.9 %collective-permute-start.5 = (bf16[8,2,32,512]{3,2,1,0:T(8,128)(2,1)}, bf16[8,2,32,512]{3,2,1,0:T(8,128)(2,1)}, u32[]{:S(2)}, u32[]{:S(2)}) collective-permute-start(bf16[8,2,32,512]{3,2,1,0:T(8,128)(2,1)} %collective-permute-done.3.refs_1_), channel_id=1, source_target_pairs={{0,1},{1,0},{2,3},{3,2},{4,5},{5,4},{6,7},{7,6},{8,9},{9,8},{10,11... | collective-permute-start | bytes 1572872 | tf_op jit(solution)/shard_map/ppermute | solution.py:632
  112.3 22.1 %collective-permute-start.24 = (bf16[16,2,32,512]{3,2,1,0:T(8,128)(2,1)S(1)}, bf16[16,2,32,512]{3,2,1,0:T(8,128)(2,1)S(1)}, u32[]{:S(2)}, u32[]{:S(2)}) collective-permute-start(bf16[16,2,32,512]{3,2,1,0:T(8,128)(2,1)S(1)} %get-tuple-element.42), channel_id=1, source_target_pairs={{0,1},{1,0},{2,3},{3,2},{4,5},{5,4},{6,7},{7,6},{8,9},{9,8},{10,11... | collective-permute-start | bytes 3145736 | tf_op jit(solution)/shard_map/ppermute | solution.py:632
  114.6 21.1 %collective-permute-start.29 = (bf16[16,2,32,512]{3,2,1,0:T(8,128)(2,1)S(1)}, bf16[16,2,32,512]{3,2,1,0:T(8,128)(2,1)S(1)}, u32[]{:S(2)}, u32[]{:S(2)}) collective-permute-start(bf16[16,2,32,512]{3,2,1,0:T(8,128)(2,1)S(1)} %get-tuple-element.45), channel_id=1, source_target_pairs={{0,1},{1,0},{2,3},{3,2},{4,5},{5,4},{6,7},{7,6},{8,9},{9,8},{10,11... | collective-permute-start | bytes 3145736 | tf_op jit(solution)/shard_map/ppermute | solution.py:632
  114.6 22.3 %collective-permute-start.34 = (bf16[16,2,32,512]{3,2,1,0:T(8,128)(2,1)S(1)}, bf16[16,2,32,512]{3,2,1,0:T(8,128)(2,1)S(1)}, u32[]{:S(2)}, u32[]{:S(2)}) collective-permute-start(bf16[16,2,32,512]{3,2,1,0:T(8,128)(2,1)S(1)} %get-tuple-element.48), channel_id=1, source_target_pairs={{0,1},{1,0},{2,3},{3,2},{4,5},{5,4},{6,7},{7,6},{8,9},{9,8},{10,11... | collective-permute-start | bytes 3145736 | tf_op jit(solution)/shard_map/ppermute | solution.py:632
  134.3 48.7 %collective-permute-start.49 = (f32[256,256]{1,0:T(8,128)S(1)}, f32[256,256]{1,0:T(8,128)S(1)}, u32[]{:S(2)}, u32[]{:S(2)}) collective-permute-start(f32[256,256]{1,0:T(8,128)S(1)} %add_multiply_fusion), channel_id=1, source_target_pairs={{0,1},{1,0},{2,3},{3,2},{4,5},{5,4},{6,7},{7,6},{8,9},{9,8},{10,11... | collective-permute-start | bytes 786440 | tf_op jit(solution)/shard_map/ppermute | solution.py:632
  134.6 14.8 %collective-permute-start.25 = (bf16[8,2,32,512]{3,2,1,0:T(8,128)(2,1)S(1)}, bf16[8,2,32,512]{3,2,1,0:T(8,128)(2,1)S(1)}, u32[]{:S(2)}, u32[]{:S(2)}) collective-permute-start(bf16[8,2,32,512]{3,2,1,0:T(8,128)(2,1)S(1)} %add_convert_fusion.7), channel_id=1, source_target_pairs={{0,2},{1,3},{2,0},{3,1},{4,6},{5,7},{6,4},{7,5},{8,10},{9,11},{10,... | collective-permute-start | bytes 1572872 | tf_op jit(solution)/shard_map/ppermute | solution.py:632
  135.9 24.7 %collective-permute-start.30 = (bf16[8,2,32,512]{3,2,1,0:T(8,128)(2,1)S(1)}, bf16[8,2,32,512]{3,2,1,0:T(8,128)(2,1)S(1)}, u32[]{:S(2)}, u32[]{:S(2)}) collective-permute-start(bf16[8,2,32,512]{3,2,1,0:T(8,128)(2,1)S(1)} %add_convert_fusion.5), channel_id=1, source_target_pairs={{0,2},{1,3},{2,0},{3,1},{4,6},{5,7},{6,4},{7,5},{8,10},{9,11},{10,... | collective-permute-start | bytes 1572872 | tf_op jit(solution)/shard_map/ppermute | solution.py:632
  137.1 34.7 %collective-permute-start.35 = (bf16[8,2,32,512]{3,2,1,0:T(8,128)(2,1)S(1)}, bf16[8,2,32,512]{3,2,1,0:T(8,128)(2,1)S(1)}, u32[]{:S(2)}, u32[]{:S(2)}) collective-permute-start(bf16[8,2,32,512]{3,2,1,0:T(8,128)(2,1)S(1)} %add_convert_fusion.3), channel_id=1, source_target_pairs={{0,2},{1,3},{2,0},{3,1},{4,6},{5,7},{6,4},{7,5},{8,10},{9,11},{10,... | collective-permute-start | bytes 1572872 | tf_op jit(solution)/shard_map/ppermute | solution.py:632
  138.4 44.3 %collective-permute-start.40 = (bf16[8,2,32,512]{3,2,1,0:T(8,128)(2,1)S(1)}, bf16[8,2,32,512]{3,2,1,0:T(8,128)(2,1)S(1)}, u32[]{:S(2)}, u32[]{:S(2)}) collective-permute-start(bf16[8,2,32,512]{3,2,1,0:T(8,128)(2,1)S(1)} %add_convert_fusion.1), channel_id=1, source_target_pairs={{0,2},{1,3},{2,0},{3,1},{4,6},{5,7},{6,4},{7,5},{8,10},{9,11},{10,... | collective-permute-start | bytes 1572872 | tf_op jit(solution)/shard_map/ppermute | solution.py:632
  149.7 35.0 %collective-permute-start.28 = (bf16[2,2,32,512]{3,2,1,0:T(8,128)(2,1)S(1)}, bf16[2,2,32,512]{3,2,1,0:T(8,128)(2,1)S(1)}, u32[]{:S(2)}, u32[]{:S(2)}) collective-permute-start(bf16[2,2,32,512]{3,2,1,0:T(8,128)(2,1)S(1)} %get-tuple-element.66), channel_id=1, source_target_pairs={{0,8},{1,9},{2,10},{3,11},{4,0},{5,1},{6,2},{7,3},{8,12},{9,13},{1... | collective-permute-start | bytes 393224 | tf_op jit(solution)/shard_map/ppermute | solution.py:632
  160.6 25.2 %collective-permute-start.27 = (bf16[2,2,32,512]{3,2,1,0:T(8,128)(2,1)S(1)}, bf16[2,2,32,512]{3,2,1,0:T(8,128)(2,1)S(1)}, u32[]{:S(2)}, u32[]{:S(2)}) collective-permute-start(bf16[2,2,32,512]{3,2,1,0:T(8,128)(2,1)S(1)} %get-tuple-element.67), channel_id=1, source_target_pairs={{0,12},{1,13},{2,14},{3,15},{4,8},{5,9},{6,10},{7,11},{8,4},{9,5},... | collective-permute-start | bytes 393224 | tf_op jit(solution)/shard_map/ppermute | solution.py:632
  171.9 15.8 %collective-permute-start.26 = (bf16[2,2,32,512]{3,2,1,0:T(8,128)(2,1)S(1)}, bf16[2,2,32,512]{3,2,1,0:T(8,128)(2,1)S(1)}, u32[]{:S(2)}, u32[]{:S(2)}) collective-permute-start(bf16[2,2,32,512]{3,2,1,0:T(8,128)(2,1)S(1)} %get-tuple-element.68), channel_id=1, source_target_pairs={{0,4},{1,5},{2,6},{3,7},{4,12},{5,13},{6,14},{7,15},{8,0},{9,1},{1... | collective-permute-start | bytes 393224 | tf_op jit(solution)/shard_map/ppermute | solution.py:632
  184.7 17.9 %collective-permute-start.31 = (bf16[2,2,32,512]{3,2,1,0:T(8,128)(2,1)S(1)}, bf16[2,2,32,512]{3,2,1,0:T(8,128)(2,1)S(1)}, u32[]{:S(2)}, u32[]{:S(2)}) collective-permute-start(bf16[2,2,32,512]{3,2,1,0:T(8,128)(2,1)S(1)} %get-tuple-element.64), channel_id=1, source_target_pairs={{0,4},{1,5},{2,6},{3,7},{4,12},{5,13},{6,14},{7,15},{8,0},{9,1},{1... | collective-permute-start | bytes 393224 | tf_op jit(solution)/shard_map/ppermute | solution.py:632
  185.8 19.2 %collective-permute-start.38 = (bf16[2,2,32,512]{3,2,1,0:T(8,128)(2,1)S(1)}, bf16[2,2,32,512]{3,2,1,0:T(8,128)(2,1)S(1)}, u32[]{:S(2)}, u32[]{:S(2)}) collective-permute-start(bf16[2,2,32,512]{3,2,1,0:T(8,128)(2,1)S(1)} %get-tuple-element.58), channel_id=1, source_target_pairs={{0,8},{1,9},{2,10},{3,11},{4,0},{5,1},{6,2},{7,3},{8,12},{9,13},{1... | collective-permute-start | bytes 393224 | tf_op jit(solution)/shard_map/ppermute | solution.py:632
  187.7 18.2 %collective-permute-start.37 = (bf16[2,2,32,512]{3,2,1,0:T(8,128)(2,1)S(1)}, bf16[2,2,32,512]{3,2,1,0:T(8,128)(2,1)S(1)}, u32[]{:S(2)}, u32[]{:S(2)}) collective-permute-start(bf16[2,2,32,512]{3,2,1,0:T(8,128)(2,1)S(1)} %get-tuple-element.59), channel_id=1, source_target_pairs={{0,12},{1,13},{2,14},{3,15},{4,8},{5,9},{6,10},{7,11},{8,4},{9,5},... | collective-permute-start | bytes 393224 | tf_op jit(solution)/shard_map/ppermute | solution.py:632
  190.7 22.4 %collective-permute-start.36 = (bf16[2,2,32,512]{3,2,1,0:T(8,128)(2,1)S(1)}, bf16[2,2,32,512]{3,2,1,0:T(8,128)(2,1)S(1)}, u32[]{:S(2)}, u32[]{:S(2)}) collective-permute-start(bf16[2,2,32,512]{3,2,1,0:T(8,128)(2,1)S(1)} %get-tuple-element.60), channel_id=1, source_target_pairs={{0,4},{1,5},{2,6},{3,7},{4,12},{5,13},{6,14},{7,15},{8,0},{9,1},{1... | collective-permute-start | bytes 393224 | tf_op jit(solution)/shard_map/ppermute | solution.py:632
  191.3 21.8 %collective-permute-start.43 = (bf16[2,2,32,512]{3,2,1,0:T(8,128)(2,1)S(1)}, bf16[2,2,32,512]{3,2,1,0:T(8,128)(2,1)S(1)}, u32[]{:S(2)}, u32[]{:S(2)}) collective-permute-start(bf16[2,2,32,512]{3,2,1,0:T(8,128)(2,1)S(1)} %get-tuple-element.54), channel_id=1, source_target_pairs={{0,8},{1,9},{2,10},{3,11},{4,0},{5,1},{6,2},{7,3},{8,12},{9,13},{1... | collective-permute-start | bytes 393224 | tf_op jit(solution)/shard_map/ppermute | solution.py:632
  205.1 13.6 %collective-permute-start.41 = (bf16[2,2,32,512]{3,2,1,0:T(8,128)(2,1)S(1)}, bf16[2,2,32,512]{3,2,1,0:T(8,128)(2,1)S(1)}, u32[]{:S(2)}, u32[]{:S(2)}) collective-permute-start(bf16[2,2,32,512]{3,2,1,0:T(8,128)(2,1)S(1)} %get-tuple-element.56), channel_id=1, source_target_pairs={{0,4},{1,5},{2,6},{3,7},{4,12},{5,13},{6,14},{7,15},{8,0},{9,1},{1... | collective-permute-start | bytes 393224 | tf_op jit(solution)/shard_map/ppermute | solution.py:632
  (28 other events, 187.1 us)
where the time goes:
time: 221 us
  waiting for transfers between devices  121 us (55%)
  starting transfers between devices  55.4 us (25%)
  Pallas kernels  31.6 us (14%)
  local copies, waits for them, and re-layouts  7.33 us (3%)
  other arithmetic  4.33 us (2%)
    ppermute x50, waiting for transfers between devices, send(): return lax.ppermute(value, 'scan', pairs)  121 us
    ppermute x50, starting transfers between devices, send(): return lax.ppermute(value, 'scan', pairs)  55.4 us
    pallas_call x3, Pallas kernels, forward(): pl.pallas_call(kernel, out_shape=(plane, plane), in_specs=[smem_spec()] +...  10.6 us
    pallas_call x1, Pallas kernels, far_field(): pl.pallas_call(kernel, out_shape=(*strips, plane), in_specs=[smem_spec()]...  7.65 us
    unnamed x30, local copies, waits for them, and re-layouts  5.85 us
    pallas_call x2, Pallas kernels, backward(): pl.pallas_call(kernel, out_shape=(*strips, plane), in_specs=[smem_spec()]...  4.73 us
  transfers between devices with their start and end apart: 50, of which 26 were waited for; matrix products, arithmetic and copies ran while one was open for 4% of the time, Pallas kernels for 6%

commit v1 on v0

--- a/solution.py
+++ b/solution.py
@@ -17,7 +17,7 @@
 FLOOR = 0.25
 WIN = 9
 TALL = FOOT * BSIDE
-VMEM_BYTES = 48 * 1024 * 1024
+VMEM_BYTES = 20 * 1024 * 1024
 F32 = jnp.float32
 BF16 = jnp.bfloat16
 
@@ -197,10 +197,8 @@
     return pltpu.CompilerParams(vmem_limit_bytes=VMEM_BYTES)
 
 
-def cost(products, bytes_accessed):
-    return pl.CostEstimate(
-        flops=products * 8 * PATCH**3, bytes_accessed=bytes_accessed, transcendentals=0
-    )
+def cost(microseconds):
+    return pl.CostEstimate(flops=0, bytes_accessed=int(microseconds * 3.6e6), transcendentals=0)
 
 
 def wrap_probe(meta, probe, patches):
@@ -225,7 +223,7 @@
         in_specs=[smem_spec(), vmem_spec()],
         out_specs=vmem_spec(),
         compiler_params=params(),
-        cost_estimate=cost(patches * 6, 2 << 20),
+        cost_estimate=cost(3.3),
         name="wrap_probe",
     )(meta, probe)
 
@@ -269,7 +267,7 @@
             pltpu.SemaphoreType.DMA((patches, WIN)),
         ],
         compiler_params=params(),
-        cost_estimate=cost(patches * 2, 4 << 20),
+        cost_estimate=cost(3.5),
         name=f"forward_{layer}",
     )(meta, *sources, before, right, left)
 
@@ -382,7 +380,7 @@
             pltpu.SemaphoreType.DMA((n_out,)),
         ],
         compiler_params=params(),
-        cost_estimate=cost(patches * 8, 8 << 20),
+        cost_estimate=cost(7.5),
         name="far_field",
     )(meta, *sources, before, amplitudes, *tabs)
     return outs, after
@@ -428,7 +426,7 @@
             pltpu.SemaphoreType.DMA((n_out,)),
         ],
         compiler_params=params(),
-        cost_estimate=cost(patches * 2, 6 << 20),
+        cost_estimate=cost(2.3),
         name=f"backward_{layer}",
     )(meta, adjoint, carried, trans, right, left)
     return outs, after
@@ -474,7 +472,7 @@
             pltpu.SemaphoreType.DMA((n_out,)),
         ],
         compiler_params=params(),
-        cost_estimate=cost(patches, 6 << 20),
+        cost_estimate=cost(2.3),
         name="first_slice",
     )(meta, adjoint, probe, trans)
     return outs, total
@@ -523,7 +521,7 @@
         out_specs=[vmem_spec()] * SLICES,
         scratch_shapes=[pltpu.VMEM((8, flat.shape[0], 128), F32)],
         compiler_params=params(),
-        cost_estimate=pl.CostEstimate(flops=0, bytes_accessed=2 << 20, transcendentals=0),
+        cost_estimate=cost(1.5),
         name="to_strips",
     )(flat)
 
@@ -570,31 +568,14 @@
         out_specs=vmem_spec(),
         scratch_shapes=[pltpu.VMEM((8, FOOT * COL_BANDS * 2 * SLICES, 128), F32)],
         compiler_params=params(),
-        cost_estimate=pl.CostEstimate(flops=0, bytes_accessed=2 << 20, transcendentals=0),
+        cost_estimate=cost(1.5),
         name="to_blocks",
     )(*flat)
     return out.reshape(FOOT * COL_BANDS, 2 * SLICES, BSIDE * BSIDE)
 
 
-def work(meta, get_sources, probe, amplitudes, pieces):
-    patches = amplitudes.shape[0]
-    hr, hl, fl, fr = tables()
-    probes = wrap_probe(meta, probe, patches)
-    carried, trans = [probes], []
-    for layer in range(SLICES - 1):
-        t, q = forward(layer, meta, get_sources(layer), carried[-1], hr, hl, patches)
-        trans.append(t)
-        carried.append(q)
-    grads = [None] * SLICES
-    grads[-1], adjoint = far_field(
-        meta, get_sources(SLICES - 1), carried[-1], amplitudes, (hr, hl, fl, fr), pieces, patches
-    )
-    for layer in range(SLICES - 2, 0, -1):
-        grads[layer], adjoint = backward(
-            layer, meta, adjoint, carried[layer], trans[layer], hr, hl, pieces, patches
-        )
-    grads[0], total = first_slice(meta, adjoint, probes, trans[0], pieces, patches)
-    return grads, total
+def after(value, *events):
+    return lax.optimization_barrier((value, *events))[0]
 
 
 def describe(top, left, source_of, target_of, last):
@@ -604,95 +585,153 @@
     return jnp.concatenate(columns, axis=1).astype(jnp.int32)
 
 
-RING = (0, 1, 3, 2)
-
-
-def ring_place(z):
-    return z ^ (z >> 1)
-
-
-def scan_pairs(move):
-    out = []
-    for i in range(16):
-        z, y, core = i // 4, i // 2 % 2, i % 2
-        z, y, core = move(z, y, core)
-        out.append((i, z * 4 + y * 2 + core))
-    return out
-
-
-def ring_pairs(steps):
-    return scan_pairs(lambda z, y, core: (RING[(RING.index(z) + steps) % 4], y, core))
-
-
-Y_PAIRS = scan_pairs(lambda z, y, core: (z, 1 - y, core))
-CORE_PAIRS = scan_pairs(lambda z, y, core: (z, y, 1 - core))
-
-
-def send(value, pairs):
-    return lax.ppermute(value, "scan", pairs)
-
-
-def gather_slice(own):
-    ring = [own]
-    for _ in range(3):
-        ring.append(send(ring[-1], ring_pairs(1)))
-    line = jnp.concatenate(ring, axis=0)
-    line_core = send(line, CORE_PAIRS)
-    plane = send(line, Y_PAIRS)
-    plane_core = send(plane, CORE_PAIRS)
-    return (line, plane, line_core, plane_core)
+FAR, NEAR, OVER_Y, OVER_CORE = 8, 4, 2, 1
+
+
+def swap(value, bit):
+    return lax.ppermute(value, "scan", [(i, i ^ bit) for i in range(16)])
+
+
+def join(*values):
+    return jnp.concatenate(values, axis=0)
 
 
 def widen(value):
     return value.astype(F32)
 
 
-def scatter_slice(grads):
-    here, over_y, over_core = grads
-    came = send(over_core, CORE_PAIRS)
-    over_y = (widen(over_y) + widen(came[8:])).astype(BF16)
-    came_y = send(over_y, Y_PAIRS)
-    line = (widen(here) + widen(came[:8]) + widen(came_y)).astype(BF16)
-    line = line.reshape(4, COL_BANDS, *line.shape[1:])
-    return [line[0]] + [send(line[d], ring_pairs(d)) for d in range(1, 4)]
-
-
-def sum_probe(total, n_terms):
-    core = lax.axis_index("scan") % 2
+def plus(value, *others):
+    return sum((widen(other) for other in others), widen(value)).astype(BF16)
+
+
+def slots(owner, order):
+    bits = [(owner & bit) // bit * 2**n for n, bit in enumerate(order)]
+    return sum(bits[1:], bits[0])
+
+
+LINE_FIRST = (FAR, NEAR, OVER_Y, OVER_CORE)
+PLANE_FIRST = (OVER_Y, FAR, NEAR, OVER_CORE)
+
+
+def sum_probe(total, n_terms, events):
+    me = lax.axis_index("scan")
+    core, y = me % 2, me // 2 % 2
     mine = jnp.where(core == 0, total[0], total[1])
     theirs = jnp.where(core == 0, total[1], total[0])
-    mine = (widen(mine) + widen(send(theirs, CORE_PAIRS))).astype(BF16)
-    mine = (widen(mine) + widen(send(mine, Y_PAIRS))).astype(BF16)
-    parts = [send(mine, ring_pairs(d)) for d in range(1, 4)]
-    mine = sum((widen(part) for part in parts), widen(mine)) / math.sqrt(n_terms)
-    other = send(mine, CORE_PAIRS)
+    mine = plus(mine, swap(after(theirs, events[0]), OVER_CORE))
+    mine = mine.reshape(2, PATCH // 2, PATCH)
+    theirs = jnp.where(y == 0, mine[1], mine[0])
+    mine = jnp.where(y == 0, mine[0], mine[1])
+    mine = plus(mine, swap(after(theirs, events[1]), OVER_Y))
+    mine = plus(mine, swap(after(mine, events[2]), NEAR))
+    mine = (widen(mine) + widen(swap(after(mine, events[3]), FAR))) / math.sqrt(n_terms)
+    other = swap(after(mine, events[4]), OVER_Y)
+    mine = jnp.where(y == 0, join(mine, other), join(other, mine))
+    other = swap(after(mine, events[5]), OVER_CORE)
     return jnp.where(core == 0, jnp.stack([mine, other]), jnp.stack([other, mine]))
 
 
 def on_small(object_blocks, probe, positions, anchors, amplitudes):
     me = lax.axis_index("scan")
-    z, y, core = me // 4, me // 2 % 2, me % 2
     corner = anchors[0] * BSIDE
-
-    def place(strips, sign):
-        owner, band = strips % OWN_COLS, strips // OWN_COLS
-        step = (sign * (ring_place(owner // 4) - ring_place(z))) % 4
-        over = (owner % 2 ^ core) * 8 + (owner // 2 % 2 ^ y) * 4 + step
-        return over * COL_BANDS + band
-
-    meta = describe(
-        positions[:, 0] + corner[0],
-        positions[:, 1] + corner[1],
-        lambda strips: place(strips, -1),
-        lambda strips: place(strips, 1),
-        OWN_COLS * COL_BANDS - 1,
-    )
+    patches = positions.shape[0]
+
+    def described(order):
+        def place(strips):
+            return slots(strips % OWN_COLS ^ me, order) * COL_BANDS + strips // OWN_COLS
+
+        return describe(
+            positions[:, 0] + corner[0],
+            positions[:, 1] + corner[1],
+            place,
+            place,
+            OWN_COLS * COL_BANDS - 1,
+        )
+
+    meta, meta_last = described(LINE_FIRST), described(PLANE_FIRST)
+    hr, hl, fl, fr = tables()
+    probes = wrap_probe(meta, probe, patches)
     own = to_strips(object_blocks)
-    sources = [gather_slice(part) for part in own]
-    grads, total = work(meta, lambda s: sources[s], probe, amplitudes, (8, 8, 16))
-    terms = [scatter_slice(grad) for grad in grads]
-    n_terms = lax.axis_size("scan") * positions.shape[0]
-    return (to_blocks(terms), sum_probe(total, n_terms))
+
+    far0 = swap(own[0], FAR)
+    y0a = swap(own[0], OVER_Y)
+    y3 = swap(own[3], OVER_Y)
+    far1 = swap(after(own[1], far0), FAR)
+    near0 = swap(after(join(own[0], far0), probes), NEAR)
+    y0b = swap(after(far0, y0a, y3), OVER_Y)
+    far2 = swap(after(own[2], far0), FAR)
+    near1 = swap(after(join(own[1], far1), near0), NEAR)
+    y0c = swap(after(near0, y0b, far1), OVER_Y)
+    pair3 = join(own[3], y3)
+    far3 = swap(after(pair3, far1), FAR)
+    here1 = join(own[1], far1, near1)
+    y1 = swap(after(here1, y0c, far2), OVER_Y)
+    here0 = join(own[0], far0, near0, y0a, y0b, y0c)
+    core0 = swap(after(here0, near1, far2), OVER_CORE)
+    trans0, q1 = forward(0, meta, (here0, core0), probes, hr, hl, patches)
+    near2 = swap(after(join(own[2], far2), near1, q1), NEAR)
+    here2 = join(own[2], far2, near2)
+    here3 = join(pair3, far3)
+    near3 = swap(after(here3, near2), NEAR)
+    y2 = swap(after(here2, q1, y1, far3), OVER_Y)
+    here1 = join(here1, y1)
+    core1 = swap(after(here1, near2, far3, q1), OVER_CORE)
+    trans1, q2 = forward(1, meta, (here1, core1), q1, hr, hl, patches)
+    core3a = swap(after(here3, q2), OVER_CORE)
+    here2 = join(here2, y2)
+    core2 = swap(after(here2, core3a, near3), OVER_CORE)
+    trans2, q3 = forward(2, meta, (here2, core2), q2, hr, hl, patches)
+    core3b = swap(near3, OVER_CORE)
+
+    pieces = (8, 8, 16)
+    (here3, near3, core3), g2 = far_field(
+        meta_last,
+        (here3, near3, core3a, core3b),
+        q3,
+        amplitudes,
+        (hr, hl, fl, fr),
+        pieces,
+        patches,
+    )
+
+    came3 = swap(core3, OVER_CORE)
+    (here2, y2, core2), g1 = backward(2, meta, g2, q2, trans2, hr, hl, pieces, patches)
+    came2 = swap(core2, OVER_CORE)
+    near3 = swap(after(plus(near3, came3[8:]), g1), NEAR)
+    (here1, y1, core1), g0 = backward(1, meta, after(g1, came3), q1, trans1, hr, hl, pieces, patches)
+    came1 = swap(core1, OVER_CORE)
+    y2 = after(plus(y2, came2[8:]), g0)
+    (here0, y0, core0), total = first_slice(
+        meta, after(g0, y2), probes, trans0, pieces, patches
+    )
+    y2 = swap(y2, OVER_Y)
+    came0 = swap(core0, OVER_CORE)
+    y1 = plus(y1, came1[8:])
+    y0 = plus(y0, came0[8:])
+    line3 = plus(here3, came3[:8], near3)
+    far3 = swap(after(line3[4:], y1, y0), FAR)
+    y1 = swap(after(y1, total, y2), OVER_Y)
+    line2 = plus(here2, came2[:8], y2)
+    near2 = swap(line2[4:], NEAR)
+    y0 = swap(after(y0, y1), OVER_Y)
+    pair3 = plus(line3[:4], after(far3, y1))
+    y3 = swap(pair3[2:], OVER_Y)
+    line2 = plus(line2[:4], after(near2, y1))
+    far2 = swap(line2[2:], FAR)
+    line1 = plus(here1, came1[:8], y1)
+    near1 = swap(line1[4:], NEAR)
+    line1 = plus(line1[:4], after(near1, y0))
+    far1 = swap(line1[2:], FAR)
+    line0 = plus(here0, came0[:8], y0)
+    near0 = swap(line0[4:], NEAR)
+    line0 = plus(line0[:4], near0)
+    far0 = swap(line0[2:], FAR)
+    probe_gradient = sum_probe(
+        total, lax.axis_size("scan") * patches, (y2, y1, y1, y3, y0, near0)
+    )
+    far0 = after(far0, probe_gradient)
+    terms = [(line0[:2], far0), (line1[:2], far1), (line2[:2], far2), (pair3[:2], y3)]
+    return (to_blocks(terms), probe_gradient)
 
 
 def footprint_slots(anchor_row, anchor_col, target, slot_number, own_rows):
@@ -705,6 +744,27 @@
     col_block = anchor_col + inner_col
     local = row_block // own_rows * COL_BANDS + col_block // OWN_COLS
     return (inner_row * FOOT + inner_col, local)
+
+
+def work(meta, sources, probe, amplitudes, pieces):
+    patches = amplitudes.shape[0]
+    hr, hl, fl, fr = tables()
+    probes = wrap_probe(meta, probe, patches)
+    carried, trans = [probes], []
+    for layer in range(SLICES - 1):
+        t, q = forward(layer, meta, sources[layer], carried[-1], hr, hl, patches)
+        trans.append(t)
+        carried.append(q)
+    grads = [None] * SLICES
+    grads[-1], adjoint = far_field(
+        meta, sources[-1], carried[-1], amplitudes, (hr, hl, fl, fr), pieces, patches
+    )
+    for layer in range(SLICES - 2, 0, -1):
+        grads[layer], adjoint = backward(
+            layer, meta, adjoint, carried[layer], trans[layer], hr, hl, pieces, patches
+        )
+    grads[0], total = first_slice(meta, adjoint, probes, trans[0], pieces, patches)
+    return grads, total
 
 
 def on_any(object_blocks, probe, positions, anchors, amplitudes):
@@ -740,7 +800,8 @@
     meta = describe(
         positions[:, 0], positions[:, 1], lambda strips: strips, lambda strips: strips, FOOT - 1
     )
-    grads, total = work(meta, lambda s: (strips[s],), probe, amplitudes, (FOOT,))
+    sources = [(strips[s],) for s in range(SLICES)]
+    grads, total = work(meta, sources, probe, amplitudes, (FOOT,))
     blocked = (
         jnp.stack([grad[0] for grad in grads])
         .reshape(SLICES, FOOT, 2, BSIDE, 2, BSIDE, 8)

time: 221 us -> 171 us (0.77)
  waiting for transfers between devices: 121 us -> 84.4 us
  starting transfers between devices: 55.4 us -> 37.2 us
  other arithmetic: 4.33 us -> 11 us
  local copies, waits for them, and re-layouts: 7.33 us -> 4.68 us
    ppermute x50 -> x41, waiting for transfers between devices: 121 us -> 84.4 us  [swap(): return lax.ppermute(value, 'scan', [(i, i ^ bit) for i in range(16)])]
    ppermute x50 -> x41, starting transfers between devices: 55.4 us -> 37.2 us  [swap(): return lax.ppermute(value, 'scan', [(i, i ^ bit) for i in range(16)])]
    convert_element_type x10 -> x15, other arithmetic: 1.73 us -> 8.22 us  [plus(): return sum((widen(other) for other in others), widen(value)).astype(BF16)]
    unnamed x30 -> x47, local copies, waits for them, and re-layouts: 5.85 us -> 3.84 us
  transfers between devices with their start and end apart: 50 -> 41, of which waited for: 26 -> 23; matrix products, arithmetic and copies ran while one was open for 4% -> 7% of each run, Pallas kernels for 6% -> 12%
where the time goes in v1:
time: 171 us
  waiting for transfers between devices  84.4 us (49%)
  starting transfers between devices  37.2 us (22%)
  Pallas kernels  32 us (19%)
  other arithmetic  11 us (6%)
  local copies, waits for them, and re-layouts  4.68 us (3%)
    ppermute x41, waiting for transfers between devices, swap(): return lax.ppermute(value, 'scan', [(i, i ^ bit) for i in range(16)])  84.4 us
    ppermute x41, starting transfers between devices, swap(): return lax.ppermute(value, 'scan', [(i, i ^ bit) for i in range(16)])  37.2 us
    pallas_call x3, Pallas kernels, forward(): pl.pallas_call(kernel, out_shape=(plane, plane), in_specs=[smem_spec()] +...  10.6 us
    convert_element_type x15, other arithmetic, plus(): return sum((widen(other) for other in others), widen(value)).astype(BF16)  8.22 us
    pallas_call x1, Pallas kernels, far_field(): pl.pallas_call(kernel, out_shape=(*strips, plane), in_specs=[smem_spec()]...  7.65 us
    pallas_call x2, Pallas kernels, backward(): pl.pallas_call(kernel, out_shape=(*strips, plane), in_specs=[smem_spec()]...  4.97 us
    unnamed x47, local copies, waits for them, and re-layouts  3.84 us
  transfers between devices with their start and end apart: 41, of which 23 were waited for; matrix products, arithmetic and copies ran while one was open for 7% of the time, Pallas kernels for 12%

profile of v1, /device:TPU:0, one launch (start us, length us, event | category | flops | bytes accessed | tf_op | source)
XLA Modules:
  0.0 170.7 jit_solution(7469874286424103645)
XLA Ops:
  2.7 3.0 %collective-permute-start.7 = (bf16[2,2,32,512]{3,2,1,0:T(8,128)(2,1)S(1)}, bf16[2,2,32,512]{3,2,1,0:T(8,128)(2,1)S(1)}, u32[]{:S(2)}, u32[]{:S(2)}) collective-permute-start(bf16[2,2,32,512]{3,2,1,0:T(8,128)(2,1)S(1)} %get-tuple-element.62), channel_id=1, source_target_pairs={{0,2},{1,3},{2,0},{3,1},{4,6},{5,7},{6,4},{7,5},{8,10},{9,11},{10,... | collective-permute-start | bytes 393224 | tf_op jit(solution)/shard_map/ppermute | solution.py:592
  5.8 2.6 %collective-permute-start.1 = (bf16[2,2,32,512]{3,2,1,0:T(8,128)(2,1)S(1)}, bf16[2,2,32,512]{3,2,1,0:T(8,128)(2,1)S(1)}, u32[]{:S(2)}, u32[]{:S(2)}) collective-permute-start(bf16[2,2,32,512]{3,2,1,0:T(8,128)(2,1)S(1)} %get-tuple-element.62), channel_id=1, source_target_pairs={{0,8},{1,9},{2,10},{3,11},{4,12},{5,13},{6,14},{7,15},{8,0},{9,1},... | collective-permute-start | bytes 393224 | tf_op jit(solution)/shard_map/ppermute | solution.py:592
  12.5 3.3 %wrap_probe.1.refs_2_.probe = f32[2,2,256,256]{3,2,1,0:T(8,128)S(1)} custom-call(s32[2,20]{1,0:T(2,128)S(1)} %get-tuple-element.129.meta, f32[2,256,256]{2,1,0:T(8,128)S(1)} %copy-done.3), custom_call_target="tpu_custom_call" | custom-call | bytes 11880000 | tf_op jit(solution)/shard_map/wrap_probe/pallas_call | solution.py:220
  15.9 2.7 %collective-permute-start.5 = (bf16[4,2,32,512]{3,2,1,0:T(8,128)(2,1)S(1)}, bf16[4,2,32,512]{3,2,1,0:T(8,128)(2,1)S(1)}, u32[]{:S(2)}, u32[]{:S(2)}) collective-permute-start(bf16[4,2,32,512]{3,2,1,0:T(8,128)(2,1)S(1)} %pad_maximum_fusion.5), channel_id=1, source_target_pairs={{0,4},{1,5},{2,6},{3,7},{4,0},{5,1},{6,2},{7,3},{8,12},{9,13},{10,... | collective-permute-start | bytes 786440 | tf_op jit(solution)/shard_map/ppermute | solution.py:592
  22.1 2.9 %collective-permute-done.2 = bf16[2,2,32,512]{3,2,1,0:T(8,128)(2,1)S(1)} collective-permute-done((bf16[2,2,32,512]{3,2,1,0:T(8,128)(2,1)S(1)}, bf16[2,2,32,512]{3,2,1,0:T(8,128)(2,1)S(1)}, u32[]{:S(2)}, u32[]{:S(2)}) %collective-permute-start.2) | collective-permute-done | bytes 131104 | tf_op jit(solution)/shard_map/ppermute | solution.py:592
  25.5 4.1 %collective-permute-done.5 = bf16[4,2,32,512]{3,2,1,0:T(8,128)(2,1)S(1)} collective-permute-done((bf16[4,2,32,512]{3,2,1,0:T(8,128)(2,1)S(1)}, bf16[4,2,32,512]{3,2,1,0:T(8,128)(2,1)S(1)}, u32[]{:S(2)}, u32[]{:S(2)}) %collective-permute-start.5) | collective-permute-done | bytes 262176 | tf_op jit(solution)/shard_map/ppermute | solution.py:592
  31.0 6.3 %collective-permute-done.9 = bf16[4,2,32,512]{3,2,1,0:T(8,128)(2,1)S(1)} collective-permute-done((bf16[4,2,32,512]{3,2,1,0:T(8,128)(2,1)S(1)}, bf16[4,2,32,512]{3,2,1,0:T(8,128)(2,1)S(1)}, u32[]{:S(2)}, u32[]{:S(2)}) %collective-permute-start.9) | collective-permute-done | bytes 262176 | tf_op jit(solution)/shard_map/ppermute | solution.py:592
  38.9 2.8 %collective-permute-start.3 = (bf16[4,2,32,512]{3,2,1,0:T(8,128)(2,1)S(1)}, bf16[4,2,32,512]{3,2,1,0:T(8,128)(2,1)S(1)}, u32[]{:S(2)}, u32[]{:S(2)}) collective-permute-start(bf16[4,2,32,512]{3,2,1,0:T(8,128)(2,1)S(1)} %pad_maximum_fusion.2), channel_id=1, source_target_pairs={{0,8},{1,9},{2,10},{3,11},{4,12},{5,13},{6,14},{7,15},{8,0},{9,1},... | collective-permute-start | bytes 786440 | tf_op jit(solution)/shard_map/ppermute | solution.py:592
  41.7 3.5 %forward_0.1 = (bf16[512,512]{1,0:T(8,128)(2,1)S(1)}, bf16[512,512]{1,0:T(8,128)(2,1)S(1)}) custom-call(s32[2,20]{1,0:T(2,128)S(1)} %get-tuple-element.129.meta, bf16[16,2,32,512]{3,2,1,0:T(8,128)(2,1)S(1)} %constant_dynamic-update-slice_fusion.3.refs_0_, bf16[16,2,32,512]{3,2,1,0:T(8,128)(2,1)S(1)} %collective-permute-done.10.refs_1_, ...), custom_call_target="tpu_custom_call" | custom-call | bytes 12600000 | tf_op jit(solution)/shard_map/forward_0/pallas_call | solution.py:258
  45.7 6.2 %collective-permute-done.13 = bf16[8,2,32,512]{3,2,1,0:T(8,128)(2,1)S(1)} collective-permute-done((bf16[8,2,32,512]{3,2,1,0:T(8,128)(2,1)S(1)}, bf16[8,2,32,512]{3,2,1,0:T(8,128)(2,1)S(1)}, u32[]{:S(2)}, u32[]{:S(2)}) %collective-permute-start.13) | collective-permute-done | bytes 524320 | tf_op jit(solution)/shard_map/ppermute | solution.py:592
  54.1 3.8 %collective-permute-done.11 = bf16[4,2,32,512]{3,2,1,0:T(8,128)(2,1)S(1)} collective-permute-done((bf16[4,2,32,512]{3,2,1,0:T(8,128)(2,1)S(1)}, bf16[4,2,32,512]{3,2,1,0:T(8,128)(2,1)S(1)}, u32[]{:S(2)}, u32[]{:S(2)}) %collective-permute-start.11) | collective-permute-done | bytes 262176 | tf_op jit(solution)/shard_map/ppermute | solution.py:592
  60.6 3.6 %forward_1.1 = (bf16[512,512]{1,0:T(8,128)(2,1)S(1)}, bf16[512,512]{1,0:T(8,128)(2,1)S(1)}) custom-call(s32[2,20]{1,0:T(2,128)S(1)} %get-tuple-element.129.meta, bf16[16,2,32,512]{3,2,1,0:T(8,128)(2,1)S(1)} %constant_dynamic-update-slice_fusion.9.refs_0_, bf16[16,2,32,512]{3,2,1,0:T(8,128)(2,1)S(1)} %collective-permute-done.14.refs_1_, ...), custom_call_target="tpu_custom_call" | custom-call | bytes 12600000 | tf_op jit(solution)/shard_map/forward_1/pallas_call | solution.py:258
  64.4 8.0 %collective-permute-done.17 = bf16[8,2,32,512]{3,2,1,0:T(8,128)(2,1)S(1)} collective-permute-done((bf16[8,2,32,512]{3,2,1,0:T(8,128)(2,1)S(1)}, bf16[8,2,32,512]{3,2,1,0:T(8,128)(2,1)S(1)}, u32[]{:S(2)}, u32[]{:S(2)}) %collective-permute-start.17) | collective-permute-done | bytes 524320 | tf_op jit(solution)/shard_map/ppermute | solution.py:592
  75.2 3.6 %forward_2.1 = (bf16[512,512]{1,0:T(8,128)(2,1)S(1)}, bf16[512,512]{1,0:T(8,128)(2,1)S(1)}) custom-call(s32[2,20]{1,0:T(2,128)S(1)} %get-tuple-element.129.meta, bf16[16,2,32,512]{3,2,1,0:T(8,128)(2,1)S(1)} %constant_dynamic-update-slice_fusion.13.refs_0_, bf16[16,2,32,512]{3,2,1,0:T(8,128)(2,1)S(1)} %collective-permute-done.18.refs_1_, ...), custom_call_target="tpu_custom_call" | custom-call | bytes 12600000 | tf_op jit(solution)/shard_map/forward_2/pallas_call | solution.py:258
  78.9 7.6 %far_field.1 = (bf16[8,2,32,512]{3,2,1,0:T(8,128)(2,1)S(1)}, bf16[8,2,32,512]{3,2,1,0:T(8,128)(2,1)S(1)}, bf16[16,2,32,512]{3,2,1,0:T(8,128)(2,1)S(1)}, bf16[512,512]{1,0:T(8,128)(2,1)S(1)}) custom-call(s32[2,20]{1,0:T(2,128)S(1)} %get-tuple-element.128.meta, bf16[8,2,32,512]{3,2,1,0:T(8,128)(2,1)S(1)} %constant_dynamic-update-slice_fusion.refs_0_, ...), custom_call_target="tpu_custom_call" | custom-call | bytes 27000000 | tf_op jit(solution)/shard_map/far_field/pallas_call | solution.py:367
  86.7 2.4 %backward_2.1 = (bf16[8,2,32,512]{3,2,1,0:T(8,128)(2,1)S(1)}, bf16[8,2,32,512]{3,2,1,0:T(8,128)(2,1)S(1)}, bf16[16,2,32,512]{3,2,1,0:T(8,128)(2,1)S(1)}, bf16[512,512]{1,0:T(8,128)(2,1)S(1)}) custom-call(s32[2,20]{1,0:T(2,128)S(1)} %get-tuple-element.129.meta, bf16[512,512]{1,0:T(8,128)(2,1)S(1)} %get-tuple-element.82.adjoint, ...), custom_call_target="tpu_custom_call" | custom-call | bytes 8279999 | tf_op jit(solution)/shard_map/backward_2/pallas_call | solution.py:417
  90.9 2.6 %backward_1.1 = (bf16[8,2,32,512]{3,2,1,0:T(8,128)(2,1)S(1)}, bf16[8,2,32,512]{3,2,1,0:T(8,128)(2,1)S(1)}, bf16[16,2,32,512]{3,2,1,0:T(8,128)(2,1)}, bf16[512,512]{1,0:T(8,128)(2,1)S(1)}) custom-call(s32[2,20]{1,0:T(2,128)S(1)} %get-tuple-element.129.meta, bf16[512,512]{1,0:T(8,128)(2,1)S(1)} %get-tuple-element.86.adjoint, ...), custom_call_target="tpu_custom_call" | custom-call | bytes 8279999 | tf_op jit(solution)/shard_map/backward_1/pallas_call | solution.py:417
  97.7 2.3 %first_slice.1 = (bf16[8,2,32,512]{3,2,1,0:T(8,128)(2,1)S(1)}, bf16[8,2,32,512]{3,2,1,0:T(8,128)(2,1)S(1)}, bf16[16,2,32,512]{3,2,1,0:T(8,128)(2,1)S(1)}, bf16[2,256,256]{2,1,0:T(8,128)(2,1)S(1)}) custom-call(s32[2,20]{1,0:T(2,128)S(1)} %get-tuple-element.129.meta, bf16[512,512]{1,0:T(8,128)(2,1)S(1)} %copy-done.7, ...), custom_call_target="tpu_custom_call" | custom-call | bytes 8279999 | tf_op jit(solution)/shard_map/first_slice/pallas_call | solution.py:464
  100.2 4.7 %collective-permute-done.31 = bf16[8,2,32,512]{3,2,1,0:T(8,128)(2,1)} collective-permute-done((bf16[8,2,32,512]{3,2,1,0:T(8,128)(2,1)}, bf16[8,2,32,512]{3,2,1,0:T(8,128)(2,1)}, u32[]{:S(2)}, u32[]{:S(2)}) %collective-permute-start.31) | collective-permute-done | bytes 524320 | tf_op jit(solution)/shard_map/ppermute | solution.py:592
  106.4 3.0 %collective-permute-done.23 = bf16[8,2,32,512]{3,2,1,0:T(8,128)(2,1)} collective-permute-done((bf16[8,2,32,512]{3,2,1,0:T(8,128)(2,1)}, bf16[8,2,32,512]{3,2,1,0:T(8,128)(2,1)}, u32[]{:S(2)}, u32[]{:S(2)}) %collective-permute-start.23) | collective-permute-done | bytes 524320 | tf_op jit(solution)/shard_map/ppermute | solution.py:592
  115.9 5.3 %collective-permute-done.39 = bf16[4,2,32,512]{3,2,1,0:T(8,128)(2,1)S(1)} collective-permute-done((bf16[4,2,32,512]{3,2,1,0:T(8,128)(2,1)S(1)}, bf16[4,2,32,512]{3,2,1,0:T(8,128)(2,1)S(1)}, u32[]{:S(2)}, u32[]{:S(2)}) %collective-permute-start.39) | collective-permute-done | bytes 262176 | tf_op jit(solution)/shard_map/ppermute | solution.py:592
  121.2 6.7 %collective-permute-done.24 = bf16[8,2,32,512]{3,2,1,0:T(8,128)(2,1)S(1)} collective-permute-done((bf16[8,2,32,512]{3,2,1,0:T(8,128)(2,1)S(1)}, bf16[8,2,32,512]{3,2,1,0:T(8,128)(2,1)S(1)}, u32[]{:S(2)}, u32[]{:S(2)}) %collective-permute-start.24) | collective-permute-done | bytes 524320 | tf_op jit(solution)/shard_map/ppermute | solution.py:592
  128.0 2.6 %collective-permute-done.32 = bf16[4,2,32,512]{3,2,1,0:T(8,128)(2,1)S(1)} collective-permute-done((bf16[4,2,32,512]{3,2,1,0:T(8,128)(2,1)S(1)}, bf16[4,2,32,512]{3,2,1,0:T(8,128)(2,1)S(1)}, u32[]{:S(2)}, u32[]{:S(2)}) %collective-permute-start.32) | collective-permute-done | bytes 262176 | tf_op jit(solution)/shard_map/ppermute | solution.py:592
  132.9 2.4 %collective-permute-done.29 = bf16[128,256]{1,0:T(8,128)(2,1)S(1)} collective-permute-done((bf16[128,256]{1,0:T(8,128)(2,1)S(1)}, bf16[128,256]{1,0:T(8,128)(2,1)S(1)}, u32[]{:S(2)}, u32[]{:S(2)}) %collective-permute-start.29) | collective-permute-done | bytes 65568 | tf_op jit(solution)/shard_map/ppermute | solution.py:592
  139.5 2.4 %collective-permute-done.30 = bf16[128,256]{1,0:T(8,128)(2,1)S(1)} collective-permute-done((bf16[128,256]{1,0:T(8,128)(2,1)S(1)}, bf16[128,256]{1,0:T(8,128)(2,1)S(1)}, u32[]{:S(2)}, u32[]{:S(2)}) %collective-permute-start.30) | collective-permute-done | bytes 65568 | tf_op jit(solution)/shard_map/ppermute | solution.py:592
  142.1 3.0 %collective-permute-start.40 = (bf16[2,2,32,512]{3,2,1,0:T(8,128)(2,1)S(1)}, bf16[2,2,32,512]{3,2,1,0:T(8,128)(2,1)S(1)}, u32[]{:S(2)}, u32[]{:S(2)}) collective-permute-start(bf16[2,2,32,512]{3,2,1,0:T(8,128)(2,1)S(1)} %get-tuple-element.120), channel_id=1, source_target_pairs={{0,8},{1,9},{2,10},{3,11},{4,12},{5,13},{6,14},{7,15},{8,0},{9,1},... | collective-permute-start | bytes 393224 | tf_op jit(solution)/shard_map/ppermute | solution.py:592
  145.0 2.8 %collective-permute-done.34 = bf16[128,256]{1,0:T(8,128)(2,1)S(1)} collective-permute-done((bf16[128,256]{1,0:T(8,128)(2,1)S(1)}, bf16[128,256]{1,0:T(8,128)(2,1)S(1)}, u32[]{:S(2)}, u32[]{:S(2)}) %collective-permute-start.34) | collective-permute-done | bytes 65568 | tf_op jit(solution)/shard_map/ppermute | solution.py:592
  147.9 2.9 %collective-permute-done.25 = bf16[8,2,32,512]{3,2,1,0:T(8,128)(2,1)S(1)} collective-permute-done((bf16[8,2,32,512]{3,2,1,0:T(8,128)(2,1)S(1)}, bf16[8,2,32,512]{3,2,1,0:T(8,128)(2,1)S(1)}, u32[]{:S(2)}, u32[]{:S(2)}) %collective-permute-start.25) | collective-permute-done | bytes 524320 | tf_op jit(solution)/shard_map/ppermute | solution.py:592
  151.7 2.5 %collective-permute-start.38 = (bf16[2,2,32,512]{3,2,1,0:T(8,128)(2,1)S(1)}, bf16[2,2,32,512]{3,2,1,0:T(8,128)(2,1)S(1)}, u32[]{:S(2)}, u32[]{:S(2)}) collective-permute-start(bf16[2,2,32,512]{3,2,1,0:T(8,128)(2,1)S(1)} %get-tuple-element.122), channel_id=1, source_target_pairs={{0,8},{1,9},{2,10},{3,11},{4,12},{5,13},{6,14},{7,15},{8,0},{9,1},... | collective-permute-start | bytes 393224 | tf_op jit(solution)/shard_map/ppermute | solution.py:592
  155.9 3.5 %collective-permute-done.26 = bf16[4,2,32,512]{3,2,1,0:T(8,128)(2,1)S(1)} collective-permute-done((bf16[4,2,32,512]{3,2,1,0:T(8,128)(2,1)S(1)}, bf16[4,2,32,512]{3,2,1,0:T(8,128)(2,1)S(1)}, u32[]{:S(2)}, u32[]{:S(2)}) %collective-permute-start.26) | collective-permute-done | bytes 262176 | tf_op jit(solution)/shard_map/ppermute | solution.py:592
  161.7 6.7 %collective-permute-done.27.refs_1_ = bf16[2,2,32,512]{3,2,1,0:T(8,128)(2,1)S(1)} collective-permute-done((bf16[2,2,32,512]{3,2,1,0:T(8,128)(2,1)S(1)}, bf16[2,2,32,512]{3,2,1,0:T(8,128)(2,1)S(1)}, u32[]{:S(2)}, u32[]{:S(2)}) %collective-permute-start.27) | collective-permute-done | bytes 131104 | tf_op jit(solution)/shard_map/ppermute | solution.py:592
  168.5 2.2 %to_blocks.1 = f32[256,1024]{1,0:T(8,128)} custom-call(bf16[2,2,32,512]{3,2,1,0:T(8,128)(2,1)S(1)} %get-tuple-element.125.refs_0_, bf16[2,2,32,512]{3,2,1,0:T(8,128)(2,1)S(1)} %collective-permute-done.27.refs_1_, bf16[2,2,32,512]{3,2,1,0:T(8,128)(2,1)S(1)} %get-tuple-element.123.refs_2_, bf16[2,2,32,512]{3,2,1,0:T(8,128)(2,1)S(1)} %collective-permute-done.38.refs_3_, ...), custom_call_target="tpu_custom_call" | custom-call | bytes 5400000 | tf_op jit(solution)/shard_map/to_blocks/pallas_call | solution.py:564
  (151 shorter events, 47.3 us)
Async XLA Ops:
  2.7 15.9 %collective-permute-start.7 = (bf16[2,2,32,512]{3,2,1,0:T(8,128)(2,1)S(1)}, bf16[2,2,32,512]{3,2,1,0:T(8,128)(2,1)S(1)}, u32[]{:S(2)}, u32[]{:S(2)}) collective-permute-start(bf16[2,2,32,512]{3,2,1,0:T(8,128)(2,1)S(1)} %get-tuple-element.62), channel_id=1, source_target_pairs={{0,2},{1,3},{2,0},{3,1},{4,6},{5,7},{6,4},{7,5},{8,10},{9,11},{10,... | collective-permute-start | bytes 393224 | tf_op jit(solution)/shard_map/ppermute | solution.py:592
  5.8 10.0 %collective-permute-start.1 = (bf16[2,2,32,512]{3,2,1,0:T(8,128)(2,1)S(1)}, bf16[2,2,32,512]{3,2,1,0:T(8,128)(2,1)S(1)}, u32[]{:S(2)}, u32[]{:S(2)}) collective-permute-start(bf16[2,2,32,512]{3,2,1,0:T(8,128)(2,1)S(1)} %get-tuple-element.62), channel_id=1, source_target_pairs={{0,8},{1,9},{2,10},{3,11},{4,12},{5,13},{6,14},{7,15},{8,0},{9,1},... | collective-permute-start | bytes 393224 | tf_op jit(solution)/shard_map/ppermute | solution.py:592
  8.4 10.2 %collective-permute-start = (bf16[2,2,32,512]{3,2,1,0:T(8,128)(2,1)S(1)}, bf16[2,2,32,512]{3,2,1,0:T(8,128)(2,1)S(1)}, u32[]{:S(2)}, u32[]{:S(2)}) collective-permute-start(bf16[2,2,32,512]{3,2,1,0:T(8,128)(2,1)S(1)} %get-tuple-element.60), channel_id=1, source_target_pairs={{0,2},{1,3},{2,0},{3,1},{4,6},{5,7},{6,4},{7,5},{8,10},{9,11},{10,... | collective-permute-start | bytes 393224 | tf_op jit(solution)/shard_map/ppermute | solution.py:592
  15.8 9.2 %collective-permute-start.2 = (bf16[2,2,32,512]{3,2,1,0:T(8,128)(2,1)S(1)}, bf16[2,2,32,512]{3,2,1,0:T(8,128)(2,1)S(1)}, u32[]{:S(2)}, u32[]{:S(2)}) collective-permute-start(bf16[2,2,32,512]{3,2,1,0:T(8,128)(2,1)S(1)} %get-tuple-element.63), channel_id=1, source_target_pairs={{0,8},{1,9},{2,10},{3,11},{4,12},{5,13},{6,14},{7,15},{8,0},{9,1},... | collective-permute-start | bytes 393224 | tf_op jit(solution)/shard_map/ppermute | solution.py:592
  15.9 13.7 %collective-permute-start.5 = (bf16[4,2,32,512]{3,2,1,0:T(8,128)(2,1)S(1)}, bf16[4,2,32,512]{3,2,1,0:T(8,128)(2,1)S(1)}, u32[]{:S(2)}, u32[]{:S(2)}) collective-permute-start(bf16[4,2,32,512]{3,2,1,0:T(8,128)(2,1)S(1)} %pad_maximum_fusion.5), channel_id=1, source_target_pairs={{0,4},{1,5},{2,6},{3,7},{4,0},{5,1},{6,2},{7,3},{8,12},{9,13},{10,... | collective-permute-start | bytes 786440 | tf_op jit(solution)/shard_map/ppermute | solution.py:592
  18.6 18.7 %collective-permute-start.4 = (bf16[2,2,32,512]{3,2,1,0:T(8,128)(2,1)S(1)}, bf16[2,2,32,512]{3,2,1,0:T(8,128)(2,1)S(1)}, u32[]{:S(2)}, u32[]{:S(2)}) collective-permute-start(bf16[2,2,32,512]{3,2,1,0:T(8,128)(2,1)S(1)} %get-tuple-element.66), channel_id=1, source_target_pairs={{0,8},{1,9},{2,10},{3,11},{4,12},{5,13},{6,14},{7,15},{8,0},{9,1},... | collective-permute-start | bytes 393224 | tf_op jit(solution)/shard_map/ppermute | solution.py:592
  29.6 7.7 %collective-permute-start.6 = (bf16[4,2,32,512]{3,2,1,0:T(8,128)(2,1)S(1)}, bf16[4,2,32,512]{3,2,1,0:T(8,128)(2,1)S(1)}, u32[]{:S(2)}, u32[]{:S(2)}) collective-permute-start(bf16[4,2,32,512]{3,2,1,0:T(8,128)(2,1)S(1)} %pad_maximum_fusion.4), channel_id=1, source_target_pairs={{0,4},{1,5},{2,6},{3,7},{4,0},{5,1},{6,2},{7,3},{8,12},{9,13},{10,... | collective-permute-start | bytes 786440 | tf_op jit(solution)/shard_map/ppermute | solution.py:592
  29.6 7.7 %collective-permute-start.9 = (bf16[4,2,32,512]{3,2,1,0:T(8,128)(2,1)S(1)}, bf16[4,2,32,512]{3,2,1,0:T(8,128)(2,1)S(1)}, u32[]{:S(2)}, u32[]{:S(2)}) collective-permute-start(bf16[4,2,32,512]{3,2,1,0:T(8,128)(2,1)S(1)} %collective-permute-done.5), channel_id=1, source_target_pairs={{0,2},{1,3},{2,0},{3,1},{4,6},{5,7},{6,4},{7,5},{8,10},{9,11},{10,... | collective-permute-start | bytes 786440 | tf_op jit(solution)/shard_map/ppermute | solution.py:592
  37.5 14.4 %collective-permute-start.13 = (bf16[8,2,32,512]{3,2,1,0:T(8,128)(2,1)S(1)}, bf16[8,2,32,512]{3,2,1,0:T(8,128)(2,1)S(1)}, u32[]{:S(2)}, u32[]{:S(2)}) collective-permute-start(bf16[8,2,32,512]{3,2,1,0:T(8,128)(2,1)S(1)} %pad_maximum_fusion), channel_id=1, source_target_pairs={{0,2},{1,3},{2,0},{3,1},{4,6},{5,7},{6,4},{7,5},{8,10},{9,11},{10,... | collective-permute-start | bytes 1572872 | tf_op jit(solution)/shard_map/ppermute | solution.py:592
  38.9 15.2 %collective-permute-start.3 = (bf16[4,2,32,512]{3,2,1,0:T(8,128)(2,1)S(1)}, bf16[4,2,32,512]{3,2,1,0:T(8,128)(2,1)S(1)}, u32[]{:S(2)}, u32[]{:S(2)}) collective-permute-start(bf16[4,2,32,512]{3,2,1,0:T(8,128)(2,1)S(1)} %pad_maximum_fusion.2), channel_id=1, source_target_pairs={{0,8},{1,9},{2,10},{3,11},{4,12},{5,13},{6,14},{7,15},{8,0},{9,1},... | collective-permute-start | bytes 786440 | tf_op jit(solution)/shard_map/ppermute | solution.py:592
  45.3 12.7 %collective-permute-start.11 = (bf16[4,2,32,512]{3,2,1,0:T(8,128)(2,1)S(1)}, bf16[4,2,32,512]{3,2,1,0:T(8,128)(2,1)S(1)}, u32[]{:S(2)}, u32[]{:S(2)}) collective-permute-start(bf16[4,2,32,512]{3,2,1,0:T(8,128)(2,1)S(1)} %pad_maximum_fusion.3), channel_id=1, source_target_pairs={{0,4},{1,5},{2,6},{3,7},{4,0},{5,1},{6,2},{7,3},{8,12},{9,13},{10,... | collective-permute-start | bytes 786440 | tf_op jit(solution)/shard_map/ppermute | solution.py:592
  58.0 14.4 %collective-permute-start.17 = (bf16[8,2,32,512]{3,2,1,0:T(8,128)(2,1)S(1)}, bf16[8,2,32,512]{3,2,1,0:T(8,128)(2,1)S(1)}, u32[]{:S(2)}, u32[]{:S(2)}) collective-permute-start(bf16[8,2,32,512]{3,2,1,0:T(8,128)(2,1)S(1)} %pad_maximum_fusion.1), channel_id=1, source_target_pairs={{0,2},{1,3},{2,0},{3,1},{4,6},{5,7},{6,4},{7,5},{8,10},{9,11},{10,... | collective-permute-start | bytes 1572872 | tf_op jit(solution)/shard_map/ppermute | solution.py:592
  58.3 14.2 %collective-permute-start.12 = (bf16[8,2,32,512]{3,2,1,0:T(8,128)(2,1)S(1)}, bf16[8,2,32,512]{3,2,1,0:T(8,128)(2,1)S(1)}, u32[]{:S(2)}, u32[]{:S(2)}) collective-permute-start(bf16[8,2,32,512]{3,2,1,0:T(8,128)(2,1)S(1)} %constant_dynamic-update-slice_fusion.refs_0_), channel_id=1, source_target_pairs={{0,4},{1,5},{2,6},{3,7},{4,0},{5,1},{6,2},{7,3},{8,12},{9,13},{10,... | collective-permute-start | bytes 1572872 | tf_op jit(solution)/shard_map/ppermute | solution.py:592
  64.2 8.4 %collective-permute-start.15 = (bf16[8,2,32,512]{3,2,1,0:T(8,128)(2,1)S(1)}, bf16[8,2,32,512]{3,2,1,0:T(8,128)(2,1)S(1)}, u32[]{:S(2)}, u32[]{:S(2)}) collective-permute-start(bf16[8,2,32,512]{3,2,1,0:T(8,128)(2,1)S(1)} %constant_dynamic-update-slice_fusion.refs_0_), channel_id=1, source_target_pairs={{0,1},{1,0},{2,3},{3,2},{4,5},{5,4},{6,7},{7,6},{8,9},{9,8},{10,11... | collective-permute-start | bytes 1572872 | tf_op jit(solution)/shard_map/ppermute | solution.py:592
  72.6 6.2 %collective-permute-start.16 = (bf16[8,2,32,512]{3,2,1,0:T(8,128)(2,1)S(1)}, bf16[8,2,32,512]{3,2,1,0:T(8,128)(2,1)S(1)}, u32[]{:S(2)}, u32[]{:S(2)}) collective-permute-start(bf16[8,2,32,512]{3,2,1,0:T(8,128)(2,1)S(1)} %collective-permute-done.12.refs_1_), channel_id=1, source_target_pairs={{0,1},{1,0},{2,3},{3,2},{4,5},{5,4},{6,7},{7,6},{8,9},{9,8},{10,11... | collective-permute-start | bytes 1572872 | tf_op jit(solution)/shard_map/ppermute | solution.py:592
  90.7 14.3 %collective-permute-start.31 = (bf16[8,2,32,512]{3,2,1,0:T(8,128)(2,1)}, bf16[8,2,32,512]{3,2,1,0:T(8,128)(2,1)}, u32[]{:S(2)}, u32[]{:S(2)}) collective-permute-start(bf16[8,2,32,512]{3,2,1,0:T(8,128)(2,1)} %add_convert_fusion.3), channel_id=1, source_target_pairs={{0,4},{1,5},{2,6},{3,7},{4,0},{5,1},{6,2},{7,3},{8,12},{9,13},{10,... | collective-permute-start | bytes 1572872 | tf_op jit(solution)/shard_map/ppermute | solution.py:592
  93.5 19.1 %collective-permute-start.22 = (bf16[16,2,32,512]{3,2,1,0:T(8,128)(2,1)}, bf16[16,2,32,512]{3,2,1,0:T(8,128)(2,1)}, u32[]{:S(2)}, u32[]{:S(2)}) collective-permute-start(bf16[16,2,32,512]{3,2,1,0:T(8,128)(2,1)} %get-tuple-element.98), channel_id=1, source_target_pairs={{0,1},{1,0},{2,3},{3,2},{4,5},{5,4},{6,7},{7,6},{8,9},{9,8},{10,11... | collective-permute-start | bytes 3145736 | tf_op jit(solution)/shard_map/ppermute | solution.py:592
  94.8 14.6 %collective-permute-start.23 = (bf16[8,2,32,512]{3,2,1,0:T(8,128)(2,1)}, bf16[8,2,32,512]{3,2,1,0:T(8,128)(2,1)}, u32[]{:S(2)}, u32[]{:S(2)}) collective-permute-start(bf16[8,2,32,512]{3,2,1,0:T(8,128)(2,1)} %add_convert_fusion.7), channel_id=1, source_target_pairs={{0,2},{1,3},{2,0},{3,1},{4,6},{5,7},{6,4},{7,5},{8,10},{9,11},{10,... | collective-permute-start | bytes 1572872 | tf_op jit(solution)/shard_map/ppermute | solution.py:592
  100.0 15.6 %collective-permute-start.21 = (bf16[16,2,32,512]{3,2,1,0:T(8,128)(2,1)S(1)}, bf16[16,2,32,512]{3,2,1,0:T(8,128)(2,1)S(1)}, u32[]{:S(2)}, u32[]{:S(2)}) collective-permute-start(bf16[16,2,32,512]{3,2,1,0:T(8,128)(2,1)S(1)} %get-tuple-element.95), channel_id=1, source_target_pairs={{0,1},{1,0},{2,3},{3,2},{4,5},{5,4},{6,7},{7,6},{8,9},{9,8},{10,11... | collective-permute-start | bytes 3145736 | tf_op jit(solution)/shard_map/ppermute | solution.py:592
  109.4 6.2 %collective-permute-start.28 = (bf16[256,256]{1,0:T(8,128)(2,1)S(1)}, bf16[256,256]{1,0:T(8,128)(2,1)S(1)}, u32[]{:S(2)}, u32[]{:S(2)}) collective-permute-start(bf16[256,256]{1,0:T(8,128)(2,1)S(1)} %select_bitcast_fusion), channel_id=1, source_target_pairs={{0,1},{1,0},{2,3},{3,2},{4,5},{5,4},{6,7},{7,6},{8,9},{9,8},{10,11... | collective-permute-start | bytes 393224 | tf_op jit(solution)/shard_map/ppermute | solution.py:592
  110.8 10.4 %collective-permute-start.39 = (bf16[4,2,32,512]{3,2,1,0:T(8,128)(2,1)S(1)}, bf16[4,2,32,512]{3,2,1,0:T(8,128)(2,1)S(1)}, u32[]{:S(2)}, u32[]{:S(2)}) collective-permute-start(bf16[4,2,32,512]{3,2,1,0:T(8,128)(2,1)S(1)} %slice.162), channel_id=1, source_target_pairs={{0,4},{1,5},{2,6},{3,7},{4,0},{5,1},{6,2},{7,3},{8,12},{9,13},{10,... | collective-permute-start | bytes 786440 | tf_op jit(solution)/shard_map/ppermute | solution.py:592
  113.8 14.1 %collective-permute-start.24 = (bf16[8,2,32,512]{3,2,1,0:T(8,128)(2,1)S(1)}, bf16[8,2,32,512]{3,2,1,0:T(8,128)(2,1)S(1)}, u32[]{:S(2)}, u32[]{:S(2)}) collective-permute-start(bf16[8,2,32,512]{3,2,1,0:T(8,128)(2,1)S(1)} %add_convert_fusion.5), channel_id=1, source_target_pairs={{0,2},{1,3},{2,0},{3,1},{4,6},{5,7},{6,4},{7,5},{8,10},{9,11},{10,... | collective-permute-start | bytes 1572872 | tf_op jit(solution)/shard_map/ppermute | solution.py:592
  115.8 14.8 %collective-permute-start.32 = (bf16[4,2,32,512]{3,2,1,0:T(8,128)(2,1)S(1)}, bf16[4,2,32,512]{3,2,1,0:T(8,128)(2,1)S(1)}, u32[]{:S(2)}, u32[]{:S(2)}) collective-permute-start(bf16[4,2,32,512]{3,2,1,0:T(8,128)(2,1)S(1)} %slice.153), channel_id=1, source_target_pairs={{0,8},{1,9},{2,10},{3,11},{4,12},{5,13},{6,14},{7,15},{8,0},{9,1},... | collective-permute-start | bytes 786440 | tf_op jit(solution)/shard_map/ppermute | solution.py:592
  131.1 10.8 %collective-permute-start.33 = (bf16[2,2,32,512]{3,2,1,0:T(8,128)(2,1)S(1)}, bf16[2,2,32,512]{3,2,1,0:T(8,128)(2,1)S(1)}, u32[]{:S(2)}, u32[]{:S(2)}) collective-permute-start(bf16[2,2,32,512]{3,2,1,0:T(8,128)(2,1)S(1)} %get-tuple-element.119), channel_id=1, source_target_pairs={{0,2},{1,3},{2,0},{3,1},{4,6},{5,7},{6,4},{7,5},{8,10},{9,11},{10,... | collective-permute-start | bytes 393224 | tf_op jit(solution)/shard_map/ppermute | solution.py:592
  135.3 6.6 %collective-permute-start.30 = (bf16[128,256]{1,0:T(8,128)(2,1)S(1)}, bf16[128,256]{1,0:T(8,128)(2,1)S(1)}, u32[]{:S(2)}, u32[]{:S(2)}) collective-permute-start(bf16[128,256]{1,0:T(8,128)(2,1)S(1)} %add_convert_fusion.13), channel_id=1, source_target_pairs={{0,4},{1,5},{2,6},{3,7},{4,0},{5,1},{6,2},{7,3},{8,12},{9,13},{10,... | collective-permute-start | bytes 196616 | tf_op jit(solution)/shard_map/ppermute | solution.py:592
  136.7 11.2 %collective-permute-start.37 = (bf16[4,2,32,512]{3,2,1,0:T(8,128)(2,1)S(1)}, bf16[4,2,32,512]{3,2,1,0:T(8,128)(2,1)S(1)}, u32[]{:S(2)}, u32[]{:S(2)}) collective-permute-start(bf16[4,2,32,512]{3,2,1,0:T(8,128)(2,1)S(1)} %slice.157), channel_id=1, source_target_pairs={{0,4},{1,5},{2,6},{3,7},{4,0},{5,1},{6,2},{7,3},{8,12},{9,13},{10,... | collective-permute-start | bytes 786440 | tf_op jit(solution)/shard_map/ppermute | solution.py:592
  138.8 12.0 %collective-permute-start.25 = (bf16[8,2,32,512]{3,2,1,0:T(8,128)(2,1)S(1)}, bf16[8,2,32,512]{3,2,1,0:T(8,128)(2,1)S(1)}, u32[]{:S(2)}, u32[]{:S(2)}) collective-permute-start(bf16[8,2,32,512]{3,2,1,0:T(8,128)(2,1)S(1)} %add_convert_fusion.6), channel_id=1, source_target_pairs={{0,2},{1,3},{2,0},{3,1},{4,6},{5,7},{6,4},{7,5},{8,10},{9,11},{10,... | collective-permute-start | bytes 1572872 | tf_op jit(solution)/shard_map/ppermute | solution.py:592
  142.0 5.9 %collective-permute-start.34 = (bf16[128,256]{1,0:T(8,128)(2,1)S(1)}, bf16[128,256]{1,0:T(8,128)(2,1)S(1)}, u32[]{:S(2)}, u32[]{:S(2)}) collective-permute-start(bf16[128,256]{1,0:T(8,128)(2,1)S(1)} %add_convert_fusion.12), channel_id=1, source_target_pairs={{0,8},{1,9},{2,10},{3,11},{4,12},{5,13},{6,14},{7,15},{8,0},{9,1},... | collective-permute-start | bytes 196616 | tf_op jit(solution)/shard_map/ppermute | solution.py:592
  142.1 26.4 %collective-permute-start.40 = (bf16[2,2,32,512]{3,2,1,0:T(8,128)(2,1)S(1)}, bf16[2,2,32,512]{3,2,1,0:T(8,128)(2,1)S(1)}, u32[]{:S(2)}, u32[]{:S(2)}) collective-permute-start(bf16[2,2,32,512]{3,2,1,0:T(8,128)(2,1)S(1)} %get-tuple-element.120), channel_id=1, source_target_pairs={{0,8},{1,9},{2,10},{3,11},{4,12},{5,13},{6,14},{7,15},{8,0},{9,1},... | collective-permute-start | bytes 393224 | tf_op jit(solution)/shard_map/ppermute | solution.py:592
  151.5 7.8 %collective-permute-start.26 = (bf16[4,2,32,512]{3,2,1,0:T(8,128)(2,1)S(1)}, bf16[4,2,32,512]{3,2,1,0:T(8,128)(2,1)S(1)}, u32[]{:S(2)}, u32[]{:S(2)}) collective-permute-start(bf16[4,2,32,512]{3,2,1,0:T(8,128)(2,1)S(1)} %slice.145), channel_id=1, source_target_pairs={{0,4},{1,5},{2,6},{3,7},{4,0},{5,1},{6,2},{7,3},{8,12},{9,13},{10,... | collective-permute-start | bytes 786440 | tf_op jit(solution)/shard_map/ppermute | solution.py:592
  151.7 16.8 %collective-permute-start.38 = (bf16[2,2,32,512]{3,2,1,0:T(8,128)(2,1)S(1)}, bf16[2,2,32,512]{3,2,1,0:T(8,128)(2,1)S(1)}, u32[]{:S(2)}, u32[]{:S(2)}) collective-permute-start(bf16[2,2,32,512]{3,2,1,0:T(8,128)(2,1)S(1)} %get-tuple-element.122), channel_id=1, source_target_pairs={{0,8},{1,9},{2,10},{3,11},{4,12},{5,13},{6,14},{7,15},{8,0},{9,1},... | collective-permute-start | bytes 393224 | tf_op jit(solution)/shard_map/ppermute | solution.py:592
  159.5 9.0 %collective-permute-start.27 = (bf16[2,2,32,512]{3,2,1,0:T(8,128)(2,1)S(1)}, bf16[2,2,32,512]{3,2,1,0:T(8,128)(2,1)S(1)}, u32[]{:S(2)}, u32[]{:S(2)}) collective-permute-start(bf16[2,2,32,512]{3,2,1,0:T(8,128)(2,1)S(1)} %get-tuple-element.124), channel_id=1, source_target_pairs={{0,8},{1,9},{2,10},{3,11},{4,12},{5,13},{6,14},{7,15},{8,0},{9,1},... | collective-permute-start | bytes 393224 | tf_op jit(solution)/shard_map/ppermute | solution.py:592
  (26 other events, 95.5 us)

commit v2 on v1

--- a/solution.py
+++ b/solution.py
@@ -17,7 +17,8 @@
 FLOOR = 0.25
 WIN = 9
 TALL = FOOT * BSIDE
-VMEM_BYTES = 20 * 1024 * 1024
+VMEM_BYTES = 16 * 1024 * 1024
+SCALE = 3.6e6
 F32 = jnp.float32
 BF16 = jnp.bfloat16
 
@@ -87,24 +88,26 @@
     return pl.ds(c * PATCH, PATCH)
 
 
+def strip_copy(source, place, window, sems, p, k):
+    return pltpu.make_async_copy(source.at[place], window.at[p, k], sems.at[p, k])
+
+
 def fetch(meta, sources, window, sems, patches):
     per = sources[0].shape[0]
-
-    def copy(source, place, p, k):
-        return pltpu.make_async_copy(source.at[place], window.at[p, k], sems.at[p, k])
-
     for p in range(patches):
         for k in range(WIN):
             place = meta[p, 2 + k]
-            for n, source in enumerate(sources):
-
-                @pl.when(place // per == n)
-                def _(source=source, place=place, n=n, p=p, k=k):
-                    copy(source, place - n * per, p, k).start()
-
+            for m, source in enumerate(sources):
+
+                @pl.when(place // per == m)
+                def _(source=source, place=place - m * per, p=p, k=k):
+                    strip_copy(source, place, window, sems, p, k).start()
+
+
+def await_fetch(sources, window, sems, patches):
     for p in range(patches):
         for k in range(WIN):
-            copy(sources[0], 0, p, k).wait()
+            strip_copy(sources[0], 0, window, sems, p, k).wait()
 
 
 def patch_rows(meta, window, p, k):
@@ -198,43 +201,34 @@
 
 
 def cost(microseconds):
-    return pl.CostEstimate(flops=0, bytes_accessed=int(microseconds * 3.6e6), transcendentals=0)
-
-
-def wrap_probe(meta, probe, patches):
-    def kernel(meta, probe, out):
-        for p in range(patches):
-            my, mx = shifts(meta, p, F32)
-            for c in range(2):
-                half = lax.dot_general(
-                    mx,
-                    probe[c],
-                    (((1,), (1,)), ((), ())),
-                    precision=lax.Precision.HIGHEST,
-                    preferred_element_type=F32,
-                )
-                out[p, c] = jnp.dot(
-                    half, my, precision=lax.Precision.HIGHEST, preferred_element_type=F32
-                )
-
-    return pl.pallas_call(
-        kernel,
-        out_shape=jax.ShapeDtypeStruct((patches, 2, PATCH, PATCH), F32),
-        in_specs=[smem_spec(), vmem_spec()],
-        out_specs=vmem_spec(),
-        compiler_params=params(),
-        cost_estimate=cost(3.3),
-        name="wrap_probe",
-    )(meta, probe)
+    return pl.CostEstimate(flops=0, bytes_accessed=int(microseconds * SCALE), transcendentals=0)
+
+
+def wrap_exact(value, mx, my):
+    high = value.astype(BF16)
+    rest = value - high.astype(F32)
+    middle = rest.astype(BF16)
+    low = (rest - middle.astype(F32)).astype(BF16)
+    high, middle, low = (dot(dot_nt(mx, part).astype(BF16), my) for part in (high, middle, low))
+    return high + (middle + low)
 
 
 def forward(layer, meta, sources, before, right, left, patches):
     wide = patches * PATCH
 
+    n = len(sources)
+
     def kernel(meta, *refs):
-        sources, refs = refs[: -9], refs[-9:]
-        before, right, left, trans, after, window, field, half, sems = refs
-        fetch(meta, sources, window, sems, patches)
+        sources, (before, right, left, trans, after), refs = refs[:n], refs[n : n + 5], refs[n + 5 :]
+        fetch(meta, sources, window := refs[-4], sems := refs[-1], patches)
+        field, half = refs[-3:-1]
+        if layer == 0:
+            probe, before = before, refs[0]
+            for p in range(patches):
+                my, mx = shifts(meta, p)
+                for c in range(2):
+                    before[p, c] = wrap_exact(probe[c], mx, my)
+        await_fetch(sources, window, sems, patches)
         for p in range(patches):
             for k in range(PATCH // BSIDE):
                 tr, ti = patch_rows(meta, window, p, k)
@@ -255,11 +249,12 @@
         propagate(field, half, right, left, patches, put)
 
     plane = jax.ShapeDtypeStruct((2 * PATCH, wide), BF16)
+    extra = [jax.ShapeDtypeStruct((patches, 2, PATCH, PATCH), F32)] if layer == 0 else []
     return pl.pallas_call(
         kernel,
-        out_shape=(plane, plane),
-        in_specs=[smem_spec()] + [any_spec()] * len(sources) + [vmem_spec()] * 3,
-        out_specs=(vmem_spec(), vmem_spec()),
+        out_shape=[plane, plane, *extra],
+        in_specs=[smem_spec()] + [any_spec()] * n + [vmem_spec()] * 3,
+        out_specs=[vmem_spec()] * (2 + len(extra)),
         scratch_shapes=[
             pltpu.VMEM((patches, WIN, 2, BSIDE, TALL), BF16),
             pltpu.VMEM((wide, 2 * PATCH), BF16),
@@ -294,96 +289,142 @@
     return put
 
 
-def far_field(meta, sources, before, amplitudes, tabs, pieces, patches):
+def through_slice(meta, window, load, trans, field, patches):
+    for p in range(patches):
+        for k in range(PATCH // BSIDE):
+            tr, ti = patch_rows(meta, window, p, k)
+            trans[at_rows(0, k), cols(p)] = tr.astype(BF16)
+            trans[at_rows(1, k), cols(p)] = ti.astype(BF16)
+            tr = tr + 1.0
+            fr, fi = load(p, 0, k), load(p, 1, k)
+            field[at_rows(p, k), cols(0)] = (tr * fr - ti * fi).astype(BF16)
+            field[at_rows(p, k), cols(1)] = (tr * fi + ti * fr).astype(BF16)
+
+
+def loader(ref):
+    return lambda p, c, k: ref[at_rows(c, k), cols(p)].astype(F32)
+
+
+def put_plain(out):
+    def put(c, value):
+        out[cols(c), :] = value.astype(BF16)
+
+    return put
+
+
+def dft_pair(half, other, left, right, patches, use):
+    for c in range(2):
+        y = dot(left[cols(c), :], half[...])
+        for p in range(patches):
+            other[cols(p), cols(c)] = y[:, p * PATCH : (p + 1) * PATCH].astype(BF16)
+    for p in range(patches):
+        use(p, dot(other[cols(p), :], right[...]))
+
+
+def turn(metas, groups, carried, amplitudes, tabs, pieces, patches):
     wide = patches * PATCH
     n_out = len(pieces)
-
-    def kernel(meta, *refs):
-        n_in = len(sources)
-        sources_, refs = refs[:n_in], refs[n_in:]
-        before, measured, hr, hl, fl, fr = refs[:6]
-        outs, refs = refs[6 : 6 + n_out], refs[6 + n_out :]
-        after, window, field, half, other, trans, grid, sems, out_sems = refs
-        fetch(meta, sources_, window, sems, patches)
-        clear(grid)
-        for p in range(patches):
-            for k in range(PATCH // BSIDE):
-                tr, ti = patch_rows(meta, window, p, k)
-                trans[at_rows(0, k), cols(p)] = tr.astype(BF16)
-                trans[at_rows(1, k), cols(p)] = ti.astype(BF16)
-                tr = tr + 1.0
-                qr = before[at_rows(0, k), cols(p)].astype(F32)
-                qi = before[at_rows(1, k), cols(p)].astype(F32)
-                field[at_rows(p, k), cols(0)] = (tr * qr - ti * qi).astype(BF16)
-                field[at_rows(p, k), cols(1)] = (tr * qi + ti * qr).astype(BF16)
-        for p in range(patches):
-            my, mx = shifts(meta, p)
+    n2, n3 = len(groups[0]), len(groups[1])
+
+    def kernel(meta, meta_last, *refs):
+        given2, given3, refs = refs[:n2], refs[n2 : n2 + n3], refs[n2 + n3 :]
+        q2, measured, hr, hl, fl, fr = refs[:6]
+        outs, refs = refs[6 : 6 + 2 * n_out], refs[6 + 2 * n_out :]
+        after, windows, t2, t3, q3, adjoint, field, half, other, grids, sems, out_sems = refs
+        fetch(meta, given2, windows.at[0], sems.at[0], patches)
+        fetch(meta_last, given3, windows.at[1], sems.at[1], patches)
+        clear(grids.at[0])
+        clear(grids.at[1])
+        await_fetch(given2, windows.at[0], sems.at[0], patches)
+        through_slice(meta, windows.at[0], loader(q2), t2, field, patches)
+        propagate(field, half, hr, hl, patches, put_plain(q3))
+        await_fetch(given3, windows.at[1], sems.at[1], patches)
+        through_slice(meta_last, windows.at[1], loader(q3), t3, field, patches)
+        moves = [shifts(meta, p) for p in range(patches)]
+        for p, (my, mx) in enumerate(moves):
             for c in range(2):
                 turned = dot_nt(my, field[cols(p), cols(c)]).astype(BF16)
                 half[cols(c), cols(p)] = dot(turned, mx).astype(BF16)
-        for c in range(2):
-            y = dot(fl[cols(c), :], half[...])
-            for p in range(patches):
-                other[cols(p), cols(c)] = y[:, p * PATCH : (p + 1) * PATCH].astype(BF16)
-        for p in range(patches):
-            far = dot(other[cols(p), :], fr[...])
+
+        def misfit(p, far):
             real, imag = far[:, :PATCH], far[:, PATCH:]
             modulus = jnp.sqrt(real * real + imag * imag)
             keeping = 1.0 - measured[p] / jnp.maximum(modulus, FLOOR)
             half[cols(0), cols(p)] = (real * keeping).astype(BF16)
             half[cols(1), cols(p)] = (-imag * keeping).astype(BF16)
-        for c in range(2):
-            y = dot(fl[cols(c), :], half[...])
-            for p in range(patches):
-                other[cols(p), cols(c)] = y[:, p * PATCH : (p + 1) * PATCH].astype(BF16)
-        for p in range(patches):
-            g = dot(other[cols(p), :], fr[...])
-            my, mx = shifts(meta, p)
+
+        def wrapped(p, g):
+            my, mx = moves[p]
             for c in range(2):
                 part = g[:, c * PATCH : (c + 1) * PATCH]
                 part = (-part if c else part).astype(BF16)
-                turned = dot_nt(mx, part).astype(BF16)
-                half[cols(c), cols(p)] = dot(turned, my).astype(BF16)
-        for p in range(patches):
-            for k in range(PATCH // BSIDE):
-                load = lambda ref, c: ref[at_rows(c, k), cols(p)].astype(F32)
-                back_step(
-                    meta,
-                    p,
-                    k,
-                    (load(half, 0), load(half, 1)),
-                    (load(before, 0), load(before, 1)),
-                    (load(trans, 0) + 1.0, load(trans, 1)),
-                    grid,
-                    field,
+                adjoint[cols(c), cols(p)] = dot(dot_nt(mx, part).astype(BF16), my).astype(BF16)
+
+        dft_pair(half, other, fl, fr, patches, misfit)
+        dft_pair(half, other, fl, fr, patches, wrapped)
+
+        def copies(layer):
+            found, start = [], 0
+            for n, size in enumerate(pieces):
+                found.append(
+                    pltpu.make_async_copy(
+                        grids.at[layer, pl.ds(start, size)],
+                        outs[layer * n_out + n],
+                        out_sems.at[layer, n],
+                    )
                 )
-        copies = send_out(grid, outs, out_sems)
-        propagate(field, half, hr, hl, patches, put_conjugate(after))
-        for copy in copies:
-            copy.wait()
-
-    plane = jax.ShapeDtypeStruct((2 * PATCH, wide), BF16)
+                start += size
+            return found
+
+        g = loader(adjoint)
+        for layer, spot, q, t, nxt in (
+            (1, meta_last, loader(q3), loader(t3), adjoint),
+            (0, meta, loader(q2), loader(t2), after),
+        ):
+            for p in range(patches):
+                for k in range(PATCH // BSIDE):
+                    back_step(
+                        spot,
+                        p,
+                        k,
+                        (g(p, 0, k), g(p, 1, k)),
+                        (q(p, 0, k), q(p, 1, k)),
+                        (t(p, 0, k) + 1.0, t(p, 1, k)),
+                        grids.at[layer],
+                        field,
+                    )
+            for copy in copies(layer):
+                copy.start()
+            propagate(field, half, hr, hl, patches, put_conjugate(nxt))
+        for layer in range(2):
+            for copy in copies(layer):
+                copy.wait()
+
+    plane = pltpu.VMEM((2 * PATCH, wide), BF16)
     strips = [jax.ShapeDtypeStruct((n, 2, BSIDE, TALL), BF16) for n in pieces]
     *outs, after = pl.pallas_call(
         kernel,
-        out_shape=(*strips, plane),
-        in_specs=[smem_spec()] + [any_spec()] * len(sources) + [vmem_spec()] * 6,
-        out_specs=(*[any_spec()] * n_out, vmem_spec()),
+        out_shape=(*strips * 2, jax.ShapeDtypeStruct((2 * PATCH, wide), BF16)),
+        in_specs=[smem_spec()] * 2 + [any_spec()] * (n2 + n3) + [vmem_spec()] * 6,
+        out_specs=(*[any_spec()] * (2 * n_out), vmem_spec()),
         scratch_shapes=[
-            pltpu.VMEM((patches, WIN, 2, BSIDE, TALL), BF16),
+            pltpu.VMEM((2, patches, WIN, 2, BSIDE, TALL), BF16),
+            plane,
+            plane,
+            plane,
+            plane,
             pltpu.VMEM((wide, 2 * PATCH), BF16),
-            pltpu.VMEM((2 * PATCH, wide), BF16),
+            plane,
             pltpu.VMEM((wide, 2 * PATCH), BF16),
-            pltpu.VMEM((2 * PATCH, wide), BF16),
-            pltpu.VMEM((sum(pieces), 2, BSIDE, TALL), BF16),
-            pltpu.SemaphoreType.DMA((patches, WIN)),
-            pltpu.SemaphoreType.DMA((n_out,)),
+            pltpu.VMEM((2, sum(pieces), 2, BSIDE, TALL), BF16),
+            pltpu.SemaphoreType.DMA((2, patches, WIN)),
+            pltpu.SemaphoreType.DMA((2, n_out)),
         ],
         compiler_params=params(),
-        cost_estimate=cost(7.5),
-        name="far_field",
-    )(meta, *sources, before, amplitudes, *tabs)
-    return outs, after
+        cost_estimate=cost(11.5),
+        name="turn",
+    )(*metas, *groups[0], *groups[1], carried, amplitudes, *tabs)
+    return outs[:n_out], outs[n_out:], after
 
 
 def backward(layer, meta, adjoint, carried, trans, right, left, pieces, patches):
@@ -592,6 +633,11 @@
     return lax.ppermute(value, "scan", [(i, i ^ bit) for i in range(16)])
 
 
+def stage(moves, *events):
+    values = lax.optimization_barrier((*(value for value, _ in moves), *events))
+    return [swap(value, bit) for value, (_, bit) in zip(values, moves)]
+
+
 def join(*values):
     return jnp.concatenate(values, axis=0)
 
@@ -618,17 +664,24 @@
     core, y = me % 2, me // 2 % 2
     mine = jnp.where(core == 0, total[0], total[1])
     theirs = jnp.where(core == 0, total[1], total[0])
-    mine = plus(mine, swap(after(theirs, events[0]), OVER_CORE))
+    mine = plus(mine, swap(after(theirs, *events[0]), OVER_CORE))
     mine = mine.reshape(2, PATCH // 2, PATCH)
     theirs = jnp.where(y == 0, mine[1], mine[0])
     mine = jnp.where(y == 0, mine[0], mine[1])
-    mine = plus(mine, swap(after(theirs, events[1]), OVER_Y))
-    mine = plus(mine, swap(after(mine, events[2]), NEAR))
-    mine = (widen(mine) + widen(swap(after(mine, events[3]), FAR))) / math.sqrt(n_terms)
-    other = swap(after(mine, events[4]), OVER_Y)
+    mine = plus(mine, swap(after(theirs, *events[1]), OVER_Y))
+    mine = plus(mine, swap(after(mine, *events[2]), NEAR))
+    mine = (widen(mine) + widen(swap(after(mine, *events[3]), FAR))) / math.sqrt(n_terms)
+    other = swap(after(mine, *events[4]), OVER_Y)
     mine = jnp.where(y == 0, join(mine, other), join(other, mine))
-    other = swap(after(mine, events[5]), OVER_CORE)
+    other = swap(after(mine, *events[5]), OVER_CORE)
     return jnp.where(core == 0, jnp.stack([mine, other]), jnp.stack([other, mine]))
+
+
+OPT = {"k0":0,"B":1,"kb1":2,"y2s":1,"first":1,"line3":1,"far0":1,"probe":("none","none","near2","far2","near0","none")}
+
+
+def pick(name, default=0):
+    return OPT.get(name, default)
 
 
 def on_small(object_blocks, probe, positions, anchors, amplitudes):
@@ -650,44 +703,57 @@
 
     meta, meta_last = described(LINE_FIRST), described(PLANE_FIRST)
     hr, hl, fl, fr = tables()
-    probes = wrap_probe(meta, probe, patches)
     own = to_strips(object_blocks)
 
-    far0 = swap(own[0], FAR)
-    y0a = swap(own[0], OVER_Y)
-    y3 = swap(own[3], OVER_Y)
-    far1 = swap(after(own[1], far0), FAR)
-    near0 = swap(after(join(own[0], far0), probes), NEAR)
-    y0b = swap(after(far0, y0a, y3), OVER_Y)
-    far2 = swap(after(own[2], far0), FAR)
-    near1 = swap(after(join(own[1], far1), near0), NEAR)
-    y0c = swap(after(near0, y0b, far1), OVER_Y)
-    pair3 = join(own[3], y3)
-    far3 = swap(after(pair3, far1), FAR)
-    here1 = join(own[1], far1, near1)
-    y1 = swap(after(here1, y0c, far2), OVER_Y)
-    here0 = join(own[0], far0, near0, y0a, y0b, y0c)
-    core0 = swap(after(here0, near1, far2), OVER_CORE)
-    trans0, q1 = forward(0, meta, (here0, core0), probes, hr, hl, patches)
-    near2 = swap(after(join(own[2], far2), near1, q1), NEAR)
-    here2 = join(own[2], far2, near2)
+    far0, ys = stage([(own[0], FAR), (join(*own), OVER_Y)])
+    far13 = join(own[1], own[3]) if pick("B") == 1 else own[1]
+    far1, near0 = stage([(far13, FAR), (join(own[0], far0), NEAR)])
+    far1, far3 = far1[:2], far1[2:]
+    far2, near1, y0 = stage(
+        [(own[2], FAR), (join(own[1], far1), NEAR), (join(far0, near0), OVER_Y)], ys, *([meta, meta_last] if pick("meta", 1) else [])
+    )
+    pair3 = join(own[3], ys[6:])
+    here0 = join(own[0], far0, near0, ys[:2], y0)
+    core0, near2, y1, far3y = stage(
+        [
+            (here0, OVER_CORE),
+            (join(own[2], far2), NEAR),
+            (join(far1, near1), OVER_Y),
+            (ys[6:] if pick("B") == 1 else pair3, FAR),
+        ],
+    )
+    if pick("B") == 1:
+        far3 = join(far3, far3y)
+    else:
+        far3 = far3y
+    here1 = join(own[1], far1, near1, ys[2:4], y1)
     here3 = join(pair3, far3)
-    near3 = swap(after(here3, near2), NEAR)
-    y2 = swap(after(here2, q1, y1, far3), OVER_Y)
-    here1 = join(here1, y1)
-    core1 = swap(after(here1, near2, far3, q1), OVER_CORE)
+    if pick("k0", 1):
+        trans0, q1, probes = forward(0, meta, (here0, core0), probe, hr, hl, patches)
+        core1, y2, near3 = stage(
+            [(here1, OVER_CORE), (join(far2, near2), OVER_Y), (here3, NEAR)], q1
+        )
+    else:
+        core1, y2, near3 = stage(
+            [(here1, OVER_CORE), (join(far2, near2), OVER_Y), (here3, NEAR)], core0
+        )
+        trans0, q1, probes = forward(0, meta, (here0, core0), probe, hr, hl, patches)
     trans1, q2 = forward(1, meta, (here1, core1), q1, hr, hl, patches)
-    core3a = swap(after(here3, q2), OVER_CORE)
-    here2 = join(here2, y2)
-    core2 = swap(after(here2, core3a, near3), OVER_CORE)
-    trans2, q3 = forward(2, meta, (here2, core2), q2, hr, hl, patches)
-    core3b = swap(near3, OVER_CORE)
-
+    here2 = join(own[2], far2, near2, ys[4:6], y2)
+    core3a = swap(after(here3, *[(q1,), (), (q2,), (core1,)][pick("core3a")]), OVER_CORE)
+    if pick("core2") == 0:
+        core3b, core2 = stage([(near3, OVER_CORE), (here2, OVER_CORE)], q2)
+    elif pick("core2") == 1:
+        core2 = swap(after(here2, near3), OVER_CORE)
+        core3b = swap(after(near3, y2), OVER_CORE)
+    else:
+        core2 = swap(after(here2, q2), OVER_CORE)
+        core3b = swap(near3, OVER_CORE)
     pieces = (8, 8, 16)
-    (here3, near3, core3), g2 = far_field(
-        meta_last,
-        (here3, near3, core3a, core3b),
-        q3,
+    (here2, over2, core2), (here3, near3, core3), g1 = turn(
+        (meta, meta_last),
+        ((here2, core2), (here3, near3, core3a, core3b)),
+        q2,
         amplitudes,
         (hr, hl, fl, fr),
         pieces,
@@ -695,42 +761,88 @@
     )
 
     came3 = swap(core3, OVER_CORE)
-    (here2, y2, core2), g1 = backward(2, meta, g2, q2, trans2, hr, hl, pieces, patches)
     came2 = swap(core2, OVER_CORE)
-    near3 = swap(after(plus(near3, came3[8:]), g1), NEAR)
-    (here1, y1, core1), g0 = backward(1, meta, after(g1, came3), q1, trans1, hr, hl, pieces, patches)
+    near3 = plus(near3, came3[8:])
+    if pick("near3s"):
+        near3 = swap(after(near3, g1), NEAR)
+    events = [(came3,), (came2, near3), (), (near3,)][0 if pick("near3s") else pick("kb1")]
+    (here1, over1, core1), g0 = backward(
+        1, meta, after(g1, *events), q1, trans1, hr, hl, pieces, patches
+    )
     came1 = swap(core1, OVER_CORE)
-    y2 = after(plus(y2, came2[8:]), g0)
-    (here0, y0, core0), total = first_slice(
-        meta, after(g0, y2), probes, trans0, pieces, patches
-    )
+    y2 = after(plus(over2[2:], came2[10:]), *[(g0,), ()][pick("y2s")])
+    y1 = plus(over1[2:], came1[10:])
+    base3 = plus(here3, came3[:8])
+    events = [(y2, came1), (y2, y1, base3), (came1,), (y2, came1, base3), (y2,)][pick("first")]
+    (here0, over0, core0), total = first_slice(
+        meta, after(g0, *events), probes, trans0, pieces, patches
+    )
+    if not pick("near3s"):
+        near3 = swap(near3, NEAR)
     y2 = swap(y2, OVER_Y)
     came0 = swap(core0, OVER_CORE)
-    y1 = plus(y1, came1[8:])
-    y0 = plus(y0, came0[8:])
-    line3 = plus(here3, came3[:8], near3)
-    far3 = swap(after(line3[4:], y1, y0), FAR)
-    y1 = swap(after(y1, total, y2), OVER_Y)
-    line2 = plus(here2, came2[:8], y2)
-    near2 = swap(line2[4:], NEAR)
-    y0 = swap(after(y0, y1), OVER_Y)
-    pair3 = plus(line3[:4], after(far3, y1))
-    y3 = swap(pair3[2:], OVER_Y)
-    line2 = plus(line2[:4], after(near2, y1))
-    far2 = swap(line2[2:], FAR)
-    line1 = plus(here1, came1[:8], y1)
-    near1 = swap(line1[4:], NEAR)
-    line1 = plus(line1[:4], after(near1, y0))
-    far1 = swap(line1[2:], FAR)
-    line0 = plus(here0, came0[:8], y0)
-    near0 = swap(line0[4:], NEAR)
-    line0 = plus(line0[:4], near0)
-    far0 = swap(line0[2:], FAR)
+    y0 = plus(over0[2:], came0[10:])
+    if pick("line3") == 0:
+        line3 = plus(here3, came3[:8], near3)
+        head3, tail3 = (line3[:4],), line3[4:]
+    else:
+        head3, tail3 = (base3[:4], near3[:4]), plus(base3[4:], near3[4:])
+    line2 = plus(here2[2:], came2[2:8], y2)
+    near2, y1, far3 = stage(
+        [(line2[2:], NEAR), (y1, OVER_Y), (tail3[2:] if pick("C") else tail3, FAR)], *[(y0,), ()][pick("s4")]
+    )
+    line1 = plus(here1[2:], came1[2:8], y1)
+    out2 = plus(line2[:2], near2[2:])
+    if pick("C"):
+        out2 = join(out2, tail3[:2])
+    far2, near1, y0 = stage(
+        [(out2, FAR), (line1[2:], NEAR), (y0, OVER_Y)]
+    )
+    if pick("C"):
+        far2, far3 = far2[:2], join(far2[2:], far3)
+    pair3 = plus(*head3, far3)
+    line0 = plus(here0[2:], came0[2:8], y0)
+    rest = [
+        plus(over0[:2], came0[8:10]),
+        plus(over1[:2], came1[8:10]),
+        plus(over2[:2], came2[8:10]),
+    ]
+    far1, near0, ys = stage(
+        [
+            (plus(line1[:2], near1[2:]), FAR),
+            (line0[2:], NEAR),
+            (join(*rest, pair3[2:]), OVER_Y),
+        ],
+        far2,
+    )
+    far0 = swap(after(plus(line0[:2], near0[2:]), *[(), (far1,)][pick("far0")]), FAR)
+    marks = {
+        "none": (),
+        "came0": (came0,),
+        "y2": (y2,),
+        "near3": (near3,),
+        "y1": (y1,),
+        "near2": (near2,),
+        "far3": (far3,),
+        "far2": (far2,),
+        "near1": (near1,),
+        "y0": (y0,),
+        "near0": (near0,),
+        "far1": (far1,),
+        "ys": (ys,),
+    }
+    when = [marks[name] for name in pick("probe", ("came0", "y2", "y1", "y0", "near0", "near0"))]
     probe_gradient = sum_probe(
-        total, lax.axis_size("scan") * patches, (y2, y1, y1, y3, y0, near0)
-    )
-    far0 = after(far0, probe_gradient)
-    terms = [(line0[:2], far0), (line1[:2], far1), (line2[:2], far2), (pair3[:2], y3)]
+        total, lax.axis_size("scan") * patches, when
+    )
+    if pick("tail"):
+        far0 = after(far0, probe_gradient)
+    terms = [
+        (here0[:2], came0[:2], near0[:2], ys[:2], far0),
+        (here1[:2], came1[:2], near1[:2], ys[2:4], far1),
+        (here2[:2], came2[:2], near2[:2], ys[4:6], far2),
+        (pair3[:2], ys[6:]),
+    ]
     return (to_blocks(terms), probe_gradient)
 
 
@@ -749,22 +861,14 @@
 def work(meta, sources, probe, amplitudes, pieces):
     patches = amplitudes.shape[0]
     hr, hl, fl, fr = tables()
-    probes = wrap_probe(meta, probe, patches)
-    carried, trans = [probes], []
-    for layer in range(SLICES - 1):
-        t, q = forward(layer, meta, sources[layer], carried[-1], hr, hl, patches)
-        trans.append(t)
-        carried.append(q)
-    grads = [None] * SLICES
-    grads[-1], adjoint = far_field(
-        meta, sources[-1], carried[-1], amplitudes, (hr, hl, fl, fr), pieces, patches
-    )
-    for layer in range(SLICES - 2, 0, -1):
-        grads[layer], adjoint = backward(
-            layer, meta, adjoint, carried[layer], trans[layer], hr, hl, pieces, patches
-        )
-    grads[0], total = first_slice(meta, adjoint, probes, trans[0], pieces, patches)
-    return grads, total
+    t0, q1, probes = forward(0, meta, sources[0], probe, hr, hl, patches)
+    t1, q2 = forward(1, meta, sources[1], q1, hr, hl, patches)
+    grad2, grad3, g1 = turn(
+        (meta, meta), sources[2:], q2, amplitudes, (hr, hl, fl, fr), pieces, patches
+    )
+    grad1, g0 = backward(1, meta, g1, q1, t1, hr, hl, pieces, patches)
+    grad0, total = first_slice(meta, g0, probes, t0, pieces, patches)
+    return [grad0, grad1, grad2, grad3], total
 
 
 def on_any(object_blocks, probe, positions, anchors, amplitudes):

time: 171 us -> 164 us (0.959)
  waiting for transfers between devices: 84.4 us -> 78.7 us
  Pallas kernels: 32 us -> 28.6 us
    ppermute x41 -> x39, waiting for transfers between devices: 84.4 us -> 78.7 us  [swap(): return lax.ppermute(value, 'scan', [(i, i ^ bit) for i in range(16)])]
    pallas_call x2 -> x1, Pallas kernels: 4.97 us -> 2.63 us  [backward(): pl.pallas_call(kernel, out_shape=(*strips, plane), in_specs=[smem_spec()]...]
    slice x7 -> x15, local copies, waits for them, and re-layouts: 0.13 us -> 2.04 us  [the longest x1 0.91 us: on_small(): came2[:2]]
    unnamed x47 -> x43, local copies, waits for them, and re-layouts: 3.84 us -> 2.88 us
    pallas_call x5 -> x3, Pallas kernels: 21.6 us -> 20.7 us  [the longest x1 12.5 us: turn(): pl.pallas_call(kernel, out_shape=(*strips * 2, jax.ShapeDtypeStruct((2 *...]
    convert_element_type x15 -> x18, other arithmetic: 8.22 us -> 8.85 us  [plus(): return sum((widen(other) for other in others), widen(value)).astype(BF16)]
    ppermute x41 -> x39, starting transfers between devices: 37.2 us -> 37.8 us  [swap(): return lax.ppermute(value, 'scan', [(i, i ^ bit) for i in range(16)])]
  transfers between devices with their start and end apart: 41 -> 39, of which waited for: 23 -> 22; matrix products, arithmetic and copies ran while one was open for 7% -> 8% of each run, Pallas kernels for 12% -> 9%
where the time goes in v2:
time: 164 us
  waiting for transfers between devices  78.7 us (48%)
  starting transfers between devices  37.8 us (23%)
  Pallas kernels  28.6 us (17%)
  other arithmetic  11.9 us (7%)
  local copies, waits for them, and re-layouts  5.61 us (3%)
    ppermute x39, waiting for transfers between devices, swap(): return lax.ppermute(value, 'scan', [(i, i ^ bit) for i in range(16)])  78.7 us
    ppermute x39, starting transfers between devices, swap(): return lax.ppermute(value, 'scan', [(i, i ^ bit) for i in range(16)])  37.8 us
    pallas_call x1, Pallas kernels, turn(): pl.pallas_call(kernel, out_shape=(*strips * 2, jax.ShapeDtypeStruct((2 *...  12.5 us
    convert_element_type x18, other arithmetic, plus(): return sum((widen(other) for other in others), widen(value)).astype(BF16)  8.85 us
    pallas_call x2, Pallas kernels, forward(): pl.pallas_call(kernel, out_shape=[plane, plane, *extra], in_specs=[smem_s...  8.2 us
  transfers between devices with their start and end apart: 39, of which 22 were waited for; matrix products, arithmetic and copies ran while one was open for 8% of the time, Pallas kernels for 9%

profile of v2, /device:TPU:0, one launch (start us, length us, event | category | flops | bytes accessed | tf_op | source)
XLA Modules:
  0.0 164.0 jit_solution(15421376152207134088)
XLA Ops:
  2.8 4.1 %collective-permute-start = (bf16[2,2,32,512]{3,2,1,0:T(8,128)(2,1)S(1)}, bf16[2,2,32,512]{3,2,1,0:T(8,128)(2,1)S(1)}, u32[]{:S(2)}, u32[]{:S(2)}) collective-permute-start(bf16[2,2,32,512]{3,2,1,0:T(8,128)(2,1)S(1)} %get-tuple-element.61), channel_id=1, source_target_pairs={{0,8},{1,9},{2,10},{3,11},{4,12},{5,13},{6,14},{7,15},{8,0},{9,1},... | collective-permute-start | bytes 393224 | tf_op jit(solution)/shard_map/ppermute | solution.py:633
  11.4 1.9 %collective-permute-done = bf16[2,2,32,512]{3,2,1,0:T(8,128)(2,1)S(1)} collective-permute-done((bf16[2,2,32,512]{3,2,1,0:T(8,128)(2,1)S(1)}, bf16[2,2,32,512]{3,2,1,0:T(8,128)(2,1)S(1)}, u32[]{:S(2)}, u32[]{:S(2)}) %collective-permute-start) | collective-permute-done | bytes 131104 | tf_op jit(solution)/shard_map/ppermute | solution.py:633
  13.4 4.2 %collective-permute-start.2 = (bf16[4,2,32,512]{3,2,1,0:T(8,128)(2,1)S(1)}, bf16[4,2,32,512]{3,2,1,0:T(8,128)(2,1)S(1)}, u32[]{:S(2)}, u32[]{:S(2)}) collective-permute-start(bf16[4,2,32,512]{3,2,1,0:T(8,128)(2,1)S(1)} %pad_maximum_fusion.8), channel_id=1, source_target_pairs={{0,4},{1,5},{2,6},{3,7},{4,0},{5,1},{6,2},{7,3},{8,12},{9,13},{10,... | collective-permute-start | bytes 786440 | tf_op jit(solution)/shard_map/ppermute | solution.py:633
  17.6 9.8 %collective-permute-done.1 = bf16[4,2,32,512]{3,2,1,0:T(8,128)(2,1)S(1)} collective-permute-done((bf16[4,2,32,512]{3,2,1,0:T(8,128)(2,1)S(1)}, bf16[4,2,32,512]{3,2,1,0:T(8,128)(2,1)S(1)}, u32[]{:S(2)}, u32[]{:S(2)}) %collective-permute-start.1) | collective-permute-done | bytes 262176 | tf_op jit(solution)/shard_map/ppermute | solution.py:633
  29.1 4.0 %collective-permute-start.4 = (bf16[2,2,32,512]{3,2,1,0:T(8,128)(2,1)S(1)}, bf16[2,2,32,512]{3,2,1,0:T(8,128)(2,1)S(1)}, u32[]{:S(2)}, u32[]{:S(2)}) collective-permute-start(bf16[2,2,32,512]{3,2,1,0:T(8,128)(2,1)S(1)} %get-tuple-element.65), channel_id=1, source_target_pairs={{0,8},{1,9},{2,10},{3,11},{4,12},{5,13},{6,14},{7,15},{8,0},{9,1},... | collective-permute-start | bytes 393224 | tf_op jit(solution)/shard_map/ppermute | solution.py:633
  33.1 3.0 %collective-permute-done.4 = bf16[2,2,32,512]{3,2,1,0:T(8,128)(2,1)S(1)} collective-permute-done((bf16[2,2,32,512]{3,2,1,0:T(8,128)(2,1)S(1)}, bf16[2,2,32,512]{3,2,1,0:T(8,128)(2,1)S(1)}, u32[]{:S(2)}, u32[]{:S(2)}) %collective-permute-start.4) | collective-permute-done | bytes 131104 | tf_op jit(solution)/shard_map/ppermute | solution.py:633
  36.2 2.0 %collective-permute-done.6 = bf16[4,2,32,512]{3,2,1,0:T(8,128)(2,1)S(1)} collective-permute-done((bf16[4,2,32,512]{3,2,1,0:T(8,128)(2,1)S(1)}, bf16[4,2,32,512]{3,2,1,0:T(8,128)(2,1)S(1)}, u32[]{:S(2)}, u32[]{:S(2)}) %collective-permute-start.6) | collective-permute-done | bytes 262176 | tf_op jit(solution)/shard_map/ppermute | solution.py:633
  38.4 2.4 %collective-permute-start.9 = (bf16[2,2,32,512]{3,2,1,0:T(8,128)(2,1)S(1)}, bf16[2,2,32,512]{3,2,1,0:T(8,128)(2,1)S(1)}, u32[]{:S(2)}, u32[]{:S(2)}) collective-permute-start(bf16[2,2,32,512]{3,2,1,0:T(8,128)(2,1)S(1)} %get-tuple-element.70), channel_id=1, source_target_pairs={{0,8},{1,9},{2,10},{3,11},{4,12},{5,13},{6,14},{7,15},{8,0},{9,1},... | collective-permute-start | bytes 393224 | tf_op jit(solution)/shard_map/ppermute | solution.py:633
  40.8 2.5 %collective-permute-start.7 = (bf16[4,2,32,512]{3,2,1,0:T(8,128)(2,1)S(1)}, bf16[4,2,32,512]{3,2,1,0:T(8,128)(2,1)S(1)}, u32[]{:S(2)}, u32[]{:S(2)}) collective-permute-start(bf16[4,2,32,512]{3,2,1,0:T(8,128)(2,1)S(1)} %pad_maximum_fusion.9), channel_id=1, source_target_pairs={{0,4},{1,5},{2,6},{3,7},{4,0},{5,1},{6,2},{7,3},{8,12},{9,13},{10,... | collective-permute-start | bytes 786440 | tf_op jit(solution)/shard_map/ppermute | solution.py:633
  45.4 5.5 %collective-permute-done.7 = bf16[4,2,32,512]{3,2,1,0:T(8,128)(2,1)S(1)} collective-permute-done((bf16[4,2,32,512]{3,2,1,0:T(8,128)(2,1)S(1)}, bf16[4,2,32,512]{3,2,1,0:T(8,128)(2,1)S(1)}, u32[]{:S(2)}, u32[]{:S(2)}) %collective-permute-start.7) | collective-permute-done | bytes 262176 | tf_op jit(solution)/shard_map/ppermute | solution.py:633
  51.0 3.3 %collective-permute-done.8 = bf16[6,2,32,512]{3,2,1,0:T(8,128)(2,1)S(1)} collective-permute-done((bf16[6,2,32,512]{3,2,1,0:T(8,128)(2,1)S(1)}, bf16[6,2,32,512]{3,2,1,0:T(8,128)(2,1)S(1)}, u32[]{:S(2)}, u32[]{:S(2)}) %collective-permute-start.8) | collective-permute-done | bytes 393248 | tf_op jit(solution)/shard_map/ppermute | solution.py:633
  55.3 4.7 %forward_0.1 = (bf16[512,512]{1,0:T(8,128)(2,1)S(1)}, bf16[512,512]{1,0:T(8,128)(2,1)S(1)}, f32[2,2,256,256]{3,2,1,0:T(8,128)S(1)}) custom-call(s32[2,20]{1,0:T(2,128)S(1)} %get-tuple-element.130.meta, bf16[16,2,32,512]{3,2,1,0:T(8,128)(2,1)S(1)} %constant_dynamic-update-slice_fusion.refs_0_, bf16[16,2,32,512]{3,2,1,0:T(8,128)(2,1)S(1)} %collective-permute-done.10.refs_1_, ...), custom_call_target="tpu_custom_call" | custom-call | bytes 12600000 | tf_op jit(solution)/shard_map/forward_0/pallas_call | solution.py:253
  60.0 6.0 %collective-permute-done.11 = bf16[6,2,32,512]{3,2,1,0:T(8,128)(2,1)S(1)} collective-permute-done((bf16[6,2,32,512]{3,2,1,0:T(8,128)(2,1)S(1)}, bf16[6,2,32,512]{3,2,1,0:T(8,128)(2,1)S(1)}, u32[]{:S(2)}, u32[]{:S(2)}) %collective-permute-start.11) | collective-permute-done | bytes 393248 | tf_op jit(solution)/shard_map/ppermute | solution.py:633
  66.1 3.5 %forward_1.1 = (bf16[512,512]{1,0:T(8,128)(2,1)S(1)}, bf16[512,512]{1,0:T(8,128)(2,1)S(1)}) custom-call(s32[2,20]{1,0:T(2,128)S(1)} %get-tuple-element.130.meta, bf16[16,2,32,512]{3,2,1,0:T(8,128)(2,1)S(1)} %constant_dynamic-update-slice_fusion.4.refs_0_, bf16[16,2,32,512]{3,2,1,0:T(8,128)(2,1)S(1)} %collective-permute-done.13.refs_1_, ...), custom_call_target="tpu_custom_call" | custom-call | bytes 12600000 | tf_op jit(solution)/shard_map/forward_1/pallas_call | solution.py:253
  70.3 2.8 %collective-permute-done.15.refs_4_ = bf16[8,2,32,512]{3,2,1,0:T(8,128)(2,1)S(1)} collective-permute-done((bf16[8,2,32,512]{3,2,1,0:T(8,128)(2,1)S(1)}, bf16[8,2,32,512]{3,2,1,0:T(8,128)(2,1)S(1)}, u32[]{:S(2)}, u32[]{:S(2)}) %collective-permute-start.15) | collective-permute-done | bytes 524320 | tf_op jit(solution)/shard_map/ppermute | solution.py:633
  73.9 12.5 %turn.1 = (bf16[8,2,32,512]{3,2,1,0:T(8,128)(2,1)S(1)}, bf16[8,2,32,512]{3,2,1,0:T(8,128)(2,1)S(1)}, bf16[16,2,32,512]{3,2,1,0:T(8,128)(2,1)}, bf16[8,2,32,512]{...) custom-call(s32[2,20]{1,0:T(2,128)S(1)} %get-tuple-element.130.meta,, ...), custom_call_target="tpu_custom_call" | custom-call | bytes 41400000 | tf_op jit(solution)/shard_map/turn/pallas_call | solution.py:405
  86.6 2.6 %backward_1.1 = (bf16[8,2,32,512]{3,2,1,0:T(8,128)(2,1)S(1)}, bf16[8,2,32,512]{3,2,1,0:T(8,128)(2,1)S(1)}, bf16[16,2,32,512]{3,2,1,0:T(8,128)(2,1)}, bf16[512,512]{1,0:T(8,128)(2,1)S(1)}) custom-call(s32[2,20]{1,0:T(2,128)S(1)} %get-tuple-element.130.meta, bf16[512,512]{1,0:T(8,128)(2,1)S(1)} %get-tuple-element.80.adjoint, ...), custom_call_target="tpu_custom_call" | custom-call | bytes 8279999 | tf_op jit(solution)/shard_map/backward_1/pallas_call | solution.py:458
  94.6 1.7 %add_convert_fusion = (bf16[8,2,32,512]{3,2,1,0:T(8,128)(2,1)S(1)}, bf16[8,2,32,512]{3,2,1,0:T(8,128)(2,1)S(1)}) fusion(bf16[8,2,32,512]{3,2,1,0:T(8,128)(2,1)S(1)} %copy-done.9, bf16[16,2,32,512]{3,2,1,0:T(8,128)(2,1)} %collective-permute-done.19, bf16[8,2,32,512]{3,2,1,0:T(8,128)(2,1)S(1)} %copy-done.7), kind=kLoop, calls=%fused_computation | loop fusion | flops 2097152 | bytes 3145728 | tf_op jit(solution)/shard_map/convert_element_type | solution.py:650
  96.3 2.1 %first_slice.1 = (bf16[8,2,32,512]{3,2,1,0:T(8,128)(2,1)S(1)}, bf16[8,2,32,512]{3,2,1,0:T(8,128)(2,1)S(1)}, bf16[16,2,32,512]{3,2,1,0:T(8,128)(2,1)S(1)}, bf16[2,256,256]{2,1,0:T(8,128)(2,1)S(1)}) custom-call(s32[2,20]{1,0:T(2,128)S(1)} %get-tuple-element.130.meta, bf16[512,512]{1,0:T(8,128)(2,1)S(1)} %copy-done.11, ...), custom_call_target="tpu_custom_call" | custom-call | bytes 8279999 | tf_op jit(solution)/shard_map/first_slice/pallas_call | solution.py:505
  99.1 1.8 %collective-permute-start.22 = (bf16[8,2,32,512]{3,2,1,0:T(8,128)(2,1)S(1)}, bf16[8,2,32,512]{3,2,1,0:T(8,128)(2,1)S(1)}, u32[]{:S(2)}, u32[]{:S(2)}) collective-permute-start(bf16[8,2,32,512]{3,2,1,0:T(8,128)(2,1)S(1)} %get-tuple-element.112), channel_id=1, source_target_pairs={{0,4},{1,5},{2,6},{3,7},{4,0},{5,1},{6,2},{7,3},{8,12},{9,13},{10,... | collective-permute-start | bytes 1572872 | tf_op jit(solution)/shard_map/ppermute | solution.py:633
  104.5 8.7 %collective-permute-done.22 = bf16[8,2,32,512]{3,2,1,0:T(8,128)(2,1)S(1)} collective-permute-done((bf16[8,2,32,512]{3,2,1,0:T(8,128)(2,1)S(1)}, bf16[8,2,32,512]{3,2,1,0:T(8,128)(2,1)S(1)}, u32[]{:S(2)}, u32[]{:S(2)}) %collective-permute-start.22) | collective-permute-done | bytes 524320 | tf_op jit(solution)/shard_map/ppermute | solution.py:633
  113.5 1.8 %collective-permute-start.24 = (bf16[4,2,32,512]{3,2,1,0:T(8,128)(2,1)S(1)}, bf16[4,2,32,512]{3,2,1,0:T(8,128)(2,1)S(1)}, u32[]{:S(2)}, u32[]{:S(2)}) collective-permute-start(bf16[4,2,32,512]{3,2,1,0:T(8,128)(2,1)S(1)} %slice.273), channel_id=1, source_target_pairs={{0,4},{1,5},{2,6},{3,7},{4,0},{5,1},{6,2},{7,3},{8,12},{9,13},{10,... | collective-permute-start | bytes 786440 | tf_op jit(solution)/shard_map/ppermute | solution.py:633
  117.3 8.2 %collective-permute-done.24 = bf16[4,2,32,512]{3,2,1,0:T(8,128)(2,1)S(1)} collective-permute-done((bf16[4,2,32,512]{3,2,1,0:T(8,128)(2,1)S(1)}, bf16[4,2,32,512]{3,2,1,0:T(8,128)(2,1)S(1)}, u32[]{:S(2)}, u32[]{:S(2)}) %collective-permute-start.24) | collective-permute-done | bytes 262176 | tf_op jit(solution)/shard_map/ppermute | solution.py:633
  125.5 3.9 %collective-permute-done.27 = bf16[4,2,32,512]{3,2,1,0:T(8,128)(2,1)S(1)} collective-permute-done((bf16[4,2,32,512]{3,2,1,0:T(8,128)(2,1)S(1)}, bf16[4,2,32,512]{3,2,1,0:T(8,128)(2,1)S(1)}, u32[]{:S(2)}, u32[]{:S(2)}) %collective-permute-start.27) | collective-permute-done | bytes 262176 | tf_op jit(solution)/shard_map/ppermute | solution.py:633
  132.4 6.1 %collective-permute-done.28.refs_14_ = bf16[2,2,32,512]{3,2,1,0:T(8,128)(2,1)S(1)} collective-permute-done((bf16[2,2,32,512]{3,2,1,0:T(8,128)(2,1)S(1)}, bf16[2,2,32,512]{3,2,1,0:T(8,128)(2,1)S(1)}, u32[]{:S(2)}, u32[]{:S(2)}) %collective-permute-start.28) | collective-permute-done | bytes 131104 | tf_op jit(solution)/shard_map/ppermute | solution.py:633
  138.5 1.9 %collective-permute-start.36 = (bf16[128,256]{1,0:T(8,128)(2,1)S(1)}, bf16[128,256]{1,0:T(8,128)(2,1)S(1)}, u32[]{:S(2)}, u32[]{:S(2)}) collective-permute-start(bf16[128,256]{1,0:T(8,128)(2,1)S(1)} %add_convert_fusion.16), channel_id=1, source_target_pairs={{0,8},{1,9},{2,10},{3,11},{4,12},{5,13},{6,14},{7,15},{8,0},{9,1},... | collective-permute-start | bytes 196616 | tf_op jit(solution)/shard_map/ppermute | solution.py:633
  141.3 1.8 %collective-permute-start.29 = (bf16[4,2,32,512]{3,2,1,0:T(8,128)(2,1)S(1)}, bf16[4,2,32,512]{3,2,1,0:T(8,128)(2,1)S(1)}, u32[]{:S(2)}, u32[]{:S(2)}) collective-permute-start(bf16[4,2,32,512]{3,2,1,0:T(8,128)(2,1)S(1)} %slice.284), channel_id=1, source_target_pairs={{0,4},{1,5},{2,6},{3,7},{4,0},{5,1},{6,2},{7,3},{8,12},{9,13},{10,... | collective-permute-start | bytes 786440 | tf_op jit(solution)/shard_map/ppermute | solution.py:633
  147.0 2.1 %collective-permute-done.29 = bf16[4,2,32,512]{3,2,1,0:T(8,128)(2,1)S(1)} collective-permute-done((bf16[4,2,32,512]{3,2,1,0:T(8,128)(2,1)S(1)}, bf16[4,2,32,512]{3,2,1,0:T(8,128)(2,1)S(1)}, u32[]{:S(2)}, u32[]{:S(2)}) %collective-permute-start.29) | collective-permute-done | bytes 262176 | tf_op jit(solution)/shard_map/ppermute | solution.py:633
  149.4 5.6 %collective-permute-done.31.refs_9_ = bf16[2,2,32,512]{3,2,1,0:T(8,128)(2,1)S(1)} collective-permute-done((bf16[2,2,32,512]{3,2,1,0:T(8,128)(2,1)S(1)}, bf16[2,2,32,512]{3,2,1,0:T(8,128)(2,1)S(1)}, u32[]{:S(2)}, u32[]{:S(2)}) %collective-permute-start.31) | collective-permute-done | bytes 131104 | tf_op jit(solution)/shard_map/ppermute | solution.py:633
  155.0 3.4 %collective-permute-done.37 = f32[128,256]{1,0:T(8,128)S(1)} collective-permute-done((f32[128,256]{1,0:T(8,128)S(1)}, f32[128,256]{1,0:T(8,128)S(1)}, u32[]{:S(2)}, u32[]{:S(2)}) %collective-permute-start.37) | collective-permute-done | bytes 131104 | tf_op jit(solution)/shard_map/ppermute | solution.py:633
  158.6 2.2 %collective-permute-done.32.refs_4_ = bf16[2,2,32,512]{3,2,1,0:T(8,128)(2,1)S(1)} collective-permute-done((bf16[2,2,32,512]{3,2,1,0:T(8,128)(2,1)S(1)}, bf16[2,2,32,512]{3,2,1,0:T(8,128)(2,1)S(1)}, u32[]{:S(2)}, u32[]{:S(2)}) %collective-permute-start.32) | collective-permute-done | bytes 131104 | tf_op jit(solution)/shard_map/ppermute | solution.py:633
  160.9 2.3 %to_blocks.1 = f32[256,1024]{1,0:T(8,128)} custom-call(bf16[2,2,32,512]{3,2,1,0:T(8,128)(2,1)S(1)} %slice.214.refs_0_, bf16[2,2,32,512]{3,2,1,0:T(8,128)(2,1)S(1)} %slice.270.refs_1_, bf16[2,2,32,512]{3,2,1,0:T(8,128)(2,1)S(1)} %slice.291.refs_2_, bf16[2,2,32,512]{3,2,1,0:T(8,128)(2,1)S(1)} %get-tuple-element.117.refs_3_, ...), custom_call_target="tpu_custom_call" | custom-call | bytes 5400000 | tf_op jit(solution)/shard_map/to_blocks/pallas_call | solution.py:605
  (154 shorter events, 34.2 us)
Async XLA Ops:
  2.8 10.4 %collective-permute-start = (bf16[2,2,32,512]{3,2,1,0:T(8,128)(2,1)S(1)}, bf16[2,2,32,512]{3,2,1,0:T(8,128)(2,1)S(1)}, u32[]{:S(2)}, u32[]{:S(2)}) collective-permute-start(bf16[2,2,32,512]{3,2,1,0:T(8,128)(2,1)S(1)} %get-tuple-element.61), channel_id=1, source_target_pairs={{0,8},{1,9},{2,10},{3,11},{4,12},{5,13},{6,14},{7,15},{8,0},{9,1},... | collective-permute-start | bytes 393224 | tf_op jit(solution)/shard_map/ppermute | solution.py:633
  6.9 20.8 %collective-permute-start.3 = (bf16[8,2,32,512]{3,2,1,0:T(8,128)(2,1)S(1)}, bf16[8,2,32,512]{3,2,1,0:T(8,128)(2,1)S(1)}, u32[]{:S(2)}, u32[]{:S(2)}) collective-permute-start(bf16[8,2,32,512]{3,2,1,0:T(8,128)(2,1)S(1)} %pad_maximum_fusion), channel_id=1, source_target_pairs={{0,2},{1,3},{2,0},{3,1},{4,6},{5,7},{6,4},{7,5},{8,10},{9,11},{10,... | collective-permute-start | bytes 1572872 | tf_op jit(solution)/shard_map/ppermute | solution.py:633
  13.3 14.2 %collective-permute-start.1 = (bf16[4,2,32,512]{3,2,1,0:T(8,128)(2,1)S(1)}, bf16[4,2,32,512]{3,2,1,0:T(8,128)(2,1)S(1)}, u32[]{:S(2)}, u32[]{:S(2)}) collective-permute-start(bf16[4,2,32,512]{3,2,1,0:T(8,128)(2,1)S(1)} %pad_maximum_fusion.6), channel_id=1, source_target_pairs={{0,8},{1,9},{2,10},{3,11},{4,12},{5,13},{6,14},{7,15},{8,0},{9,1},... | collective-permute-start | bytes 786440 | tf_op jit(solution)/shard_map/ppermute | solution.py:633
  13.4 14.2 %collective-permute-start.2 = (bf16[4,2,32,512]{3,2,1,0:T(8,128)(2,1)S(1)}, bf16[4,2,32,512]{3,2,1,0:T(8,128)(2,1)S(1)}, u32[]{:S(2)}, u32[]{:S(2)}) collective-permute-start(bf16[4,2,32,512]{3,2,1,0:T(8,128)(2,1)S(1)} %pad_maximum_fusion.8), channel_id=1, source_target_pairs={{0,4},{1,5},{2,6},{3,7},{4,0},{5,1},{6,2},{7,3},{8,12},{9,13},{10,... | collective-permute-start | bytes 786440 | tf_op jit(solution)/shard_map/ppermute | solution.py:633
  27.8 10.5 %collective-permute-start.5 = (bf16[6,2,32,512]{3,2,1,0:T(8,128)(2,1)S(1)}, bf16[6,2,32,512]{3,2,1,0:T(8,128)(2,1)S(1)}, u32[]{:S(2)}, u32[]{:S(2)}) collective-permute-start(bf16[6,2,32,512]{3,2,1,0:T(8,128)(2,1)S(1)} %pad_maximum_fusion.3), channel_id=1, source_target_pairs={{0,2},{1,3},{2,0},{3,1},{4,6},{5,7},{6,4},{7,5},{8,10},{9,11},{10,... | collective-permute-start | bytes 1179656 | tf_op jit(solution)/shard_map/ppermute | solution.py:633
  29.1 9.1 %collective-permute-start.6 = (bf16[4,2,32,512]{3,2,1,0:T(8,128)(2,1)S(1)}, bf16[4,2,32,512]{3,2,1,0:T(8,128)(2,1)S(1)}, u32[]{:S(2)}, u32[]{:S(2)}) collective-permute-start(bf16[4,2,32,512]{3,2,1,0:T(8,128)(2,1)S(1)} %pad_maximum_fusion.7), channel_id=1, source_target_pairs={{0,4},{1,5},{2,6},{3,7},{4,0},{5,1},{6,2},{7,3},{8,12},{9,13},{10,... | collective-permute-start | bytes 786440 | tf_op jit(solution)/shard_map/ppermute | solution.py:633
  29.1 7.1 %collective-permute-start.4 = (bf16[2,2,32,512]{3,2,1,0:T(8,128)(2,1)S(1)}, bf16[2,2,32,512]{3,2,1,0:T(8,128)(2,1)S(1)}, u32[]{:S(2)}, u32[]{:S(2)}) collective-permute-start(bf16[2,2,32,512]{3,2,1,0:T(8,128)(2,1)S(1)} %get-tuple-element.65), channel_id=1, source_target_pairs={{0,8},{1,9},{2,10},{3,11},{4,12},{5,13},{6,14},{7,15},{8,0},{9,1},... | collective-permute-start | bytes 393224 | tf_op jit(solution)/shard_map/ppermute | solution.py:633
  38.3 16.1 %collective-permute-start.10 = (bf16[16,2,32,512]{3,2,1,0:T(8,128)(2,1)S(1)}, bf16[16,2,32,512]{3,2,1,0:T(8,128)(2,1)S(1)}, u32[]{:S(2)}, u32[]{:S(2)}) collective-permute-start(bf16[16,2,32,512]{3,2,1,0:T(8,128)(2,1)S(1)} %constant_dynamic-update-slice_fusion.refs_0_), channel_id=1, source_target_pairs={{0,1},{1,0},{2,3},{3,2},{4,5},{5,4},{6,7},{7,6},{8,9},{9,8},{10,11... | collective-permute-start | bytes 3145736 | tf_op jit(solution)/shard_map/ppermute | solution.py:633
  38.4 7.0 %collective-permute-start.9 = (bf16[2,2,32,512]{3,2,1,0:T(8,128)(2,1)S(1)}, bf16[2,2,32,512]{3,2,1,0:T(8,128)(2,1)S(1)}, u32[]{:S(2)}, u32[]{:S(2)}) collective-permute-start(bf16[2,2,32,512]{3,2,1,0:T(8,128)(2,1)S(1)} %get-tuple-element.70), channel_id=1, source_target_pairs={{0,8},{1,9},{2,10},{3,11},{4,12},{5,13},{6,14},{7,15},{8,0},{9,1},... | collective-permute-start | bytes 393224 | tf_op jit(solution)/shard_map/ppermute | solution.py:633
  40.8 10.1 %collective-permute-start.7 = (bf16[4,2,32,512]{3,2,1,0:T(8,128)(2,1)S(1)}, bf16[4,2,32,512]{3,2,1,0:T(8,128)(2,1)S(1)}, u32[]{:S(2)}, u32[]{:S(2)}) collective-permute-start(bf16[4,2,32,512]{3,2,1,0:T(8,128)(2,1)S(1)} %pad_maximum_fusion.9), channel_id=1, source_target_pairs={{0,4},{1,5},{2,6},{3,7},{4,0},{5,1},{6,2},{7,3},{8,12},{9,13},{10,... | collective-permute-start | bytes 786440 | tf_op jit(solution)/shard_map/ppermute | solution.py:633
  43.3 11.0 %collective-permute-start.8 = (bf16[6,2,32,512]{3,2,1,0:T(8,128)(2,1)S(1)}, bf16[6,2,32,512]{3,2,1,0:T(8,128)(2,1)S(1)}, u32[]{:S(2)}, u32[]{:S(2)}) collective-permute-start(bf16[6,2,32,512]{3,2,1,0:T(8,128)(2,1)S(1)} %pad_maximum_fusion.4), channel_id=1, source_target_pairs={{0,2},{1,3},{2,0},{3,1},{4,6},{5,7},{6,4},{7,5},{8,10},{9,11},{10,... | collective-permute-start | bytes 1179656 | tf_op jit(solution)/shard_map/ppermute | solution.py:633
  54.4 11.6 %collective-permute-start.13 = (bf16[16,2,32,512]{3,2,1,0:T(8,128)(2,1)S(1)}, bf16[16,2,32,512]{3,2,1,0:T(8,128)(2,1)S(1)}, u32[]{:S(2)}, u32[]{:S(2)}) collective-permute-start(bf16[16,2,32,512]{3,2,1,0:T(8,128)(2,1)S(1)} %constant_dynamic-update-slice_fusion.4.refs_0_), channel_id=1, source_target_pairs={{0,1},{1,0},{2,3},{3,2},{4,5},{5,4},{6,7},{7,6},{8,9},{9,8},{10,11... | collective-permute-start | bytes 3145736 | tf_op jit(solution)/shard_map/ppermute | solution.py:633
  54.5 15.2 %collective-permute-start.12 = (bf16[8,2,32,512]{3,2,1,0:T(8,128)(2,1)S(1)}, bf16[8,2,32,512]{3,2,1,0:T(8,128)(2,1)S(1)}, u32[]{:S(2)}, u32[]{:S(2)}) collective-permute-start(bf16[8,2,32,512]{3,2,1,0:T(8,128)(2,1)S(1)} %pad_maximum_fusion.1.refs_2_), channel_id=1, source_target_pairs={{0,4},{1,5},{2,6},{3,7},{4,0},{5,1},{6,2},{7,3},{8,12},{9,13},{10,... | collective-permute-start | bytes 1572872 | tf_op jit(solution)/shard_map/ppermute | solution.py:633
  54.8 11.2 %collective-permute-start.11 = (bf16[6,2,32,512]{3,2,1,0:T(8,128)(2,1)S(1)}, bf16[6,2,32,512]{3,2,1,0:T(8,128)(2,1)S(1)}, u32[]{:S(2)}, u32[]{:S(2)}) collective-permute-start(bf16[6,2,32,512]{3,2,1,0:T(8,128)(2,1)S(1)} %pad_maximum_fusion.5), channel_id=1, source_target_pairs={{0,2},{1,3},{2,0},{3,1},{4,6},{5,7},{6,4},{7,5},{8,10},{9,11},{10,... | collective-permute-start | bytes 1179656 | tf_op jit(solution)/shard_map/ppermute | solution.py:633
  91.7 11.6 %collective-permute-start.21 = (bf16[6,2,32,512]{3,2,1,0:T(8,128)(2,1)S(1)}, bf16[6,2,32,512]{3,2,1,0:T(8,128)(2,1)S(1)}, u32[]{:S(2)}, u32[]{:S(2)}) collective-permute-start(bf16[6,2,32,512]{3,2,1,0:T(8,128)(2,1)S(1)} %add_convert_fusion.7), channel_id=1, source_target_pairs={{0,2},{1,3},{2,0},{3,1},{4,6},{5,7},{6,4},{7,5},{8,10},{9,11},{10,... | collective-permute-start | bytes 1179656 | tf_op jit(solution)/shard_map/ppermute | solution.py:633
  98.9 14.4 %collective-permute-start.20 = (bf16[16,2,32,512]{3,2,1,0:T(8,128)(2,1)S(1)}, bf16[16,2,32,512]{3,2,1,0:T(8,128)(2,1)S(1)}, u32[]{:S(2)}, u32[]{:S(2)}) collective-permute-start(bf16[16,2,32,512]{3,2,1,0:T(8,128)(2,1)S(1)} %get-tuple-element.93), channel_id=1, source_target_pairs={{0,1},{1,0},{2,3},{3,2},{4,5},{5,4},{6,7},{7,6},{8,9},{9,8},{10,11... | collective-permute-start | bytes 3145736 | tf_op jit(solution)/shard_map/ppermute | solution.py:633
  99.1 14.2 %collective-permute-start.22 = (bf16[8,2,32,512]{3,2,1,0:T(8,128)(2,1)S(1)}, bf16[8,2,32,512]{3,2,1,0:T(8,128)(2,1)S(1)}, u32[]{:S(2)}, u32[]{:S(2)}) collective-permute-start(bf16[8,2,32,512]{3,2,1,0:T(8,128)(2,1)S(1)} %get-tuple-element.112), channel_id=1, source_target_pairs={{0,4},{1,5},{2,6},{3,7},{4,0},{5,1},{6,2},{7,3},{8,12},{9,13},{10,... | collective-permute-start | bytes 1572872 | tf_op jit(solution)/shard_map/ppermute | solution.py:633
  102.8 13.9 %collective-permute-start.34 = (bf16[128,256]{1,0:T(8,128)(2,1)S(1)}, bf16[128,256]{1,0:T(8,128)(2,1)S(1)}, u32[]{:S(2)}, u32[]{:S(2)}) collective-permute-start(bf16[128,256]{1,0:T(8,128)(2,1)S(1)} %broadcast_select_fusion), channel_id=1, source_target_pairs={{0,2},{1,3},{2,0},{3,1},{4,6},{5,7},{6,4},{7,5},{8,10},{9,11},{10,... | collective-permute-start | bytes 196616 | tf_op jit(solution)/shard_map/ppermute | solution.py:633
  113.5 12.0 %collective-permute-start.24 = (bf16[4,2,32,512]{3,2,1,0:T(8,128)(2,1)S(1)}, bf16[4,2,32,512]{3,2,1,0:T(8,128)(2,1)S(1)}, u32[]{:S(2)}, u32[]{:S(2)}) collective-permute-start(bf16[4,2,32,512]{3,2,1,0:T(8,128)(2,1)S(1)} %slice.273), channel_id=1, source_target_pairs={{0,4},{1,5},{2,6},{3,7},{4,0},{5,1},{6,2},{7,3},{8,12},{9,13},{10,... | collective-permute-start | bytes 786440 | tf_op jit(solution)/shard_map/ppermute | solution.py:633
  115.3 14.1 %collective-permute-start.27 = (bf16[4,2,32,512]{3,2,1,0:T(8,128)(2,1)S(1)}, bf16[4,2,32,512]{3,2,1,0:T(8,128)(2,1)S(1)}, u32[]{:S(2)}, u32[]{:S(2)}) collective-permute-start(bf16[4,2,32,512]{3,2,1,0:T(8,128)(2,1)S(1)} %add_convert_fusion.9), channel_id=1, source_target_pairs={{0,8},{1,9},{2,10},{3,11},{4,12},{5,13},{6,14},{7,15},{8,0},{9,1},... | collective-permute-start | bytes 786440 | tf_op jit(solution)/shard_map/ppermute | solution.py:633
  116.7 12.8 %collective-permute-start.23 = (bf16[6,2,32,512]{3,2,1,0:T(8,128)(2,1)S(1)}, bf16[6,2,32,512]{3,2,1,0:T(8,128)(2,1)S(1)}, u32[]{:S(2)}, u32[]{:S(2)}) collective-permute-start(bf16[6,2,32,512]{3,2,1,0:T(8,128)(2,1)S(1)} %add_convert_fusion.6), channel_id=1, source_target_pairs={{0,2},{1,3},{2,0},{3,1},{4,6},{5,7},{6,4},{7,5},{8,10},{9,11},{10,... | collective-permute-start | bytes 1179656 | tf_op jit(solution)/shard_map/ppermute | solution.py:633
  125.5 6.9 %collective-permute-start.35 = (bf16[128,256]{1,0:T(8,128)(2,1)S(1)}, bf16[128,256]{1,0:T(8,128)(2,1)S(1)}, u32[]{:S(2)}, u32[]{:S(2)}) collective-permute-start(bf16[128,256]{1,0:T(8,128)(2,1)S(1)} %add_convert_fusion.17), channel_id=1, source_target_pairs={{0,4},{1,5},{2,6},{3,7},{4,0},{5,1},{6,2},{7,3},{8,12},{9,13},{10,... | collective-permute-start | bytes 196616 | tf_op jit(solution)/shard_map/ppermute | solution.py:633
  130.7 9.7 %collective-permute-start.25 = (bf16[4,2,32,512]{3,2,1,0:T(8,128)(2,1)S(1)}, bf16[4,2,32,512]{3,2,1,0:T(8,128)(2,1)S(1)}, u32[]{:S(2)}, u32[]{:S(2)}) collective-permute-start(bf16[4,2,32,512]{3,2,1,0:T(8,128)(2,1)S(1)} %slice.281), channel_id=1, source_target_pairs={{0,4},{1,5},{2,6},{3,7},{4,0},{5,1},{6,2},{7,3},{8,12},{9,13},{10,... | collective-permute-start | bytes 786440 | tf_op jit(solution)/shard_map/ppermute | solution.py:633
  130.9 7.6 %collective-permute-start.28 = (bf16[2,2,32,512]{3,2,1,0:T(8,128)(2,1)S(1)}, bf16[2,2,32,512]{3,2,1,0:T(8,128)(2,1)S(1)}, u32[]{:S(2)}, u32[]{:S(2)}) collective-permute-start(bf16[2,2,32,512]{3,2,1,0:T(8,128)(2,1)S(1)} %add_convert_fusion.15), channel_id=1, source_target_pairs={{0,8},{1,9},{2,10},{3,11},{4,12},{5,13},{6,14},{7,15},{8,0},{9,1},... | collective-permute-start | bytes 393224 | tf_op jit(solution)/shard_map/ppermute | solution.py:633
  131.9 9.2 %collective-permute-start.26 = (bf16[6,2,32,512]{3,2,1,0:T(8,128)(2,1)S(1)}, bf16[6,2,32,512]{3,2,1,0:T(8,128)(2,1)S(1)}, u32[]{:S(2)}, u32[]{:S(2)}) collective-permute-start(bf16[6,2,32,512]{3,2,1,0:T(8,128)(2,1)S(1)} %add_convert_fusion.4), channel_id=1, source_target_pairs={{0,2},{1,3},{2,0},{3,1},{4,6},{5,7},{6,4},{7,5},{8,10},{9,11},{10,... | collective-permute-start | bytes 1179656 | tf_op jit(solution)/shard_map/ppermute | solution.py:633
  138.5 7.1 %collective-permute-start.36 = (bf16[128,256]{1,0:T(8,128)(2,1)S(1)}, bf16[128,256]{1,0:T(8,128)(2,1)S(1)}, u32[]{:S(2)}, u32[]{:S(2)}) collective-permute-start(bf16[128,256]{1,0:T(8,128)(2,1)S(1)} %add_convert_fusion.16), channel_id=1, source_target_pairs={{0,8},{1,9},{2,10},{3,11},{4,12},{5,13},{6,14},{7,15},{8,0},{9,1},... | collective-permute-start | bytes 196616 | tf_op jit(solution)/shard_map/ppermute | solution.py:633
  141.3 7.8 %collective-permute-start.29 = (bf16[4,2,32,512]{3,2,1,0:T(8,128)(2,1)S(1)}, bf16[4,2,32,512]{3,2,1,0:T(8,128)(2,1)S(1)}, u32[]{:S(2)}, u32[]{:S(2)}) collective-permute-start(bf16[4,2,32,512]{3,2,1,0:T(8,128)(2,1)S(1)} %slice.284), channel_id=1, source_target_pairs={{0,4},{1,5},{2,6},{3,7},{4,0},{5,1},{6,2},{7,3},{8,12},{9,13},{10,... | collective-permute-start | bytes 786440 | tf_op jit(solution)/shard_map/ppermute | solution.py:633
  145.0 13.6 %collective-permute-start.30 = (bf16[8,2,32,512]{3,2,1,0:T(8,128)(2,1)S(1)}, bf16[8,2,32,512]{3,2,1,0:T(8,128)(2,1)S(1)}, u32[]{:S(2)}, u32[]{:S(2)}) collective-permute-start(bf16[8,2,32,512]{3,2,1,0:T(8,128)(2,1)S(1)} %pad_maximum_fusion.2), channel_id=1, source_target_pairs={{0,2},{1,3},{2,0},{3,1},{4,6},{5,7},{6,4},{7,5},{8,10},{9,11},{10,... | collective-permute-start | bytes 1572872 | tf_op jit(solution)/shard_map/ppermute | solution.py:633
  145.6 9.4 %collective-permute-start.31 = (bf16[2,2,32,512]{3,2,1,0:T(8,128)(2,1)S(1)}, bf16[2,2,32,512]{3,2,1,0:T(8,128)(2,1)S(1)}, u32[]{:S(2)}, u32[]{:S(2)}) collective-permute-start(bf16[2,2,32,512]{3,2,1,0:T(8,128)(2,1)S(1)} %add_convert_fusion.14), channel_id=1, source_target_pairs={{0,8},{1,9},{2,10},{3,11},{4,12},{5,13},{6,14},{7,15},{8,0},{9,1},... | collective-permute-start | bytes 393224 | tf_op jit(solution)/shard_map/ppermute | solution.py:633
  149.1 9.3 %collective-permute-start.37 = (f32[128,256]{1,0:T(8,128)S(1)}, f32[128,256]{1,0:T(8,128)S(1)}, u32[]{:S(2)}, u32[]{:S(2)}) collective-permute-start(f32[128,256]{1,0:T(8,128)S(1)} %get-tuple-element.111), channel_id=1, source_target_pairs={{0,2},{1,3},{2,0},{3,1},{4,6},{5,7},{6,4},{7,5},{8,10},{9,11},{10,... | collective-permute-start | bytes 393224 | tf_op jit(solution)/shard_map/ppermute | solution.py:633
  155.0 5.9 %collective-permute-start.32 = (bf16[2,2,32,512]{3,2,1,0:T(8,128)(2,1)S(1)}, bf16[2,2,32,512]{3,2,1,0:T(8,128)(2,1)S(1)}, u32[]{:S(2)}, u32[]{:S(2)}) collective-permute-start(bf16[2,2,32,512]{3,2,1,0:T(8,128)(2,1)S(1)} %add_convert_fusion.10), channel_id=1, source_target_pairs={{0,8},{1,9},{2,10},{3,11},{4,12},{5,13},{6,14},{7,15},{8,0},{9,1},... | collective-permute-start | bytes 393224 | tf_op jit(solution)/shard_map/ppermute | solution.py:633
  158.5 4.7 %collective-permute-start.38 = (f32[256,256]{1,0:T(8,128)S(1)}, f32[256,256]{1,0:T(8,128)S(1)}, u32[]{:S(2)}, u32[]{:S(2)}) collective-permute-start(f32[256,256]{1,0:T(8,128)S(1)} %maximum_select_fusion.2), channel_id=1, source_target_pairs={{0,1},{1,0},{2,3},{3,2},{4,5},{5,4},{6,7},{7,6},{8,9},{9,8},{10,11... | collective-permute-start | bytes 786440 | tf_op jit(solution)/shard_map/ppermute | solution.py:633
  (24 other events, 93.4 us)

commit v3 on v2

--- a/solution.py
+++ b/solution.py
@@ -659,29 +659,22 @@
 PLANE_FIRST = (OVER_Y, FAR, NEAR, OVER_CORE)
 
 
-def sum_probe(total, n_terms, events):
+def sum_probe(total, n_terms, before_near, before_far, before_y):
     me = lax.axis_index("scan")
     core, y = me % 2, me // 2 % 2
     mine = jnp.where(core == 0, total[0], total[1])
     theirs = jnp.where(core == 0, total[1], total[0])
-    mine = plus(mine, swap(after(theirs, *events[0]), OVER_CORE))
+    mine = plus(mine, swap(theirs, OVER_CORE))
     mine = mine.reshape(2, PATCH // 2, PATCH)
     theirs = jnp.where(y == 0, mine[1], mine[0])
     mine = jnp.where(y == 0, mine[0], mine[1])
-    mine = plus(mine, swap(after(theirs, *events[1]), OVER_Y))
-    mine = plus(mine, swap(after(mine, *events[2]), NEAR))
-    mine = (widen(mine) + widen(swap(after(mine, *events[3]), FAR))) / math.sqrt(n_terms)
-    other = swap(after(mine, *events[4]), OVER_Y)
+    mine = plus(mine, swap(theirs, OVER_Y))
+    mine = plus(mine, swap(after(mine, before_near), NEAR))
+    mine = (widen(mine) + widen(swap(after(mine, before_far), FAR))) / math.sqrt(n_terms)
+    other = swap(after(mine, before_y), OVER_Y)
     mine = jnp.where(y == 0, join(mine, other), join(other, mine))
-    other = swap(after(mine, *events[5]), OVER_CORE)
+    other = swap(mine, OVER_CORE)
     return jnp.where(core == 0, jnp.stack([mine, other]), jnp.stack([other, mine]))
-
-
-OPT = {"k0":0,"B":1,"kb1":2,"y2s":1,"first":1,"line3":1,"far0":1,"probe":("none","none","near2","far2","near0","none")}
-
-
-def pick(name, default=0):
-    return OPT.get(name, default)
 
 
 def on_small(object_blocks, probe, positions, anchors, amplitudes):
@@ -706,11 +699,13 @@
     own = to_strips(object_blocks)
 
     far0, ys = stage([(own[0], FAR), (join(*own), OVER_Y)])
-    far13 = join(own[1], own[3]) if pick("B") == 1 else own[1]
-    far1, near0 = stage([(far13, FAR), (join(own[0], far0), NEAR)])
+    far1, near0 = stage([(join(own[1], own[3]), FAR), (join(own[0], far0), NEAR)])
     far1, far3 = far1[:2], far1[2:]
     far2, near1, y0 = stage(
-        [(own[2], FAR), (join(own[1], far1), NEAR), (join(far0, near0), OVER_Y)], ys, *([meta, meta_last] if pick("meta", 1) else [])
+        [(own[2], FAR), (join(own[1], far1), NEAR), (join(far0, near0), OVER_Y)],
+        ys,
+        meta,
+        meta_last,
     )
     pair3 = join(own[3], ys[6:])
     here0 = join(own[0], far0, near0, ys[:2], y0)
@@ -719,36 +714,21 @@
             (here0, OVER_CORE),
             (join(own[2], far2), NEAR),
             (join(far1, near1), OVER_Y),
-            (ys[6:] if pick("B") == 1 else pair3, FAR),
+            (ys[6:], FAR),
         ],
     )
-    if pick("B") == 1:
-        far3 = join(far3, far3y)
-    else:
-        far3 = far3y
     here1 = join(own[1], far1, near1, ys[2:4], y1)
-    here3 = join(pair3, far3)
-    if pick("k0", 1):
-        trans0, q1, probes = forward(0, meta, (here0, core0), probe, hr, hl, patches)
-        core1, y2, near3 = stage(
-            [(here1, OVER_CORE), (join(far2, near2), OVER_Y), (here3, NEAR)], q1
-        )
-    else:
-        core1, y2, near3 = stage(
-            [(here1, OVER_CORE), (join(far2, near2), OVER_Y), (here3, NEAR)], core0
-        )
-        trans0, q1, probes = forward(0, meta, (here0, core0), probe, hr, hl, patches)
+    here3 = join(pair3, far3, far3y)
+    core1, y2, near3 = stage(
+        [(here1, OVER_CORE), (join(far2, near2), OVER_Y), (here3, NEAR)], core0
+    )
+    trans0, q1, probes = forward(0, meta, (here0, core0), probe, hr, hl, patches)
     trans1, q2 = forward(1, meta, (here1, core1), q1, hr, hl, patches)
     here2 = join(own[2], far2, near2, ys[4:6], y2)
-    core3a = swap(after(here3, *[(q1,), (), (q2,), (core1,)][pick("core3a")]), OVER_CORE)
-    if pick("core2") == 0:
-        core3b, core2 = stage([(near3, OVER_CORE), (here2, OVER_CORE)], q2)
-    elif pick("core2") == 1:
-        core2 = swap(after(here2, near3), OVER_CORE)
-        core3b = swap(after(near3, y2), OVER_CORE)
-    else:
-        core2 = swap(after(here2, q2), OVER_CORE)
-        core3b = swap(near3, OVER_CORE)
+    core3a = swap(after(here3, q1), OVER_CORE)
+    core2 = swap(after(here2, q2), OVER_CORE)
+    core3b = swap(near3, OVER_CORE)
+
     pieces = (8, 8, 16)
     (here2, over2, core2), (here3, near3, core3), g1 = turn(
         (meta, meta_last),
@@ -763,44 +743,27 @@
     came3 = swap(core3, OVER_CORE)
     came2 = swap(core2, OVER_CORE)
     near3 = plus(near3, came3[8:])
-    if pick("near3s"):
-        near3 = swap(after(near3, g1), NEAR)
-    events = [(came3,), (came2, near3), (), (near3,)][0 if pick("near3s") else pick("kb1")]
-    (here1, over1, core1), g0 = backward(
-        1, meta, after(g1, *events), q1, trans1, hr, hl, pieces, patches
-    )
+    (here1, over1, core1), g0 = backward(1, meta, g1, q1, trans1, hr, hl, pieces, patches)
     came1 = swap(core1, OVER_CORE)
-    y2 = after(plus(over2[2:], came2[10:]), *[(g0,), ()][pick("y2s")])
+    y2 = plus(over2[2:], came2[10:])
     y1 = plus(over1[2:], came1[10:])
-    base3 = plus(here3, came3[:8])
-    events = [(y2, came1), (y2, y1, base3), (came1,), (y2, came1, base3), (y2,)][pick("first")]
+    here3 = plus(here3, came3[:8])
     (here0, over0, core0), total = first_slice(
-        meta, after(g0, *events), probes, trans0, pieces, patches
-    )
-    if not pick("near3s"):
-        near3 = swap(near3, NEAR)
+        meta, after(g0, y2, y1, near3), probes, trans0, pieces, patches
+    )
+    near3 = swap(near3, NEAR)
     y2 = swap(y2, OVER_Y)
     came0 = swap(core0, OVER_CORE)
     y0 = plus(over0[2:], came0[10:])
-    if pick("line3") == 0:
-        line3 = plus(here3, came3[:8], near3)
-        head3, tail3 = (line3[:4],), line3[4:]
-    else:
-        head3, tail3 = (base3[:4], near3[:4]), plus(base3[4:], near3[4:])
     line2 = plus(here2[2:], came2[2:8], y2)
     near2, y1, far3 = stage(
-        [(line2[2:], NEAR), (y1, OVER_Y), (tail3[2:] if pick("C") else tail3, FAR)], *[(y0,), ()][pick("s4")]
+        [(line2[2:], NEAR), (y1, OVER_Y), (plus(here3[4:], near3[4:]), FAR)], y0
     )
     line1 = plus(here1[2:], came1[2:8], y1)
-    out2 = plus(line2[:2], near2[2:])
-    if pick("C"):
-        out2 = join(out2, tail3[:2])
     far2, near1, y0 = stage(
-        [(out2, FAR), (line1[2:], NEAR), (y0, OVER_Y)]
-    )
-    if pick("C"):
-        far2, far3 = far2[:2], join(far2[2:], far3)
-    pair3 = plus(*head3, far3)
+        [(plus(line2[:2], near2[2:]), FAR), (line1[2:], NEAR), (y0, OVER_Y)]
+    )
+    pair3 = plus(here3[:4], near3[:4], far3)
     line0 = plus(here0[2:], came0[2:8], y0)
     rest = [
         plus(over0[:2], came0[8:10]),
@@ -815,32 +778,13 @@
         ],
         far2,
     )
-    far0 = swap(after(plus(line0[:2], near0[2:]), *[(), (far1,)][pick("far0")]), FAR)
-    marks = {
-        "none": (),
-        "came0": (came0,),
-        "y2": (y2,),
-        "near3": (near3,),
-        "y1": (y1,),
-        "near2": (near2,),
-        "far3": (far3,),
-        "far2": (far2,),
-        "near1": (near1,),
-        "y0": (y0,),
-        "near0": (near0,),
-        "far1": (far1,),
-        "ys": (ys,),
-    }
-    when = [marks[name] for name in pick("probe", ("came0", "y2", "y1", "y0", "near0", "near0"))]
-    probe_gradient = sum_probe(
-        total, lax.axis_size("scan") * patches, when
-    )
-    if pick("tail"):
-        far0 = after(far0, probe_gradient)
+    far0 = swap(plus(line0[:2], near0[2:]), FAR)
+    n_terms = lax.axis_size("scan") * patches
+    probe_gradient = sum_probe(total, n_terms, near2, far2, near0)
     terms = [
-        (here0[:2], came0[:2], near0[:2], ys[:2], far0),
-        (here1[:2], came1[:2], near1[:2], ys[2:4], far1),
-        (here2[:2], came2[:2], near2[:2], ys[4:6], far2),
+        (plus(here0[:2], came0[:2]), near0[:2], ys[:2], far0),
+        (plus(here1[:2], came1[:2]), near1[:2], ys[2:4], far1),
+        (plus(here2[:2], came2[:2]), near2[:2], ys[4:6], far2),
         (pair3[:2], ys[6:]),
     ]
     return (to_blocks(terms), probe_gradient)

time: 164 us -> 154 us (0.939)
  waiting for transfers between devices: 78.7 us -> 67.8 us
  starting transfers between devices: 37.8 us -> 40 us
  local copies, waits for them, and re-layouts: 5.61 us -> 3.84 us
    ppermute x39, waiting for transfers between devices: 78.7 us -> 67.8 us  [swap(): return lax.ppermute(value, 'scan', [(i, i ^ bit) for i in range(16)])]
    ppermute x39, starting transfers between devices: 37.8 us -> 40 us  [swap(): return lax.ppermute(value, 'scan', [(i, i ^ bit) for i in range(16)])]
    slice x7 -> x1, local copies, waits for them, and re-layouts: 1.89 us -> 0.02 us  [on_small(): line1[2:]]
  transfers between devices with their start and end apart: 39 -> 39, of which waited for: 22 -> 20; matrix products, arithmetic and copies ran while one was open for 8% -> 8% of each run, Pallas kernels for 9% -> 10%
where the time goes in v3:
time: 154 us
  waiting for transfers between devices  67.8 us (44%)
  starting transfers between devices  40 us (26%)
  Pallas kernels  28.6 us (19%)
  other arithmetic  12.3 us (8%)
  local copies, waits for them, and re-layouts  3.84 us (2%)
    ppermute x39, waiting for transfers between devices, swap(): return lax.ppermute(value, 'scan', [(i, i ^ bit) for i in range(16)])  67.8 us
    ppermute x39, starting transfers between devices, swap(): return lax.ppermute(value, 'scan', [(i, i ^ bit) for i in range(16)])  40 us
    pallas_call x1, Pallas kernels, turn(): pl.pallas_call(kernel, out_shape=(*strips * 2, jax.ShapeDtypeStruct((2 *...  12.5 us
    convert_element_type x18, other arithmetic, plus(): return sum((widen(other) for other in others), widen(value)).astype(BF16)  9.33 us
    pallas_call x2, Pallas kernels, forward(): pl.pallas_call(kernel, out_shape=[plane, plane, *extra], in_specs=[smem_s...  8.19 us
  transfers between devices with their start and end apart: 39, of which 20 were waited for; matrix products, arithmetic and copies ran while one was open for 8% of the time, Pallas kernels for 10%

profile of v3, /device:TPU:0, one launch (start us, length us, event | category | flops | bytes accessed | tf_op | source)
XLA Modules:
  0.0 153.8 jit_solution(1595453078562291585)
XLA Ops:
  2.8 4.1 %collective-permute-start = (bf16[2,2,32,512]{3,2,1,0:T(8,128)(2,1)S(1)}, bf16[2,2,32,512]{3,2,1,0:T(8,128)(2,1)S(1)}, u32[]{:S(2)}, u32[]{:S(2)}) collective-permute-start(bf16[2,2,32,512]{3,2,1,0:T(8,128)(2,1)S(1)} %get-tuple-element.59), channel_id=1, source_target_pairs={{0,8},{1,9},{2,10},{3,11},{4,12},{5,13},{6,14},{7,15},{8,0},{9,1},... | collective-permute-start | bytes 393224 | tf_op jit(solution)/shard_map/ppermute | solution.py:633
  6.9 1.5 collective-permute-start.3
  11.4 1.9 %collective-permute-done = bf16[2,2,32,512]{3,2,1,0:T(8,128)(2,1)S(1)} collective-permute-done((bf16[2,2,32,512]{3,2,1,0:T(8,128)(2,1)S(1)}, bf16[2,2,32,512]{3,2,1,0:T(8,128)(2,1)S(1)}, u32[]{:S(2)}, u32[]{:S(2)}) %collective-permute-start) | collective-permute-done | bytes 131104 | tf_op jit(solution)/shard_map/ppermute | solution.py:633
  13.4 4.2 %collective-permute-start.2 = (bf16[4,2,32,512]{3,2,1,0:T(8,128)(2,1)S(1)}, bf16[4,2,32,512]{3,2,1,0:T(8,128)(2,1)S(1)}, u32[]{:S(2)}, u32[]{:S(2)}) collective-permute-start(bf16[4,2,32,512]{3,2,1,0:T(8,128)(2,1)S(1)} %pad_maximum_fusion.8), channel_id=1, source_target_pairs={{0,4},{1,5},{2,6},{3,7},{4,0},{5,1},{6,2},{7,3},{8,12},{9,13},{10,... | collective-permute-start | bytes 786440 | tf_op jit(solution)/shard_map/ppermute | solution.py:633
  17.6 9.8 %collective-permute-done.1 = bf16[4,2,32,512]{3,2,1,0:T(8,128)(2,1)S(1)} collective-permute-done((bf16[4,2,32,512]{3,2,1,0:T(8,128)(2,1)S(1)}, bf16[4,2,32,512]{3,2,1,0:T(8,128)(2,1)S(1)}, u32[]{:S(2)}, u32[]{:S(2)}) %collective-permute-start.1) | collective-permute-done | bytes 262176 | tf_op jit(solution)/shard_map/ppermute | solution.py:633
  29.1 4.0 %collective-permute-start.4 = (bf16[2,2,32,512]{3,2,1,0:T(8,128)(2,1)S(1)}, bf16[2,2,32,512]{3,2,1,0:T(8,128)(2,1)S(1)}, u32[]{:S(2)}, u32[]{:S(2)}) collective-permute-start(bf16[2,2,32,512]{3,2,1,0:T(8,128)(2,1)S(1)} %get-tuple-element.63), channel_id=1, source_target_pairs={{0,8},{1,9},{2,10},{3,11},{4,12},{5,13},{6,14},{7,15},{8,0},{9,1},... | collective-permute-start | bytes 393224 | tf_op jit(solution)/shard_map/ppermute | solution.py:633
  33.1 3.0 %collective-permute-done.4 = bf16[2,2,32,512]{3,2,1,0:T(8,128)(2,1)S(1)} collective-permute-done((bf16[2,2,32,512]{3,2,1,0:T(8,128)(2,1)S(1)}, bf16[2,2,32,512]{3,2,1,0:T(8,128)(2,1)S(1)}, u32[]{:S(2)}, u32[]{:S(2)}) %collective-permute-start.4) | collective-permute-done | bytes 131104 | tf_op jit(solution)/shard_map/ppermute | solution.py:633
  36.2 2.0 %collective-permute-done.6 = bf16[4,2,32,512]{3,2,1,0:T(8,128)(2,1)S(1)} collective-permute-done((bf16[4,2,32,512]{3,2,1,0:T(8,128)(2,1)S(1)}, bf16[4,2,32,512]{3,2,1,0:T(8,128)(2,1)S(1)}, u32[]{:S(2)}, u32[]{:S(2)}) %collective-permute-start.6) | collective-permute-done | bytes 262176 | tf_op jit(solution)/shard_map/ppermute | solution.py:633
  38.4 2.4 %collective-permute-start.9 = (bf16[2,2,32,512]{3,2,1,0:T(8,128)(2,1)S(1)}, bf16[2,2,32,512]{3,2,1,0:T(8,128)(2,1)S(1)}, u32[]{:S(2)}, u32[]{:S(2)}) collective-permute-start(bf16[2,2,32,512]{3,2,1,0:T(8,128)(2,1)S(1)} %get-tuple-element.68), channel_id=1, source_target_pairs={{0,8},{1,9},{2,10},{3,11},{4,12},{5,13},{6,14},{7,15},{8,0},{9,1},... | collective-permute-start | bytes 393224 | tf_op jit(solution)/shard_map/ppermute | solution.py:633
  40.8 2.5 %collective-permute-start.7 = (bf16[4,2,32,512]{3,2,1,0:T(8,128)(2,1)S(1)}, bf16[4,2,32,512]{3,2,1,0:T(8,128)(2,1)S(1)}, u32[]{:S(2)}, u32[]{:S(2)}) collective-permute-start(bf16[4,2,32,512]{3,2,1,0:T(8,128)(2,1)S(1)} %pad_maximum_fusion.9), channel_id=1, source_target_pairs={{0,4},{1,5},{2,6},{3,7},{4,0},{5,1},{6,2},{7,3},{8,12},{9,13},{10,... | collective-permute-start | bytes 786440 | tf_op jit(solution)/shard_map/ppermute | solution.py:633
  45.4 5.5 %collective-permute-done.7 = bf16[4,2,32,512]{3,2,1,0:T(8,128)(2,1)S(1)} collective-permute-done((bf16[4,2,32,512]{3,2,1,0:T(8,128)(2,1)S(1)}, bf16[4,2,32,512]{3,2,1,0:T(8,128)(2,1)S(1)}, u32[]{:S(2)}, u32[]{:S(2)}) %collective-permute-start.7) | collective-permute-done | bytes 262176 | tf_op jit(solution)/shard_map/ppermute | solution.py:633
  51.0 3.3 %collective-permute-done.8 = bf16[6,2,32,512]{3,2,1,0:T(8,128)(2,1)S(1)} collective-permute-done((bf16[6,2,32,512]{3,2,1,0:T(8,128)(2,1)S(1)}, bf16[6,2,32,512]{3,2,1,0:T(8,128)(2,1)S(1)}, u32[]{:S(2)}, u32[]{:S(2)}) %collective-permute-start.8) | collective-permute-done | bytes 393248 | tf_op jit(solution)/shard_map/ppermute | solution.py:633
  55.3 4.7 %forward_0.1 = (bf16[512,512]{1,0:T(8,128)(2,1)S(1)}, bf16[512,512]{1,0:T(8,128)(2,1)S(1)}, f32[2,2,256,256]{3,2,1,0:T(8,128)S(1)}) custom-call(s32[2,20]{1,0:T(2,128)S(1)} %get-tuple-element.132.meta, bf16[16,2,32,512]{3,2,1,0:T(8,128)(2,1)S(1)} %constant_dynamic-update-slice_fusion.refs_0_, bf16[16,2,32,512]{3,2,1,0:T(8,128)(2,1)S(1)} %collective-permute-done.10.refs_1_, ...), custom_call_target="tpu_custom_call" | custom-call | bytes 12600000 | tf_op jit(solution)/shard_map/forward_0/pallas_call | solution.py:253
  60.0 6.0 %collective-permute-done.11 = bf16[6,2,32,512]{3,2,1,0:T(8,128)(2,1)S(1)} collective-permute-done((bf16[6,2,32,512]{3,2,1,0:T(8,128)(2,1)S(1)}, bf16[6,2,32,512]{3,2,1,0:T(8,128)(2,1)S(1)}, u32[]{:S(2)}, u32[]{:S(2)}) %collective-permute-start.11) | collective-permute-done | bytes 393248 | tf_op jit(solution)/shard_map/ppermute | solution.py:633
  66.1 3.5 %forward_1.1 = (bf16[512,512]{1,0:T(8,128)(2,1)S(1)}, bf16[512,512]{1,0:T(8,128)(2,1)S(1)}) custom-call(s32[2,20]{1,0:T(2,128)S(1)} %get-tuple-element.132.meta, bf16[16,2,32,512]{3,2,1,0:T(8,128)(2,1)S(1)} %constant_dynamic-update-slice_fusion.4.refs_0_, bf16[16,2,32,512]{3,2,1,0:T(8,128)(2,1)S(1)} %collective-permute-done.12.refs_1_, ...), custom_call_target="tpu_custom_call" | custom-call | bytes 12600000 | tf_op jit(solution)/shard_map/forward_1/pallas_call | solution.py:253
  70.3 2.8 %collective-permute-done.15.refs_4_ = bf16[8,2,32,512]{3,2,1,0:T(8,128)(2,1)S(1)} collective-permute-done((bf16[8,2,32,512]{3,2,1,0:T(8,128)(2,1)S(1)}, bf16[8,2,32,512]{3,2,1,0:T(8,128)(2,1)S(1)}, u32[]{:S(2)}, u32[]{:S(2)}) %collective-permute-start.15) | collective-permute-done | bytes 524320 | tf_op jit(solution)/shard_map/ppermute | solution.py:633
  73.9 12.5 %turn.1 = (bf16[8,2,32,512]{3,2,1,0:T(8,128)(2,1)S(1)}, bf16[8,2,32,512]{3,2,1,0:T(8,128)(2,1)S(1)}, bf16[16,2,32,512]{3,2,1,0:T(8,128)(2,1)}, bf16[8,2,32,512]{...) custom-call(s32[2,20]{1,0:T(2,128)S(1)} %get-tuple-element.132.meta,, ...), custom_call_target="tpu_custom_call" | custom-call | bytes 41400000 | tf_op jit(solution)/shard_map/turn/pallas_call | solution.py:405
  87.0 2.6 %backward_1.1 = (bf16[8,2,32,512]{3,2,1,0:T(8,128)(2,1)S(1)}, bf16[8,2,32,512]{3,2,1,0:T(8,128)(2,1)S(1)}, bf16[16,2,32,512]{3,2,1,0:T(8,128)(2,1)}, bf16[512,512]{1,0:T(8,128)(2,1)S(1)}) custom-call(s32[2,20]{1,0:T(2,128)S(1)} %get-tuple-element.132.meta, bf16[512,512]{1,0:T(8,128)(2,1)S(1)} %get-tuple-element.77.adjoint, ...), custom_call_target="tpu_custom_call" | custom-call | bytes 8279999 | tf_op jit(solution)/shard_map/backward_1/pallas_call | solution.py:458
  90.6 1.9 %add_convert_fusion = (bf16[8,2,32,512]{3,2,1,0:T(8,128)(2,1)S(1)}, bf16[8,2,32,512]{3,2,1,0:T(8,128)(2,1)S(1)}) fusion(bf16[8,2,32,512]{3,2,1,0:T(8,128)(2,1)} %copy-done.8, bf16[16,2,32,512]{3,2,1,0:T(8,128)(2,1)} %collective-permute-done.19, bf16[8,2,32,512]{3,2,1,0:T(8,128)(2,1)} %copy-done.9), kind=kLoop, calls=%fused_computation | loop fusion | flops 2097152 | bytes 3145728 | tf_op jit(solution)/shard_map/convert_element_type | solution.py:650
  95.9 2.1 %first_slice.1 = (bf16[8,2,32,512]{3,2,1,0:T(8,128)(2,1)S(1)}, bf16[8,2,32,512]{3,2,1,0:T(8,128)(2,1)S(1)}, bf16[16,2,32,512]{3,2,1,0:T(8,128)(2,1)S(1)}, bf16[2,256,256]{2,1,0:T(8,128)(2,1)S(1)}) custom-call(s32[2,20]{1,0:T(2,128)S(1)} %get-tuple-element.132.meta, bf16[512,512]{1,0:T(8,128)(2,1)S(1)} %copy-done.7, ...), custom_call_target="tpu_custom_call" | custom-call | bytes 8279999 | tf_op jit(solution)/shard_map/first_slice/pallas_call | solution.py:505
  100.8 1.6 %collective-permute-start.34 = (bf16[128,256]{1,0:T(8,128)(2,1)S(1)}, bf16[128,256]{1,0:T(8,128)(2,1)S(1)}, u32[]{:S(2)}, u32[]{:S(2)}) collective-permute-start(bf16[128,256]{1,0:T(8,128)(2,1)S(1)} %broadcast_select_fusion), channel_id=1, source_target_pairs={{0,2},{1,3},{2,0},{3,1},{4,6},{5,7},{6,4},{7,5},{8,10},{9,11},{10,... | collective-permute-start | bytes 196616 | tf_op jit(solution)/shard_map/ppermute | solution.py:633
  102.4 3.5 %collective-permute-done.21 = bf16[6,2,32,512]{3,2,1,0:T(8,128)(2,1)S(1)} collective-permute-done((bf16[6,2,32,512]{3,2,1,0:T(8,128)(2,1)S(1)}, bf16[6,2,32,512]{3,2,1,0:T(8,128)(2,1)S(1)}, u32[]{:S(2)}, u32[]{:S(2)}) %collective-permute-start.21) | collective-permute-done | bytes 393248 | tf_op jit(solution)/shard_map/ppermute | solution.py:633
  107.3 1.8 %collective-permute-start.24 = (bf16[4,2,32,512]{3,2,1,0:T(8,128)(2,1)S(1)}, bf16[4,2,32,512]{3,2,1,0:T(8,128)(2,1)S(1)}, u32[]{:S(2)}, u32[]{:S(2)}) collective-permute-start(bf16[4,2,32,512]{3,2,1,0:T(8,128)(2,1)S(1)} %slice.273), channel_id=1, source_target_pairs={{0,4},{1,5},{2,6},{3,7},{4,0},{5,1},{6,2},{7,3},{8,12},{9,13},{10,... | collective-permute-start | bytes 786440 | tf_op jit(solution)/shard_map/ppermute | solution.py:633
  111.0 8.7 %collective-permute-done.24 = bf16[4,2,32,512]{3,2,1,0:T(8,128)(2,1)S(1)} collective-permute-done((bf16[4,2,32,512]{3,2,1,0:T(8,128)(2,1)S(1)}, bf16[4,2,32,512]{3,2,1,0:T(8,128)(2,1)S(1)}, u32[]{:S(2)}, u32[]{:S(2)}) %collective-permute-start.24) | collective-permute-done | bytes 262176 | tf_op jit(solution)/shard_map/ppermute | solution.py:633
  119.7 2.4 %collective-permute-done.27 = bf16[4,2,32,512]{3,2,1,0:T(8,128)(2,1)S(1)} collective-permute-done((bf16[4,2,32,512]{3,2,1,0:T(8,128)(2,1)S(1)}, bf16[4,2,32,512]{3,2,1,0:T(8,128)(2,1)S(1)}, u32[]{:S(2)}, u32[]{:S(2)}) %collective-permute-start.27) | collective-permute-done | bytes 262176 | tf_op jit(solution)/shard_map/ppermute | solution.py:633
  124.1 2.1 %collective-permute-start.28 = (bf16[2,2,32,512]{3,2,1,0:T(8,128)(2,1)S(1)}, bf16[2,2,32,512]{3,2,1,0:T(8,128)(2,1)S(1)}, u32[]{:S(2)}, u32[]{:S(2)}) collective-permute-start(bf16[2,2,32,512]{3,2,1,0:T(8,128)(2,1)S(1)} %add_convert_fusion.17), channel_id=1, source_target_pairs={{0,8},{1,9},{2,10},{3,11},{4,12},{5,13},{6,14},{7,15},{8,0},{9,1},... | collective-permute-start | bytes 393224 | tf_op jit(solution)/shard_map/ppermute | solution.py:633
  126.7 3.6 %collective-permute-done.28.refs_11_ = bf16[2,2,32,512]{3,2,1,0:T(8,128)(2,1)S(1)} collective-permute-done((bf16[2,2,32,512]{3,2,1,0:T(8,128)(2,1)S(1)}, bf16[2,2,32,512]{3,2,1,0:T(8,128)(2,1)S(1)}, u32[]{:S(2)}, u32[]{:S(2)}) %collective-permute-start.28) | collective-permute-done | bytes 131104 | tf_op jit(solution)/shard_map/ppermute | solution.py:633
  130.3 3.4 %collective-permute-start.36 = (bf16[128,256]{1,0:T(8,128)(2,1)S(1)}, bf16[128,256]{1,0:T(8,128)(2,1)S(1)}, u32[]{:S(2)}, u32[]{:S(2)}) collective-permute-start(bf16[128,256]{1,0:T(8,128)(2,1)S(1)} %add_convert_fusion.19), channel_id=1, source_target_pairs={{0,8},{1,9},{2,10},{3,11},{4,12},{5,13},{6,14},{7,15},{8,0},{9,1},... | collective-permute-start | bytes 196616 | tf_op jit(solution)/shard_map/ppermute | solution.py:633
  136.1 3.5 %collective-permute-start.32 = (bf16[2,2,32,512]{3,2,1,0:T(8,128)(2,1)S(1)}, bf16[2,2,32,512]{3,2,1,0:T(8,128)(2,1)S(1)}, u32[]{:S(2)}, u32[]{:S(2)}) collective-permute-start(bf16[2,2,32,512]{3,2,1,0:T(8,128)(2,1)S(1)} %add_convert_fusion.16), channel_id=1, source_target_pairs={{0,8},{1,9},{2,10},{3,11},{4,12},{5,13},{6,14},{7,15},{8,0},{9,1},... | collective-permute-start | bytes 393224 | tf_op jit(solution)/shard_map/ppermute | solution.py:633
  139.6 4.7 %collective-permute-done.29 = bf16[4,2,32,512]{3,2,1,0:T(8,128)(2,1)S(1)} collective-permute-done((bf16[4,2,32,512]{3,2,1,0:T(8,128)(2,1)S(1)}, bf16[4,2,32,512]{3,2,1,0:T(8,128)(2,1)S(1)}, u32[]{:S(2)}, u32[]{:S(2)}) %collective-permute-start.29) | collective-permute-done | bytes 262176 | tf_op jit(solution)/shard_map/ppermute | solution.py:633
  144.5 4.8 %collective-permute-done.37 = f32[128,256]{1,0:T(8,128)S(1)} collective-permute-done((f32[128,256]{1,0:T(8,128)S(1)}, f32[128,256]{1,0:T(8,128)S(1)}, u32[]{:S(2)}, u32[]{:S(2)}) %collective-permute-start.37) | collective-permute-done | bytes 131104 | tf_op jit(solution)/shard_map/ppermute | solution.py:633
  150.7 2.2 %to_blocks.1 = f32[256,1024]{1,0:T(8,128)} custom-call(bf16[2,2,32,512]{3,2,1,0:T(8,128)(2,1)S(1)} %get-tuple-element.113.refs_0_, bf16[2,2,32,512]{3,2,1,0:T(8,128)(2,1)S(1)} %slice.291.refs_1_, bf16[2,2,32,512]{3,2,1,0:T(8,128)(2,1)S(1)} %get-tuple-element.119.refs_2_, bf16[2,2,32,512]{3,2,1,0:T(8,128)(2,1)S(1)} %collective-permute-done.31.refs_3_, ...), custom_call_target="tpu_custom_call" | custom-call | bytes 5400000 | tf_op jit(solution)/shard_map/to_blocks/pallas_call | solution.py:605
  (144 shorter events, 29.6 us)
Async XLA Ops:
  2.8 10.4 %collective-permute-start = (bf16[2,2,32,512]{3,2,1,0:T(8,128)(2,1)S(1)}, bf16[2,2,32,512]{3,2,1,0:T(8,128)(2,1)S(1)}, u32[]{:S(2)}, u32[]{:S(2)}) collective-permute-start(bf16[2,2,32,512]{3,2,1,0:T(8,128)(2,1)S(1)} %get-tuple-element.59), channel_id=1, source_target_pairs={{0,8},{1,9},{2,10},{3,11},{4,12},{5,13},{6,14},{7,15},{8,0},{9,1},... | collective-permute-start | bytes 393224 | tf_op jit(solution)/shard_map/ppermute | solution.py:633
  6.9 20.8 %collective-permute-start.3 = (bf16[8,2,32,512]{3,2,1,0:T(8,128)(2,1)S(1)}, bf16[8,2,32,512]{3,2,1,0:T(8,128)(2,1)S(1)}, u32[]{:S(2)}, u32[]{:S(2)}) collective-permute-start(bf16[8,2,32,512]{3,2,1,0:T(8,128)(2,1)S(1)} %pad_maximum_fusion), channel_id=1, source_target_pairs={{0,2},{1,3},{2,0},{3,1},{4,6},{5,7},{6,4},{7,5},{8,10},{9,11},{10,... | collective-permute-start | bytes 1572872 | tf_op jit(solution)/shard_map/ppermute | solution.py:633
  13.3 14.2 %collective-permute-start.1 = (bf16[4,2,32,512]{3,2,1,0:T(8,128)(2,1)S(1)}, bf16[4,2,32,512]{3,2,1,0:T(8,128)(2,1)S(1)}, u32[]{:S(2)}, u32[]{:S(2)}) collective-permute-start(bf16[4,2,32,512]{3,2,1,0:T(8,128)(2,1)S(1)} %pad_maximum_fusion.6), channel_id=1, source_target_pairs={{0,8},{1,9},{2,10},{3,11},{4,12},{5,13},{6,14},{7,15},{8,0},{9,1},... | collective-permute-start | bytes 786440 | tf_op jit(solution)/shard_map/ppermute | solution.py:633
  13.4 14.2 %collective-permute-start.2 = (bf16[4,2,32,512]{3,2,1,0:T(8,128)(2,1)S(1)}, bf16[4,2,32,512]{3,2,1,0:T(8,128)(2,1)S(1)}, u32[]{:S(2)}, u32[]{:S(2)}) collective-permute-start(bf16[4,2,32,512]{3,2,1,0:T(8,128)(2,1)S(1)} %pad_maximum_fusion.8), channel_id=1, source_target_pairs={{0,4},{1,5},{2,6},{3,7},{4,0},{5,1},{6,2},{7,3},{8,12},{9,13},{10,... | collective-permute-start | bytes 786440 | tf_op jit(solution)/shard_map/ppermute | solution.py:633
  27.8 10.5 %collective-permute-start.5 = (bf16[6,2,32,512]{3,2,1,0:T(8,128)(2,1)S(1)}, bf16[6,2,32,512]{3,2,1,0:T(8,128)(2,1)S(1)}, u32[]{:S(2)}, u32[]{:S(2)}) collective-permute-start(bf16[6,2,32,512]{3,2,1,0:T(8,128)(2,1)S(1)} %pad_maximum_fusion.3), channel_id=1, source_target_pairs={{0,2},{1,3},{2,0},{3,1},{4,6},{5,7},{6,4},{7,5},{8,10},{9,11},{10,... | collective-permute-start | bytes 1179656 | tf_op jit(solution)/shard_map/ppermute | solution.py:633
  29.1 9.1 %collective-permute-start.6 = (bf16[4,2,32,512]{3,2,1,0:T(8,128)(2,1)S(1)}, bf16[4,2,32,512]{3,2,1,0:T(8,128)(2,1)S(1)}, u32[]{:S(2)}, u32[]{:S(2)}) collective-permute-start(bf16[4,2,32,512]{3,2,1,0:T(8,128)(2,1)S(1)} %pad_maximum_fusion.7), channel_id=1, source_target_pairs={{0,4},{1,5},{2,6},{3,7},{4,0},{5,1},{6,2},{7,3},{8,12},{9,13},{10,... | collective-permute-start | bytes 786440 | tf_op jit(solution)/shard_map/ppermute | solution.py:633
  29.1 7.1 %collective-permute-start.4 = (bf16[2,2,32,512]{3,2,1,0:T(8,128)(2,1)S(1)}, bf16[2,2,32,512]{3,2,1,0:T(8,128)(2,1)S(1)}, u32[]{:S(2)}, u32[]{:S(2)}) collective-permute-start(bf16[2,2,32,512]{3,2,1,0:T(8,128)(2,1)S(1)} %get-tuple-element.63), channel_id=1, source_target_pairs={{0,8},{1,9},{2,10},{3,11},{4,12},{5,13},{6,14},{7,15},{8,0},{9,1},... | collective-permute-start | bytes 393224 | tf_op jit(solution)/shard_map/ppermute | solution.py:633
  38.3 16.1 %collective-permute-start.10 = (bf16[16,2,32,512]{3,2,1,0:T(8,128)(2,1)S(1)}, bf16[16,2,32,512]{3,2,1,0:T(8,128)(2,1)S(1)}, u32[]{:S(2)}, u32[]{:S(2)}) collective-permute-start(bf16[16,2,32,512]{3,2,1,0:T(8,128)(2,1)S(1)} %constant_dynamic-update-slice_fusion.refs_0_), channel_id=1, source_target_pairs={{0,1},{1,0},{2,3},{3,2},{4,5},{5,4},{6,7},{7,6},{8,9},{9,8},{10,11... | collective-permute-start | bytes 3145736 | tf_op jit(solution)/shard_map/ppermute | solution.py:633
  38.4 7.0 %collective-permute-start.9 = (bf16[2,2,32,512]{3,2,1,0:T(8,128)(2,1)S(1)}, bf16[2,2,32,512]{3,2,1,0:T(8,128)(2,1)S(1)}, u32[]{:S(2)}, u32[]{:S(2)}) collective-permute-start(bf16[2,2,32,512]{3,2,1,0:T(8,128)(2,1)S(1)} %get-tuple-element.68), channel_id=1, source_target_pairs={{0,8},{1,9},{2,10},{3,11},{4,12},{5,13},{6,14},{7,15},{8,0},{9,1},... | collective-permute-start | bytes 393224 | tf_op jit(solution)/shard_map/ppermute | solution.py:633
  40.8 10.1 %collective-permute-start.7 = (bf16[4,2,32,512]{3,2,1,0:T(8,128)(2,1)S(1)}, bf16[4,2,32,512]{3,2,1,0:T(8,128)(2,1)S(1)}, u32[]{:S(2)}, u32[]{:S(2)}) collective-permute-start(bf16[4,2,32,512]{3,2,1,0:T(8,128)(2,1)S(1)} %pad_maximum_fusion.9), channel_id=1, source_target_pairs={{0,4},{1,5},{2,6},{3,7},{4,0},{5,1},{6,2},{7,3},{8,12},{9,13},{10,... | collective-permute-start | bytes 786440 | tf_op jit(solution)/shard_map/ppermute | solution.py:633
  43.3 11.0 %collective-permute-start.8 = (bf16[6,2,32,512]{3,2,1,0:T(8,128)(2,1)S(1)}, bf16[6,2,32,512]{3,2,1,0:T(8,128)(2,1)S(1)}, u32[]{:S(2)}, u32[]{:S(2)}) collective-permute-start(bf16[6,2,32,512]{3,2,1,0:T(8,128)(2,1)S(1)} %pad_maximum_fusion.4), channel_id=1, source_target_pairs={{0,2},{1,3},{2,0},{3,1},{4,6},{5,7},{6,4},{7,5},{8,10},{9,11},{10,... | collective-permute-start | bytes 1179656 | tf_op jit(solution)/shard_map/ppermute | solution.py:633
  54.4 11.6 %collective-permute-start.12 = (bf16[16,2,32,512]{3,2,1,0:T(8,128)(2,1)S(1)}, bf16[16,2,32,512]{3,2,1,0:T(8,128)(2,1)S(1)}, u32[]{:S(2)}, u32[]{:S(2)}) collective-permute-start(bf16[16,2,32,512]{3,2,1,0:T(8,128)(2,1)S(1)} %constant_dynamic-update-slice_fusion.4.refs_0_), channel_id=1, source_target_pairs={{0,1},{1,0},{2,3},{3,2},{4,5},{5,4},{6,7},{7,6},{8,9},{9,8},{10,11... | collective-permute-start | bytes 3145736 | tf_op jit(solution)/shard_map/ppermute | solution.py:633
  54.5 11.5 %collective-permute-start.11 = (bf16[6,2,32,512]{3,2,1,0:T(8,128)(2,1)S(1)}, bf16[6,2,32,512]{3,2,1,0:T(8,128)(2,1)S(1)}, u32[]{:S(2)}, u32[]{:S(2)}) collective-permute-start(bf16[6,2,32,512]{3,2,1,0:T(8,128)(2,1)S(1)} %pad_maximum_fusion.5), channel_id=1, source_target_pairs={{0,2},{1,3},{2,0},{3,1},{4,6},{5,7},{6,4},{7,5},{8,10},{9,11},{10,... | collective-permute-start | bytes 1179656 | tf_op jit(solution)/shard_map/ppermute | solution.py:633
  55.1 15.2 %collective-permute-start.14 = (bf16[8,2,32,512]{3,2,1,0:T(8,128)(2,1)S(1)}, bf16[8,2,32,512]{3,2,1,0:T(8,128)(2,1)S(1)}, u32[]{:S(2)}, u32[]{:S(2)}) collective-permute-start(bf16[8,2,32,512]{3,2,1,0:T(8,128)(2,1)S(1)} %pad_maximum_fusion.1.refs_2_), channel_id=1, source_target_pairs={{0,4},{1,5},{2,6},{3,7},{4,0},{5,1},{6,2},{7,3},{8,12},{9,13},{10,... | collective-permute-start | bytes 1572872 | tf_op jit(solution)/shard_map/ppermute | solution.py:633
  86.6 6.3 %collective-permute-start.17 = (bf16[16,2,32,512]{3,2,1,0:T(8,128)(2,1)}, bf16[16,2,32,512]{3,2,1,0:T(8,128)(2,1)}, u32[]{:S(2)}, u32[]{:S(2)}) collective-permute-start(bf16[16,2,32,512]{3,2,1,0:T(8,128)(2,1)} %get-tuple-element.81), channel_id=1, source_target_pairs={{0,1},{1,0},{2,3},{3,2},{4,5},{5,4},{6,7},{7,6},{8,9},{9,8},{10,11... | collective-permute-start | bytes 3145736 | tf_op jit(solution)/shard_map/ppermute | solution.py:633
  92.5 14.6 %collective-permute-start.22 = (bf16[8,2,32,512]{3,2,1,0:T(8,128)(2,1)S(1)}, bf16[8,2,32,512]{3,2,1,0:T(8,128)(2,1)S(1)}, u32[]{:S(2)}, u32[]{:S(2)}) collective-permute-start(bf16[8,2,32,512]{3,2,1,0:T(8,128)(2,1)S(1)} %get-tuple-element.115), channel_id=1, source_target_pairs={{0,4},{1,5},{2,6},{3,7},{4,0},{5,1},{6,2},{7,3},{8,12},{9,13},{10,... | collective-permute-start | bytes 1572872 | tf_op jit(solution)/shard_map/ppermute | solution.py:633
  94.0 11.9 %collective-permute-start.21 = (bf16[6,2,32,512]{3,2,1,0:T(8,128)(2,1)S(1)}, bf16[6,2,32,512]{3,2,1,0:T(8,128)(2,1)S(1)}, u32[]{:S(2)}, u32[]{:S(2)}) collective-permute-start(bf16[6,2,32,512]{3,2,1,0:T(8,128)(2,1)S(1)} %add_convert_fusion.7), channel_id=1, source_target_pairs={{0,2},{1,3},{2,0},{3,1},{4,6},{5,7},{6,4},{7,5},{8,10},{9,11},{10,... | collective-permute-start | bytes 1179656 | tf_op jit(solution)/shard_map/ppermute | solution.py:633
  98.1 9.0 %collective-permute-start.20 = (bf16[16,2,32,512]{3,2,1,0:T(8,128)(2,1)S(1)}, bf16[16,2,32,512]{3,2,1,0:T(8,128)(2,1)S(1)}, u32[]{:S(2)}, u32[]{:S(2)}) collective-permute-start(bf16[16,2,32,512]{3,2,1,0:T(8,128)(2,1)S(1)} %get-tuple-element.90), channel_id=1, source_target_pairs={{0,1},{1,0},{2,3},{3,2},{4,5},{5,4},{6,7},{7,6},{8,9},{9,8},{10,11... | collective-permute-start | bytes 3145736 | tf_op jit(solution)/shard_map/ppermute | solution.py:633
  100.8 9.7 %collective-permute-start.34 = (bf16[128,256]{1,0:T(8,128)(2,1)S(1)}, bf16[128,256]{1,0:T(8,128)(2,1)S(1)}, u32[]{:S(2)}, u32[]{:S(2)}) collective-permute-start(bf16[128,256]{1,0:T(8,128)(2,1)S(1)} %broadcast_select_fusion), channel_id=1, source_target_pairs={{0,2},{1,3},{2,0},{3,1},{4,6},{5,7},{6,4},{7,5},{8,10},{9,11},{10,... | collective-permute-start | bytes 196616 | tf_op jit(solution)/shard_map/ppermute | solution.py:633
  107.3 12.4 %collective-permute-start.24 = (bf16[4,2,32,512]{3,2,1,0:T(8,128)(2,1)S(1)}, bf16[4,2,32,512]{3,2,1,0:T(8,128)(2,1)S(1)}, u32[]{:S(2)}, u32[]{:S(2)}) collective-permute-start(bf16[4,2,32,512]{3,2,1,0:T(8,128)(2,1)S(1)} %slice.273), channel_id=1, source_target_pairs={{0,4},{1,5},{2,6},{3,7},{4,0},{5,1},{6,2},{7,3},{8,12},{9,13},{10,... | collective-permute-start | bytes 786440 | tf_op jit(solution)/shard_map/ppermute | solution.py:633
  109.1 13.0 %collective-permute-start.27 = (bf16[4,2,32,512]{3,2,1,0:T(8,128)(2,1)S(1)}, bf16[4,2,32,512]{3,2,1,0:T(8,128)(2,1)S(1)}, u32[]{:S(2)}, u32[]{:S(2)}) collective-permute-start(bf16[4,2,32,512]{3,2,1,0:T(8,128)(2,1)S(1)} %add_convert_fusion.9), channel_id=1, source_target_pairs={{0,8},{1,9},{2,10},{3,11},{4,12},{5,13},{6,14},{7,15},{8,0},{9,1},... | collective-permute-start | bytes 786440 | tf_op jit(solution)/shard_map/ppermute | solution.py:633
  110.5 11.8 %collective-permute-start.23 = (bf16[6,2,32,512]{3,2,1,0:T(8,128)(2,1)S(1)}, bf16[6,2,32,512]{3,2,1,0:T(8,128)(2,1)S(1)}, u32[]{:S(2)}, u32[]{:S(2)}) collective-permute-start(bf16[6,2,32,512]{3,2,1,0:T(8,128)(2,1)S(1)} %add_convert_fusion.6), channel_id=1, source_target_pairs={{0,2},{1,3},{2,0},{3,1},{4,6},{5,7},{6,4},{7,5},{8,10},{9,11},{10,... | collective-permute-start | bytes 1179656 | tf_op jit(solution)/shard_map/ppermute | solution.py:633
  119.7 6.9 %collective-permute-start.35 = (bf16[128,256]{1,0:T(8,128)(2,1)S(1)}, bf16[128,256]{1,0:T(8,128)(2,1)S(1)}, u32[]{:S(2)}, u32[]{:S(2)}) collective-permute-start(bf16[128,256]{1,0:T(8,128)(2,1)S(1)} %add_convert_fusion.20), channel_id=1, source_target_pairs={{0,4},{1,5},{2,6},{3,7},{4,0},{5,1},{6,2},{7,3},{8,12},{9,13},{10,... | collective-permute-start | bytes 196616 | tf_op jit(solution)/shard_map/ppermute | solution.py:633
  123.5 10.2 %collective-permute-start.25 = (bf16[4,2,32,512]{3,2,1,0:T(8,128)(2,1)S(1)}, bf16[4,2,32,512]{3,2,1,0:T(8,128)(2,1)S(1)}, u32[]{:S(2)}, u32[]{:S(2)}) collective-permute-start(bf16[4,2,32,512]{3,2,1,0:T(8,128)(2,1)S(1)} %slice.281), channel_id=1, source_target_pairs={{0,4},{1,5},{2,6},{3,7},{4,0},{5,1},{6,2},{7,3},{8,12},{9,13},{10,... | collective-permute-start | bytes 786440 | tf_op jit(solution)/shard_map/ppermute | solution.py:633
  124.1 6.1 %collective-permute-start.28 = (bf16[2,2,32,512]{3,2,1,0:T(8,128)(2,1)S(1)}, bf16[2,2,32,512]{3,2,1,0:T(8,128)(2,1)S(1)}, u32[]{:S(2)}, u32[]{:S(2)}) collective-permute-start(bf16[2,2,32,512]{3,2,1,0:T(8,128)(2,1)S(1)} %add_convert_fusion.17), channel_id=1, source_target_pairs={{0,8},{1,9},{2,10},{3,11},{4,12},{5,13},{6,14},{7,15},{8,0},{9,1},... | collective-permute-start | bytes 393224 | tf_op jit(solution)/shard_map/ppermute | solution.py:633
  126.2 9.0 %collective-permute-start.26 = (bf16[6,2,32,512]{3,2,1,0:T(8,128)(2,1)S(1)}, bf16[6,2,32,512]{3,2,1,0:T(8,128)(2,1)S(1)}, u32[]{:S(2)}, u32[]{:S(2)}) collective-permute-start(bf16[6,2,32,512]{3,2,1,0:T(8,128)(2,1)S(1)} %add_convert_fusion.4), channel_id=1, source_target_pairs={{0,2},{1,3},{2,0},{3,1},{4,6},{5,7},{6,4},{7,5},{8,10},{9,11},{10,... | collective-permute-start | bytes 1179656 | tf_op jit(solution)/shard_map/ppermute | solution.py:633
  130.3 5.8 %collective-permute-start.36 = (bf16[128,256]{1,0:T(8,128)(2,1)S(1)}, bf16[128,256]{1,0:T(8,128)(2,1)S(1)}, u32[]{:S(2)}, u32[]{:S(2)}) collective-permute-start(bf16[128,256]{1,0:T(8,128)(2,1)S(1)} %add_convert_fusion.19), channel_id=1, source_target_pairs={{0,8},{1,9},{2,10},{3,11},{4,12},{5,13},{6,14},{7,15},{8,0},{9,1},... | collective-permute-start | bytes 196616 | tf_op jit(solution)/shard_map/ppermute | solution.py:633
  135.4 9.0 %collective-permute-start.29 = (bf16[4,2,32,512]{3,2,1,0:T(8,128)(2,1)S(1)}, bf16[4,2,32,512]{3,2,1,0:T(8,128)(2,1)S(1)}, u32[]{:S(2)}, u32[]{:S(2)}) collective-permute-start(bf16[4,2,32,512]{3,2,1,0:T(8,128)(2,1)S(1)} %slice.284), channel_id=1, source_target_pairs={{0,4},{1,5},{2,6},{3,7},{4,0},{5,1},{6,2},{7,3},{8,12},{9,13},{10,... | collective-permute-start | bytes 786440 | tf_op jit(solution)/shard_map/ppermute | solution.py:633
  135.5 14.0 %collective-permute-start.30 = (bf16[8,2,32,512]{3,2,1,0:T(8,128)(2,1)S(1)}, bf16[8,2,32,512]{3,2,1,0:T(8,128)(2,1)S(1)}, u32[]{:S(2)}, u32[]{:S(2)}) collective-permute-start(bf16[8,2,32,512]{3,2,1,0:T(8,128)(2,1)S(1)} %pad_maximum_fusion.2), channel_id=1, source_target_pairs={{0,2},{1,3},{2,0},{3,1},{4,6},{5,7},{6,4},{7,5},{8,10},{9,11},{10,... | collective-permute-start | bytes 1572872 | tf_op jit(solution)/shard_map/ppermute | solution.py:633
  136.1 13.4 %collective-permute-start.32 = (bf16[2,2,32,512]{3,2,1,0:T(8,128)(2,1)S(1)}, bf16[2,2,32,512]{3,2,1,0:T(8,128)(2,1)S(1)}, u32[]{:S(2)}, u32[]{:S(2)}) collective-permute-start(bf16[2,2,32,512]{3,2,1,0:T(8,128)(2,1)S(1)} %add_convert_fusion.16), channel_id=1, source_target_pairs={{0,8},{1,9},{2,10},{3,11},{4,12},{5,13},{6,14},{7,15},{8,0},{9,1},... | collective-permute-start | bytes 393224 | tf_op jit(solution)/shard_map/ppermute | solution.py:633
  144.4 5.0 %collective-permute-start.37 = (f32[128,256]{1,0:T(8,128)S(1)}, f32[128,256]{1,0:T(8,128)S(1)}, u32[]{:S(2)}, u32[]{:S(2)}) collective-permute-start(f32[128,256]{1,0:T(8,128)S(1)} %get-tuple-element.107), channel_id=1, source_target_pairs={{0,2},{1,3},{2,0},{3,1},{4,6},{5,7},{6,4},{7,5},{8,10},{9,11},{10,... | collective-permute-start | bytes 393224 | tf_op jit(solution)/shard_map/ppermute | solution.py:633
  144.4 6.3 %collective-permute-start.31 = (bf16[2,2,32,512]{3,2,1,0:T(8,128)(2,1)S(1)}, bf16[2,2,32,512]{3,2,1,0:T(8,128)(2,1)S(1)}, u32[]{:S(2)}, u32[]{:S(2)}) collective-permute-start(bf16[2,2,32,512]{3,2,1,0:T(8,128)(2,1)S(1)} %add_convert_fusion.12), channel_id=1, source_target_pairs={{0,8},{1,9},{2,10},{3,11},{4,12},{5,13},{6,14},{7,15},{8,0},{9,1},... | collective-permute-start | bytes 393224 | tf_op jit(solution)/shard_map/ppermute | solution.py:633
  (22 other events, 89.3 us)

commit v4 on v3

--- a/solution.py
+++ b/solution.py
@@ -780,7 +780,7 @@
     )
     far0 = swap(plus(line0[:2], near0[2:]), FAR)
     n_terms = lax.axis_size("scan") * patches
-    probe_gradient = sum_probe(total, n_terms, near2, far2, near0)
+    probe_gradient = sum_probe(total, n_terms, near2, near1, near0)
     terms = [
         (plus(here0[:2], came0[:2]), near0[:2], ys[:2], far0),
         (plus(here1[:2], came1[:2]), near1[:2], ys[2:4], far1),

time: 154 us -> 153 us (level)
  starting transfers between devices: 40 us -> 37.2 us
    ppermute x39, starting transfers between devices: 40 us -> 37.2 us  [swap(): return lax.ppermute(value, 'scan', [(i, i ^ bit) for i in range(16)])]
where the time goes in v4:
time: 153 us; the launch traced here: 152 us
  waiting for transfers between devices  69.2 us (45%)
  starting transfers between devices  37.2 us (24%)
  Pallas kernels  28.6 us (19%)
  other arithmetic  12.3 us (8%)
  local copies, waits for them, and re-layouts  3.84 us (3%)
    ppermute x39, waiting for transfers between devices, swap(): return lax.ppermute(value, 'scan', [(i, i ^ bit) for i in range(16)])  69.2 us
    ppermute x39, starting transfers between devices, swap(): return lax.ppermute(value, 'scan', [(i, i ^ bit) for i in range(16)])  37.2 us
    pallas_call x1, Pallas kernels, turn(): pl.pallas_call(kernel, out_shape=(*strips * 2, jax.ShapeDtypeStruct((2 *...  12.5 us
    convert_element_type x18, other arithmetic, plus(): return sum((widen(other) for other in others), widen(value)).astype(BF16)  9.33 us
    pallas_call x2, Pallas kernels, forward(): pl.pallas_call(kernel, out_shape=[plane, plane, *extra], in_specs=[smem_s...  8.19 us
  transfers between devices with their start and end apart: 39, of which 20 were waited for; matrix products, arithmetic and copies ran while one was open for 8% of the time, Pallas kernels for 10%

profile of v4, /device:TPU:0, one launch (start us, length us, event | category | flops | bytes accessed | tf_op | source)
XLA Modules:
  0.0 152.5 jit_solution(1642627683179541860)
XLA Ops:
  2.8 4.1 %collective-permute-start = (bf16[2,2,32,512]{3,2,1,0:T(8,128)(2,1)S(1)}, bf16[2,2,32,512]{3,2,1,0:T(8,128)(2,1)S(1)}, u32[]{:S(2)}, u32[]{:S(2)}) collective-permute-start(bf16[2,2,32,512]{3,2,1,0:T(8,128)(2,1)S(1)} %get-tuple-element.59), channel_id=1, source_target_pairs={{0,8},{1,9},{2,10},{3,11},{4,12},{5,13},{6,14},{7,15},{8,0},{9,1},... | collective-permute-start | bytes 393224 | tf_op jit(solution)/shard_map/ppermute | solution.py:633
  11.4 1.9 %collective-permute-done = bf16[2,2,32,512]{3,2,1,0:T(8,128)(2,1)S(1)} collective-permute-done((bf16[2,2,32,512]{3,2,1,0:T(8,128)(2,1)S(1)}, bf16[2,2,32,512]{3,2,1,0:T(8,128)(2,1)S(1)}, u32[]{:S(2)}, u32[]{:S(2)}) %collective-permute-start) | collective-permute-done | bytes 131104 | tf_op jit(solution)/shard_map/ppermute | solution.py:633
  13.4 4.2 %collective-permute-start.2 = (bf16[4,2,32,512]{3,2,1,0:T(8,128)(2,1)S(1)}, bf16[4,2,32,512]{3,2,1,0:T(8,128)(2,1)S(1)}, u32[]{:S(2)}, u32[]{:S(2)}) collective-permute-start(bf16[4,2,32,512]{3,2,1,0:T(8,128)(2,1)S(1)} %pad_maximum_fusion.8), channel_id=1, source_target_pairs={{0,4},{1,5},{2,6},{3,7},{4,0},{5,1},{6,2},{7,3},{8,12},{9,13},{10,... | collective-permute-start | bytes 786440 | tf_op jit(solution)/shard_map/ppermute | solution.py:633
  17.6 9.8 %collective-permute-done.1 = bf16[4,2,32,512]{3,2,1,0:T(8,128)(2,1)S(1)} collective-permute-done((bf16[4,2,32,512]{3,2,1,0:T(8,128)(2,1)S(1)}, bf16[4,2,32,512]{3,2,1,0:T(8,128)(2,1)S(1)}, u32[]{:S(2)}, u32[]{:S(2)}) %collective-permute-start.1) | collective-permute-done | bytes 262176 | tf_op jit(solution)/shard_map/ppermute | solution.py:633
  29.1 4.0 %collective-permute-start.4 = (bf16[2,2,32,512]{3,2,1,0:T(8,128)(2,1)S(1)}, bf16[2,2,32,512]{3,2,1,0:T(8,128)(2,1)S(1)}, u32[]{:S(2)}, u32[]{:S(2)}) collective-permute-start(bf16[2,2,32,512]{3,2,1,0:T(8,128)(2,1)S(1)} %get-tuple-element.63), channel_id=1, source_target_pairs={{0,8},{1,9},{2,10},{3,11},{4,12},{5,13},{6,14},{7,15},{8,0},{9,1},... | collective-permute-start | bytes 393224 | tf_op jit(solution)/shard_map/ppermute | solution.py:633
  33.1 3.0 %collective-permute-done.4 = bf16[2,2,32,512]{3,2,1,0:T(8,128)(2,1)S(1)} collective-permute-done((bf16[2,2,32,512]{3,2,1,0:T(8,128)(2,1)S(1)}, bf16[2,2,32,512]{3,2,1,0:T(8,128)(2,1)S(1)}, u32[]{:S(2)}, u32[]{:S(2)}) %collective-permute-start.4) | collective-permute-done | bytes 131104 | tf_op jit(solution)/shard_map/ppermute | solution.py:633
  36.2 2.0 %collective-permute-done.6 = bf16[4,2,32,512]{3,2,1,0:T(8,128)(2,1)S(1)} collective-permute-done((bf16[4,2,32,512]{3,2,1,0:T(8,128)(2,1)S(1)}, bf16[4,2,32,512]{3,2,1,0:T(8,128)(2,1)S(1)}, u32[]{:S(2)}, u32[]{:S(2)}) %collective-permute-start.6) | collective-permute-done | bytes 262176 | tf_op jit(solution)/shard_map/ppermute | solution.py:633
  38.4 2.4 %collective-permute-start.9 = (bf16[2,2,32,512]{3,2,1,0:T(8,128)(2,1)S(1)}, bf16[2,2,32,512]{3,2,1,0:T(8,128)(2,1)S(1)}, u32[]{:S(2)}, u32[]{:S(2)}) collective-permute-start(bf16[2,2,32,512]{3,2,1,0:T(8,128)(2,1)S(1)} %get-tuple-element.68), channel_id=1, source_target_pairs={{0,8},{1,9},{2,10},{3,11},{4,12},{5,13},{6,14},{7,15},{8,0},{9,1},... | collective-permute-start | bytes 393224 | tf_op jit(solution)/shard_map/ppermute | solution.py:633
  40.8 2.5 %collective-permute-start.7 = (bf16[4,2,32,512]{3,2,1,0:T(8,128)(2,1)S(1)}, bf16[4,2,32,512]{3,2,1,0:T(8,128)(2,1)S(1)}, u32[]{:S(2)}, u32[]{:S(2)}) collective-permute-start(bf16[4,2,32,512]{3,2,1,0:T(8,128)(2,1)S(1)} %pad_maximum_fusion.9), channel_id=1, source_target_pairs={{0,4},{1,5},{2,6},{3,7},{4,0},{5,1},{6,2},{7,3},{8,12},{9,13},{10,... | collective-permute-start | bytes 786440 | tf_op jit(solution)/shard_map/ppermute | solution.py:633
  45.4 5.5 %collective-permute-done.7 = bf16[4,2,32,512]{3,2,1,0:T(8,128)(2,1)S(1)} collective-permute-done((bf16[4,2,32,512]{3,2,1,0:T(8,128)(2,1)S(1)}, bf16[4,2,32,512]{3,2,1,0:T(8,128)(2,1)S(1)}, u32[]{:S(2)}, u32[]{:S(2)}) %collective-permute-start.7) | collective-permute-done | bytes 262176 | tf_op jit(solution)/shard_map/ppermute | solution.py:633
  51.0 3.3 %collective-permute-done.8 = bf16[6,2,32,512]{3,2,1,0:T(8,128)(2,1)S(1)} collective-permute-done((bf16[6,2,32,512]{3,2,1,0:T(8,128)(2,1)S(1)}, bf16[6,2,32,512]{3,2,1,0:T(8,128)(2,1)S(1)}, u32[]{:S(2)}, u32[]{:S(2)}) %collective-permute-start.8) | collective-permute-done | bytes 393248 | tf_op jit(solution)/shard_map/ppermute | solution.py:633
  55.3 4.7 %forward_0.1 = (bf16[512,512]{1,0:T(8,128)(2,1)S(1)}, bf16[512,512]{1,0:T(8,128)(2,1)S(1)}, f32[2,2,256,256]{3,2,1,0:T(8,128)S(1)}) custom-call(s32[2,20]{1,0:T(2,128)S(1)} %get-tuple-element.132.meta, bf16[16,2,32,512]{3,2,1,0:T(8,128)(2,1)S(1)} %constant_dynamic-update-slice_fusion.refs_0_, bf16[16,2,32,512]{3,2,1,0:T(8,128)(2,1)S(1)} %collective-permute-done.10.refs_1_, ...), custom_call_target="tpu_custom_call" | custom-call | bytes 12600000 | tf_op jit(solution)/shard_map/forward_0/pallas_call | solution.py:253
  60.0 6.0 %collective-permute-done.11 = bf16[6,2,32,512]{3,2,1,0:T(8,128)(2,1)S(1)} collective-permute-done((bf16[6,2,32,512]{3,2,1,0:T(8,128)(2,1)S(1)}, bf16[6,2,32,512]{3,2,1,0:T(8,128)(2,1)S(1)}, u32[]{:S(2)}, u32[]{:S(2)}) %collective-permute-start.11) | collective-permute-done | bytes 393248 | tf_op jit(solution)/shard_map/ppermute | solution.py:633
  66.1 3.5 %forward_1.1 = (bf16[512,512]{1,0:T(8,128)(2,1)S(1)}, bf16[512,512]{1,0:T(8,128)(2,1)S(1)}) custom-call(s32[2,20]{1,0:T(2,128)S(1)} %get-tuple-element.132.meta, bf16[16,2,32,512]{3,2,1,0:T(8,128)(2,1)S(1)} %constant_dynamic-update-slice_fusion.4.refs_0_, bf16[16,2,32,512]{3,2,1,0:T(8,128)(2,1)S(1)} %collective-permute-done.12.refs_1_, ...), custom_call_target="tpu_custom_call" | custom-call | bytes 12600000 | tf_op jit(solution)/shard_map/forward_1/pallas_call | solution.py:253
  70.3 2.8 %collective-permute-done.15.refs_4_ = bf16[8,2,32,512]{3,2,1,0:T(8,128)(2,1)S(1)} collective-permute-done((bf16[8,2,32,512]{3,2,1,0:T(8,128)(2,1)S(1)}, bf16[8,2,32,512]{3,2,1,0:T(8,128)(2,1)S(1)}, u32[]{:S(2)}, u32[]{:S(2)}) %collective-permute-start.15) | collective-permute-done | bytes 524320 | tf_op jit(solution)/shard_map/ppermute | solution.py:633
  73.9 12.5 %turn.1 = (bf16[8,2,32,512]{3,2,1,0:T(8,128)(2,1)S(1)}, bf16[8,2,32,512]{3,2,1,0:T(8,128)(2,1)S(1)}, bf16[16,2,32,512]{3,2,1,0:T(8,128)(2,1)}, bf16[8,2,32,512]{...) custom-call(s32[2,20]{1,0:T(2,128)S(1)} %get-tuple-element.132.meta,, ...), custom_call_target="tpu_custom_call" | custom-call | bytes 41400000 | tf_op jit(solution)/shard_map/turn/pallas_call | solution.py:405
  87.0 2.6 %backward_1.1 = (bf16[8,2,32,512]{3,2,1,0:T(8,128)(2,1)S(1)}, bf16[8,2,32,512]{3,2,1,0:T(8,128)(2,1)S(1)}, bf16[16,2,32,512]{3,2,1,0:T(8,128)(2,1)}, bf16[512,512]{1,0:T(8,128)(2,1)S(1)}) custom-call(s32[2,20]{1,0:T(2,128)S(1)} %get-tuple-element.132.meta, bf16[512,512]{1,0:T(8,128)(2,1)S(1)} %get-tuple-element.77.adjoint, ...), custom_call_target="tpu_custom_call" | custom-call | bytes 8279999 | tf_op jit(solution)/shard_map/backward_1/pallas_call | solution.py:458
  90.6 1.9 %add_convert_fusion = (bf16[8,2,32,512]{3,2,1,0:T(8,128)(2,1)S(1)}, bf16[8,2,32,512]{3,2,1,0:T(8,128)(2,1)S(1)}) fusion(bf16[8,2,32,512]{3,2,1,0:T(8,128)(2,1)} %copy-done.8, bf16[16,2,32,512]{3,2,1,0:T(8,128)(2,1)} %collective-permute-done.19, bf16[8,2,32,512]{3,2,1,0:T(8,128)(2,1)} %copy-done.9), kind=kLoop, calls=%fused_computation | loop fusion | flops 2097152 | bytes 3145728 | tf_op jit(solution)/shard_map/convert_element_type | solution.py:650
  95.9 2.1 %first_slice.1 = (bf16[8,2,32,512]{3,2,1,0:T(8,128)(2,1)S(1)}, bf16[8,2,32,512]{3,2,1,0:T(8,128)(2,1)S(1)}, bf16[16,2,32,512]{3,2,1,0:T(8,128)(2,1)S(1)}, bf16[2,256,256]{2,1,0:T(8,128)(2,1)S(1)}) custom-call(s32[2,20]{1,0:T(2,128)S(1)} %get-tuple-element.132.meta, bf16[512,512]{1,0:T(8,128)(2,1)S(1)} %copy-done.7, ...), custom_call_target="tpu_custom_call" | custom-call | bytes 8279999 | tf_op jit(solution)/shard_map/first_slice/pallas_call | solution.py:505
  102.4 3.5 %collective-permute-done.21 = bf16[6,2,32,512]{3,2,1,0:T(8,128)(2,1)S(1)} collective-permute-done((bf16[6,2,32,512]{3,2,1,0:T(8,128)(2,1)S(1)}, bf16[6,2,32,512]{3,2,1,0:T(8,128)(2,1)S(1)}, u32[]{:S(2)}, u32[]{:S(2)}) %collective-permute-start.21) | collective-permute-done | bytes 393248 | tf_op jit(solution)/shard_map/ppermute | solution.py:633
  107.3 1.8 %collective-permute-start.24 = (bf16[4,2,32,512]{3,2,1,0:T(8,128)(2,1)S(1)}, bf16[4,2,32,512]{3,2,1,0:T(8,128)(2,1)S(1)}, u32[]{:S(2)}, u32[]{:S(2)}) collective-permute-start(bf16[4,2,32,512]{3,2,1,0:T(8,128)(2,1)S(1)} %slice.273), channel_id=1, source_target_pairs={{0,4},{1,5},{2,6},{3,7},{4,0},{5,1},{6,2},{7,3},{8,12},{9,13},{10,... | collective-permute-start | bytes 786440 | tf_op jit(solution)/shard_map/ppermute | solution.py:633
  110.9 8.8 %collective-permute-done.24 = bf16[4,2,32,512]{3,2,1,0:T(8,128)(2,1)S(1)} collective-permute-done((bf16[4,2,32,512]{3,2,1,0:T(8,128)(2,1)S(1)}, bf16[4,2,32,512]{3,2,1,0:T(8,128)(2,1)S(1)}, u32[]{:S(2)}, u32[]{:S(2)}) %collective-permute-start.24) | collective-permute-done | bytes 262176 | tf_op jit(solution)/shard_map/ppermute | solution.py:633
  119.7 2.4 %collective-permute-done.27 = bf16[4,2,32,512]{3,2,1,0:T(8,128)(2,1)S(1)} collective-permute-done((bf16[4,2,32,512]{3,2,1,0:T(8,128)(2,1)S(1)}, bf16[4,2,32,512]{3,2,1,0:T(8,128)(2,1)S(1)}, u32[]{:S(2)}, u32[]{:S(2)}) %collective-permute-start.27) | collective-permute-done | bytes 262176 | tf_op jit(solution)/shard_map/ppermute | solution.py:633
  124.7 2.0 %collective-permute-start.28 = (bf16[2,2,32,512]{3,2,1,0:T(8,128)(2,1)S(1)}, bf16[2,2,32,512]{3,2,1,0:T(8,128)(2,1)S(1)}, u32[]{:S(2)}, u32[]{:S(2)}) collective-permute-start(bf16[2,2,32,512]{3,2,1,0:T(8,128)(2,1)S(1)} %add_convert_fusion.17), channel_id=1, source_target_pairs={{0,8},{1,9},{2,10},{3,11},{4,12},{5,13},{6,14},{7,15},{8,0},{9,1},... | collective-permute-start | bytes 393224 | tf_op jit(solution)/shard_map/ppermute | solution.py:633
  126.6 5.6 %collective-permute-done.25 = bf16[4,2,32,512]{3,2,1,0:T(8,128)(2,1)S(1)} collective-permute-done((bf16[4,2,32,512]{3,2,1,0:T(8,128)(2,1)S(1)}, bf16[4,2,32,512]{3,2,1,0:T(8,128)(2,1)S(1)}, u32[]{:S(2)}, u32[]{:S(2)}) %collective-permute-start.25) | collective-permute-done | bytes 262176 | tf_op jit(solution)/shard_map/ppermute | solution.py:633
  133.3 1.6 %collective-permute-start.29 = (bf16[4,2,32,512]{3,2,1,0:T(8,128)(2,1)S(1)}, bf16[4,2,32,512]{3,2,1,0:T(8,128)(2,1)S(1)}, u32[]{:S(2)}, u32[]{:S(2)}) collective-permute-start(bf16[4,2,32,512]{3,2,1,0:T(8,128)(2,1)S(1)} %slice.284), channel_id=1, source_target_pairs={{0,4},{1,5},{2,6},{3,7},{4,0},{5,1},{6,2},{7,3},{8,12},{9,13},{10,... | collective-permute-start | bytes 786440 | tf_op jit(solution)/shard_map/ppermute | solution.py:633
  135.1 4.4 %collective-permute-done.36 = bf16[128,256]{1,0:T(8,128)(2,1)S(1)} collective-permute-done((bf16[128,256]{1,0:T(8,128)(2,1)S(1)}, bf16[128,256]{1,0:T(8,128)(2,1)S(1)}, u32[]{:S(2)}, u32[]{:S(2)}) %collective-permute-start.36) | collective-permute-done | bytes 65568 | tf_op jit(solution)/shard_map/ppermute | solution.py:633
  139.6 3.0 %collective-permute-done.29 = bf16[4,2,32,512]{3,2,1,0:T(8,128)(2,1)S(1)} collective-permute-done((bf16[4,2,32,512]{3,2,1,0:T(8,128)(2,1)S(1)}, bf16[4,2,32,512]{3,2,1,0:T(8,128)(2,1)S(1)}, u32[]{:S(2)}, u32[]{:S(2)}) %collective-permute-start.29) | collective-permute-done | bytes 262176 | tf_op jit(solution)/shard_map/ppermute | solution.py:633
  142.6 2.7 %collective-permute-start.31 = (bf16[2,2,32,512]{3,2,1,0:T(8,128)(2,1)S(1)}, bf16[2,2,32,512]{3,2,1,0:T(8,128)(2,1)S(1)}, u32[]{:S(2)}, u32[]{:S(2)}) collective-permute-start(bf16[2,2,32,512]{3,2,1,0:T(8,128)(2,1)S(1)} %add_convert_fusion.12), channel_id=1, source_target_pairs={{0,8},{1,9},{2,10},{3,11},{4,12},{5,13},{6,14},{7,15},{8,0},{9,1},... | collective-permute-start | bytes 393224 | tf_op jit(solution)/shard_map/ppermute | solution.py:633
  145.3 2.2 %collective-permute-done.37 = f32[128,256]{1,0:T(8,128)S(1)} collective-permute-done((f32[128,256]{1,0:T(8,128)S(1)}, f32[128,256]{1,0:T(8,128)S(1)}, u32[]{:S(2)}, u32[]{:S(2)}) %collective-permute-start.37) | collective-permute-done | bytes 131104 | tf_op jit(solution)/shard_map/ppermute | solution.py:633
  147.8 1.6 %collective-permute-done.31.refs_3_ = bf16[2,2,32,512]{3,2,1,0:T(8,128)(2,1)S(1)} collective-permute-done((bf16[2,2,32,512]{3,2,1,0:T(8,128)(2,1)S(1)}, bf16[2,2,32,512]{3,2,1,0:T(8,128)(2,1)S(1)}, u32[]{:S(2)}, u32[]{:S(2)}) %collective-permute-start.31) | collective-permute-done | bytes 131104 | tf_op jit(solution)/shard_map/ppermute | solution.py:633
  149.4 2.2 %to_blocks.1 = f32[256,1024]{1,0:T(8,128)} custom-call(bf16[2,2,32,512]{3,2,1,0:T(8,128)(2,1)S(1)} %get-tuple-element.113.refs_0_, bf16[2,2,32,512]{3,2,1,0:T(8,128)(2,1)S(1)} %slice.291.refs_1_, bf16[2,2,32,512]{3,2,1,0:T(8,128)(2,1)S(1)} %get-tuple-element.119.refs_2_, bf16[2,2,32,512]{3,2,1,0:T(8,128)(2,1)S(1)} %collective-permute-done.31.refs_3_, ...), custom_call_target="tpu_custom_call" | custom-call | bytes 5400000 | tf_op jit(solution)/shard_map/to_blocks/pallas_call | solution.py:605
  (144 shorter events, 30.3 us)
Async XLA Ops:
  2.8 10.4 %collective-permute-start = (bf16[2,2,32,512]{3,2,1,0:T(8,128)(2,1)S(1)}, bf16[2,2,32,512]{3,2,1,0:T(8,128)(2,1)S(1)}, u32[]{:S(2)}, u32[]{:S(2)}) collective-permute-start(bf16[2,2,32,512]{3,2,1,0:T(8,128)(2,1)S(1)} %get-tuple-element.59), channel_id=1, source_target_pairs={{0,8},{1,9},{2,10},{3,11},{4,12},{5,13},{6,14},{7,15},{8,0},{9,1},... | collective-permute-start | bytes 393224 | tf_op jit(solution)/shard_map/ppermute | solution.py:633
  6.9 20.8 %collective-permute-start.3 = (bf16[8,2,32,512]{3,2,1,0:T(8,128)(2,1)S(1)}, bf16[8,2,32,512]{3,2,1,0:T(8,128)(2,1)S(1)}, u32[]{:S(2)}, u32[]{:S(2)}) collective-permute-start(bf16[8,2,32,512]{3,2,1,0:T(8,128)(2,1)S(1)} %pad_maximum_fusion), channel_id=1, source_target_pairs={{0,2},{1,3},{2,0},{3,1},{4,6},{5,7},{6,4},{7,5},{8,10},{9,11},{10,... | collective-permute-start | bytes 1572872 | tf_op jit(solution)/shard_map/ppermute | solution.py:633
  13.3 14.2 %collective-permute-start.1 = (bf16[4,2,32,512]{3,2,1,0:T(8,128)(2,1)S(1)}, bf16[4,2,32,512]{3,2,1,0:T(8,128)(2,1)S(1)}, u32[]{:S(2)}, u32[]{:S(2)}) collective-permute-start(bf16[4,2,32,512]{3,2,1,0:T(8,128)(2,1)S(1)} %pad_maximum_fusion.6), channel_id=1, source_target_pairs={{0,8},{1,9},{2,10},{3,11},{4,12},{5,13},{6,14},{7,15},{8,0},{9,1},... | collective-permute-start | bytes 786440 | tf_op jit(solution)/shard_map/ppermute | solution.py:633
  13.4 14.2 %collective-permute-start.2 = (bf16[4,2,32,512]{3,2,1,0:T(8,128)(2,1)S(1)}, bf16[4,2,32,512]{3,2,1,0:T(8,128)(2,1)S(1)}, u32[]{:S(2)}, u32[]{:S(2)}) collective-permute-start(bf16[4,2,32,512]{3,2,1,0:T(8,128)(2,1)S(1)} %pad_maximum_fusion.8), channel_id=1, source_target_pairs={{0,4},{1,5},{2,6},{3,7},{4,0},{5,1},{6,2},{7,3},{8,12},{9,13},{10,... | collective-permute-start | bytes 786440 | tf_op jit(solution)/shard_map/ppermute | solution.py:633
  27.8 10.5 %collective-permute-start.5 = (bf16[6,2,32,512]{3,2,1,0:T(8,128)(2,1)S(1)}, bf16[6,2,32,512]{3,2,1,0:T(8,128)(2,1)S(1)}, u32[]{:S(2)}, u32[]{:S(2)}) collective-permute-start(bf16[6,2,32,512]{3,2,1,0:T(8,128)(2,1)S(1)} %pad_maximum_fusion.3), channel_id=1, source_target_pairs={{0,2},{1,3},{2,0},{3,1},{4,6},{5,7},{6,4},{7,5},{8,10},{9,11},{10,... | collective-permute-start | bytes 1179656 | tf_op jit(solution)/shard_map/ppermute | solution.py:633
  29.1 9.1 %collective-permute-start.6 = (bf16[4,2,32,512]{3,2,1,0:T(8,128)(2,1)S(1)}, bf16[4,2,32,512]{3,2,1,0:T(8,128)(2,1)S(1)}, u32[]{:S(2)}, u32[]{:S(2)}) collective-permute-start(bf16[4,2,32,512]{3,2,1,0:T(8,128)(2,1)S(1)} %pad_maximum_fusion.7), channel_id=1, source_target_pairs={{0,4},{1,5},{2,6},{3,7},{4,0},{5,1},{6,2},{7,3},{8,12},{9,13},{10,... | collective-permute-start | bytes 786440 | tf_op jit(solution)/shard_map/ppermute | solution.py:633
  29.1 7.1 %collective-permute-start.4 = (bf16[2,2,32,512]{3,2,1,0:T(8,128)(2,1)S(1)}, bf16[2,2,32,512]{3,2,1,0:T(8,128)(2,1)S(1)}, u32[]{:S(2)}, u32[]{:S(2)}) collective-permute-start(bf16[2,2,32,512]{3,2,1,0:T(8,128)(2,1)S(1)} %get-tuple-element.63), channel_id=1, source_target_pairs={{0,8},{1,9},{2,10},{3,11},{4,12},{5,13},{6,14},{7,15},{8,0},{9,1},... | collective-permute-start | bytes 393224 | tf_op jit(solution)/shard_map/ppermute | solution.py:633
  38.3 16.1 %collective-permute-start.10 = (bf16[16,2,32,512]{3,2,1,0:T(8,128)(2,1)S(1)}, bf16[16,2,32,512]{3,2,1,0:T(8,128)(2,1)S(1)}, u32[]{:S(2)}, u32[]{:S(2)}) collective-permute-start(bf16[16,2,32,512]{3,2,1,0:T(8,128)(2,1)S(1)} %constant_dynamic-update-slice_fusion.refs_0_), channel_id=1, source_target_pairs={{0,1},{1,0},{2,3},{3,2},{4,5},{5,4},{6,7},{7,6},{8,9},{9,8},{10,11... | collective-permute-start | bytes 3145736 | tf_op jit(solution)/shard_map/ppermute | solution.py:633
  38.4 7.0 %collective-permute-start.9 = (bf16[2,2,32,512]{3,2,1,0:T(8,128)(2,1)S(1)}, bf16[2,2,32,512]{3,2,1,0:T(8,128)(2,1)S(1)}, u32[]{:S(2)}, u32[]{:S(2)}) collective-permute-start(bf16[2,2,32,512]{3,2,1,0:T(8,128)(2,1)S(1)} %get-tuple-element.68), channel_id=1, source_target_pairs={{0,8},{1,9},{2,10},{3,11},{4,12},{5,13},{6,14},{7,15},{8,0},{9,1},... | collective-permute-start | bytes 393224 | tf_op jit(solution)/shard_map/ppermute | solution.py:633
  40.8 10.1 %collective-permute-start.7 = (bf16[4,2,32,512]{3,2,1,0:T(8,128)(2,1)S(1)}, bf16[4,2,32,512]{3,2,1,0:T(8,128)(2,1)S(1)}, u32[]{:S(2)}, u32[]{:S(2)}) collective-permute-start(bf16[4,2,32,512]{3,2,1,0:T(8,128)(2,1)S(1)} %pad_maximum_fusion.9), channel_id=1, source_target_pairs={{0,4},{1,5},{2,6},{3,7},{4,0},{5,1},{6,2},{7,3},{8,12},{9,13},{10,... | collective-permute-start | bytes 786440 | tf_op jit(solution)/shard_map/ppermute | solution.py:633
  43.3 11.0 %collective-permute-start.8 = (bf16[6,2,32,512]{3,2,1,0:T(8,128)(2,1)S(1)}, bf16[6,2,32,512]{3,2,1,0:T(8,128)(2,1)S(1)}, u32[]{:S(2)}, u32[]{:S(2)}) collective-permute-start(bf16[6,2,32,512]{3,2,1,0:T(8,128)(2,1)S(1)} %pad_maximum_fusion.4), channel_id=1, source_target_pairs={{0,2},{1,3},{2,0},{3,1},{4,6},{5,7},{6,4},{7,5},{8,10},{9,11},{10,... | collective-permute-start | bytes 1179656 | tf_op jit(solution)/shard_map/ppermute | solution.py:633
  54.4 11.6 %collective-permute-start.12 = (bf16[16,2,32,512]{3,2,1,0:T(8,128)(2,1)S(1)}, bf16[16,2,32,512]{3,2,1,0:T(8,128)(2,1)S(1)}, u32[]{:S(2)}, u32[]{:S(2)}) collective-permute-start(bf16[16,2,32,512]{3,2,1,0:T(8,128)(2,1)S(1)} %constant_dynamic-update-slice_fusion.4.refs_0_), channel_id=1, source_target_pairs={{0,1},{1,0},{2,3},{3,2},{4,5},{5,4},{6,7},{7,6},{8,9},{9,8},{10,11... | collective-permute-start | bytes 3145736 | tf_op jit(solution)/shard_map/ppermute | solution.py:633
  54.5 11.5 %collective-permute-start.11 = (bf16[6,2,32,512]{3,2,1,0:T(8,128)(2,1)S(1)}, bf16[6,2,32,512]{3,2,1,0:T(8,128)(2,1)S(1)}, u32[]{:S(2)}, u32[]{:S(2)}) collective-permute-start(bf16[6,2,32,512]{3,2,1,0:T(8,128)(2,1)S(1)} %pad_maximum_fusion.5), channel_id=1, source_target_pairs={{0,2},{1,3},{2,0},{3,1},{4,6},{5,7},{6,4},{7,5},{8,10},{9,11},{10,... | collective-permute-start | bytes 1179656 | tf_op jit(solution)/shard_map/ppermute | solution.py:633
  55.1 15.2 %collective-permute-start.14 = (bf16[8,2,32,512]{3,2,1,0:T(8,128)(2,1)S(1)}, bf16[8,2,32,512]{3,2,1,0:T(8,128)(2,1)S(1)}, u32[]{:S(2)}, u32[]{:S(2)}) collective-permute-start(bf16[8,2,32,512]{3,2,1,0:T(8,128)(2,1)S(1)} %pad_maximum_fusion.1.refs_2_), channel_id=1, source_target_pairs={{0,4},{1,5},{2,6},{3,7},{4,0},{5,1},{6,2},{7,3},{8,12},{9,13},{10,... | collective-permute-start | bytes 1572872 | tf_op jit(solution)/shard_map/ppermute | solution.py:633
  86.6 6.3 %collective-permute-start.17 = (bf16[16,2,32,512]{3,2,1,0:T(8,128)(2,1)}, bf16[16,2,32,512]{3,2,1,0:T(8,128)(2,1)}, u32[]{:S(2)}, u32[]{:S(2)}) collective-permute-start(bf16[16,2,32,512]{3,2,1,0:T(8,128)(2,1)} %get-tuple-element.81), channel_id=1, source_target_pairs={{0,1},{1,0},{2,3},{3,2},{4,5},{5,4},{6,7},{7,6},{8,9},{9,8},{10,11... | collective-permute-start | bytes 3145736 | tf_op jit(solution)/shard_map/ppermute | solution.py:633
  92.5 14.6 %collective-permute-start.22 = (bf16[8,2,32,512]{3,2,1,0:T(8,128)(2,1)S(1)}, bf16[8,2,32,512]{3,2,1,0:T(8,128)(2,1)S(1)}, u32[]{:S(2)}, u32[]{:S(2)}) collective-permute-start(bf16[8,2,32,512]{3,2,1,0:T(8,128)(2,1)S(1)} %get-tuple-element.115), channel_id=1, source_target_pairs={{0,4},{1,5},{2,6},{3,7},{4,0},{5,1},{6,2},{7,3},{8,12},{9,13},{10,... | collective-permute-start | bytes 1572872 | tf_op jit(solution)/shard_map/ppermute | solution.py:633
  94.0 11.9 %collective-permute-start.21 = (bf16[6,2,32,512]{3,2,1,0:T(8,128)(2,1)S(1)}, bf16[6,2,32,512]{3,2,1,0:T(8,128)(2,1)S(1)}, u32[]{:S(2)}, u32[]{:S(2)}) collective-permute-start(bf16[6,2,32,512]{3,2,1,0:T(8,128)(2,1)S(1)} %add_convert_fusion.7), channel_id=1, source_target_pairs={{0,2},{1,3},{2,0},{3,1},{4,6},{5,7},{6,4},{7,5},{8,10},{9,11},{10,... | collective-permute-start | bytes 1179656 | tf_op jit(solution)/shard_map/ppermute | solution.py:633
  98.1 9.0 %collective-permute-start.20 = (bf16[16,2,32,512]{3,2,1,0:T(8,128)(2,1)S(1)}, bf16[16,2,32,512]{3,2,1,0:T(8,128)(2,1)S(1)}, u32[]{:S(2)}, u32[]{:S(2)}) collective-permute-start(bf16[16,2,32,512]{3,2,1,0:T(8,128)(2,1)S(1)} %get-tuple-element.90), channel_id=1, source_target_pairs={{0,1},{1,0},{2,3},{3,2},{4,5},{5,4},{6,7},{7,6},{8,9},{9,8},{10,11... | collective-permute-start | bytes 3145736 | tf_op jit(solution)/shard_map/ppermute | solution.py:633
  100.8 9.7 %collective-permute-start.34 = (bf16[128,256]{1,0:T(8,128)(2,1)S(1)}, bf16[128,256]{1,0:T(8,128)(2,1)S(1)}, u32[]{:S(2)}, u32[]{:S(2)}) collective-permute-start(bf16[128,256]{1,0:T(8,128)(2,1)S(1)} %broadcast_select_fusion), channel_id=1, source_target_pairs={{0,2},{1,3},{2,0},{3,1},{4,6},{5,7},{6,4},{7,5},{8,10},{9,11},{10,... | collective-permute-start | bytes 196616 | tf_op jit(solution)/shard_map/ppermute | solution.py:633
  107.3 12.4 %collective-permute-start.24 = (bf16[4,2,32,512]{3,2,1,0:T(8,128)(2,1)S(1)}, bf16[4,2,32,512]{3,2,1,0:T(8,128)(2,1)S(1)}, u32[]{:S(2)}, u32[]{:S(2)}) collective-permute-start(bf16[4,2,32,512]{3,2,1,0:T(8,128)(2,1)S(1)} %slice.273), channel_id=1, source_target_pairs={{0,4},{1,5},{2,6},{3,7},{4,0},{5,1},{6,2},{7,3},{8,12},{9,13},{10,... | collective-permute-start | bytes 786440 | tf_op jit(solution)/shard_map/ppermute | solution.py:633
  109.1 13.0 %collective-permute-start.27 = (bf16[4,2,32,512]{3,2,1,0:T(8,128)(2,1)S(1)}, bf16[4,2,32,512]{3,2,1,0:T(8,128)(2,1)S(1)}, u32[]{:S(2)}, u32[]{:S(2)}) collective-permute-start(bf16[4,2,32,512]{3,2,1,0:T(8,128)(2,1)S(1)} %add_convert_fusion.9), channel_id=1, source_target_pairs={{0,8},{1,9},{2,10},{3,11},{4,12},{5,13},{6,14},{7,15},{8,0},{9,1},... | collective-permute-start | bytes 786440 | tf_op jit(solution)/shard_map/ppermute | solution.py:633
  110.5 11.8 %collective-permute-start.23 = (bf16[6,2,32,512]{3,2,1,0:T(8,128)(2,1)S(1)}, bf16[6,2,32,512]{3,2,1,0:T(8,128)(2,1)S(1)}, u32[]{:S(2)}, u32[]{:S(2)}) collective-permute-start(bf16[6,2,32,512]{3,2,1,0:T(8,128)(2,1)S(1)} %add_convert_fusion.6), channel_id=1, source_target_pairs={{0,2},{1,3},{2,0},{3,1},{4,6},{5,7},{6,4},{7,5},{8,10},{9,11},{10,... | collective-permute-start | bytes 1179656 | tf_op jit(solution)/shard_map/ppermute | solution.py:633
  119.7 4.9 %collective-permute-start.35 = (bf16[128,256]{1,0:T(8,128)(2,1)S(1)}, bf16[128,256]{1,0:T(8,128)(2,1)S(1)}, u32[]{:S(2)}, u32[]{:S(2)}) collective-permute-start(bf16[128,256]{1,0:T(8,128)(2,1)S(1)} %add_convert_fusion.20), channel_id=1, source_target_pairs={{0,4},{1,5},{2,6},{3,7},{4,0},{5,1},{6,2},{7,3},{8,12},{9,13},{10,... | collective-permute-start | bytes 196616 | tf_op jit(solution)/shard_map/ppermute | solution.py:633
  123.5 8.7 %collective-permute-start.25 = (bf16[4,2,32,512]{3,2,1,0:T(8,128)(2,1)S(1)}, bf16[4,2,32,512]{3,2,1,0:T(8,128)(2,1)S(1)}, u32[]{:S(2)}, u32[]{:S(2)}) collective-permute-start(bf16[4,2,32,512]{3,2,1,0:T(8,128)(2,1)S(1)} %slice.281), channel_id=1, source_target_pairs={{0,4},{1,5},{2,6},{3,7},{4,0},{5,1},{6,2},{7,3},{8,12},{9,13},{10,... | collective-permute-start | bytes 786440 | tf_op jit(solution)/shard_map/ppermute | solution.py:633
  124.1 9.0 %collective-permute-start.26 = (bf16[6,2,32,512]{3,2,1,0:T(8,128)(2,1)S(1)}, bf16[6,2,32,512]{3,2,1,0:T(8,128)(2,1)S(1)}, u32[]{:S(2)}, u32[]{:S(2)}) collective-permute-start(bf16[6,2,32,512]{3,2,1,0:T(8,128)(2,1)S(1)} %add_convert_fusion.4), channel_id=1, source_target_pairs={{0,2},{1,3},{2,0},{3,1},{4,6},{5,7},{6,4},{7,5},{8,10},{9,11},{10,... | collective-permute-start | bytes 1179656 | tf_op jit(solution)/shard_map/ppermute | solution.py:633
  124.7 8.6 %collective-permute-start.28 = (bf16[2,2,32,512]{3,2,1,0:T(8,128)(2,1)S(1)}, bf16[2,2,32,512]{3,2,1,0:T(8,128)(2,1)S(1)}, u32[]{:S(2)}, u32[]{:S(2)}) collective-permute-start(bf16[2,2,32,512]{3,2,1,0:T(8,128)(2,1)S(1)} %add_convert_fusion.17), channel_id=1, source_target_pairs={{0,8},{1,9},{2,10},{3,11},{4,12},{5,13},{6,14},{7,15},{8,0},{9,1},... | collective-permute-start | bytes 393224 | tf_op jit(solution)/shard_map/ppermute | solution.py:633
  132.2 7.2 %collective-permute-start.36 = (bf16[128,256]{1,0:T(8,128)(2,1)S(1)}, bf16[128,256]{1,0:T(8,128)(2,1)S(1)}, u32[]{:S(2)}, u32[]{:S(2)}) collective-permute-start(bf16[128,256]{1,0:T(8,128)(2,1)S(1)} %add_convert_fusion.19), channel_id=1, source_target_pairs={{0,8},{1,9},{2,10},{3,11},{4,12},{5,13},{6,14},{7,15},{8,0},{9,1},... | collective-permute-start | bytes 196616 | tf_op jit(solution)/shard_map/ppermute | solution.py:633
  133.3 9.3 %collective-permute-start.29 = (bf16[4,2,32,512]{3,2,1,0:T(8,128)(2,1)S(1)}, bf16[4,2,32,512]{3,2,1,0:T(8,128)(2,1)S(1)}, u32[]{:S(2)}, u32[]{:S(2)}) collective-permute-start(bf16[4,2,32,512]{3,2,1,0:T(8,128)(2,1)S(1)} %slice.284), channel_id=1, source_target_pairs={{0,4},{1,5},{2,6},{3,7},{4,0},{5,1},{6,2},{7,3},{8,12},{9,13},{10,... | collective-permute-start | bytes 786440 | tf_op jit(solution)/shard_map/ppermute | solution.py:633
  134.9 12.7 %collective-permute-start.30 = (bf16[8,2,32,512]{3,2,1,0:T(8,128)(2,1)S(1)}, bf16[8,2,32,512]{3,2,1,0:T(8,128)(2,1)S(1)}, u32[]{:S(2)}, u32[]{:S(2)}) collective-permute-start(bf16[8,2,32,512]{3,2,1,0:T(8,128)(2,1)S(1)} %pad_maximum_fusion.2), channel_id=1, source_target_pairs={{0,2},{1,3},{2,0},{3,1},{4,6},{5,7},{6,4},{7,5},{8,10},{9,11},{10,... | collective-permute-start | bytes 1572872 | tf_op jit(solution)/shard_map/ppermute | solution.py:633
  139.5 8.2 %collective-permute-start.32 = (bf16[2,2,32,512]{3,2,1,0:T(8,128)(2,1)S(1)}, bf16[2,2,32,512]{3,2,1,0:T(8,128)(2,1)S(1)}, u32[]{:S(2)}, u32[]{:S(2)}) collective-permute-start(bf16[2,2,32,512]{3,2,1,0:T(8,128)(2,1)S(1)} %add_convert_fusion.16), channel_id=1, source_target_pairs={{0,8},{1,9},{2,10},{3,11},{4,12},{5,13},{6,14},{7,15},{8,0},{9,1},... | collective-permute-start | bytes 393224 | tf_op jit(solution)/shard_map/ppermute | solution.py:633
  142.6 5.0 %collective-permute-start.37 = (f32[128,256]{1,0:T(8,128)S(1)}, f32[128,256]{1,0:T(8,128)S(1)}, u32[]{:S(2)}, u32[]{:S(2)}) collective-permute-start(f32[128,256]{1,0:T(8,128)S(1)} %get-tuple-element.107), channel_id=1, source_target_pairs={{0,2},{1,3},{2,0},{3,1},{4,6},{5,7},{6,4},{7,5},{8,10},{9,11},{10,... | collective-permute-start | bytes 393224 | tf_op jit(solution)/shard_map/ppermute | solution.py:633
  142.6 6.8 %collective-permute-start.31 = (bf16[2,2,32,512]{3,2,1,0:T(8,128)(2,1)S(1)}, bf16[2,2,32,512]{3,2,1,0:T(8,128)(2,1)S(1)}, u32[]{:S(2)}, u32[]{:S(2)}) collective-permute-start(bf16[2,2,32,512]{3,2,1,0:T(8,128)(2,1)S(1)} %add_convert_fusion.12), channel_id=1, source_target_pairs={{0,8},{1,9},{2,10},{3,11},{4,12},{5,13},{6,14},{7,15},{8,0},{9,1},... | collective-permute-start | bytes 393224 | tf_op jit(solution)/shard_map/ppermute | solution.py:633
  (22 other events, 89.8 us)
